TPU v7x, 128 devices: a whole 4x4x4 slice. The times are simulated.
128 devices in a mesh: dp: 16 (over z_hi, y, core), fsdp: 8 (over x, z_lo).
Axes of the slice: x: 4, y: 4, z: 4 (z_hi: 2, z_lo: 2; z = z_hi * 2 + z_lo), core: 2. Of those that a mesh axis runs over, the one named last changes fastest.
Arguments:
- tokens: bfloat16 [16384, 640], P(('dp', 'fsdp')), may hold values from -6 to 6
- w_query: bfloat16 [640, 1024], P(('dp', 'fsdp')), may hold values from -0.25 to 0.25
- w_key: bfloat16 [640, 256], P(('dp', 'fsdp')), may hold values from -0.25 to 0.25
- w_value: bfloat16 [640, 256], P(('dp', 'fsdp')), may hold values from -0.25 to 0.25
- w_out: bfloat16 [1024, 640], P(('dp', 'fsdp')), may hold values from -0.75 to 0.75
- w_gate: bfloat16 [640, 2048], P(('dp', 'fsdp')), may hold values from -0.25 to 0.25
- w_up: bfloat16 [640, 2048], P(('dp', 'fsdp')), may hold values from -0.25 to 0.25
- w_down: bfloat16 [2048, 640], P(('dp', 'fsdp')), may hold values from -0.125 to 0.125
- attn_gain: bfloat16 [640], P(('dp', 'fsdp')), may hold values from 0.5 to 1.5
- ffn_gain: bfloat16 [640], P(('dp', 'fsdp')), may hold values from 0.5 to 1.5
- head_gains: bfloat16 [512], P(('dp', 'fsdp')), may hold values from 0.8984375 to 1.59375
- lengths: int32 [16, 2], P('dp'), may hold values from 0 to 1024, as said below
- cotangent: bfloat16 [16384, 640], P(('dp', 'fsdp')), may hold values from -6 to 6
Outputs:
- block_out: bfloat16 [16384, 640], P(('dp', 'fsdp'))
- input_grad: float32 [16384, 640], P(('dp', 'fsdp'))
- grad_query: float32 [640, 1024], P(('dp', 'fsdp'))
- grad_key: float32 [640, 256], P(('dp', 'fsdp'))
- grad_value: float32 [640, 256], P(('dp', 'fsdp'))
- grad_out: float32 [1024, 640], P(('dp', 'fsdp'))
- grad_gate: float32 [640, 2048], P(('dp', 'fsdp'))
- grad_up: float32 [640, 2048], P(('dp', 'fsdp'))
- grad_down: float32 [2048, 640], P(('dp', 'fsdp'))
- grad_attn_gain: float32 [640], P(('dp', 'fsdp'))
- grad_ffn_gain: float32 [640], P(('dp', 'fsdp'))
- grad_head_gains: float32 [512], P(('dp', 'fsdp'))
Inputs may be any that keep to these rules, and one draw needn't show every extreme that they name: `lengths`: each row is either one sequence of the whole group (1024, then 0) or two sequences of half the group each; in every draw at least one row, drawn from the seed, is a single sequence.
All inputs are finite; a program needn't handle non-finite values.
Results may differ from a plain program's by a relative error of at most 0.035.
Values may be sent and summed in bfloat16 or wider, within the bound.
A program may use at most 128 MiB of HBM per device.

v0:
```python
import math

import jax
import jax.numpy as jnp
from jax import lax
from jax.sharding import PartitionSpec as P

H = 4
KV = 1
HD = 256


eps_norm = 1e-05
rope_base = 1000000.0
neg_large = -1e30


def rms_scale(values):
    return lax.rsqrt(jnp.mean(values * values, axis=-1, keepdims=True) + eps_norm)


def gelu_tanh(values):
    return jax.nn.gelu(values, approximate=True)


def rope_tables(positions):
    half_dim = HD // 2
    exponents = jnp.arange(half_dim, dtype=jnp.float32) * (2.0 / HD)
    frequencies = jnp.exp(-exponents * math.log(rope_base))
    angles = positions.astype(jnp.float32)[:, None] * frequencies[None, :]
    return (jnp.cos(angles)[:, None, :], jnp.sin(angles)[:, None, :])


def rotate(values, cosines, sine_table):
    half_dim = HD // 2
    first_half = values[..., :half_dim]
    second = values[..., half_dim:]
    return jnp.concatenate(
        [first_half * cosines - second * sine_table, second * cosines + first_half * sine_table],
        axis=-1,
    )


def rotate_back(grads, cosines, sine_table):
    half_dim = HD // 2
    first_half = grads[..., :half_dim]
    second = grads[..., half_dim:]
    return jnp.concatenate(
        [first_half * cosines + second * sine_table, second * cosines - first_half * sine_table],
        axis=-1,
    )


def seg_start(token_ids, seq_lengths):
    seq_ends = jnp.cumsum(seq_lengths)
    past_end = (token_ids[:, None] >= seq_ends[None, :]).astype(jnp.int32)
    segment = jnp.sum(past_end, axis=1)
    seq_start = jnp.sum(past_end * seq_lengths[None, :], axis=1)
    return (segment, token_ids - seq_start)


def norm_back(grad_normed, raw_values, inverse_rms, gain_values, gain_axes):
    scaled = grad_normed * gain_values
    raw_grad = inverse_rms * scaled - raw_values * inverse_rms**3 * jnp.mean(
        scaled * raw_values, axis=-1, keepdims=True
    )
    gain_grad = jnp.sum(grad_normed * raw_values * inverse_rms, axis=gain_axes)
    return (raw_grad, gain_grad)


def contract_rows(left, right):
    return lax.dot_general(
        left, right, (((0,), (0,)), ((), ())), preferred_element_type=jnp.float32
    )


def times_transposed(left, right):
    return lax.dot_general(
        left, right, (((1,), (1,)), ((), ())), preferred_element_type=jnp.float32
    )


def body(
    tokens,
    w_query,
    w_key,
    w_value,
    w_out,
    w_gate,
    w_up,
    w_down,
    attn_gain,
    ffn_gain,
    head_gains,
    lengths,
    cotangent,
):
    shards = (w_query, w_key, w_value, w_out, w_gate, w_up, w_down, attn_gain, ffn_gain, head_gains)
    weights = (
        lax.all_gather(shards[0], ("dp", "fsdp"), axis=0, tiled=True),
        lax.all_gather(shards[1], ("dp", "fsdp"), axis=0, tiled=True),
        lax.all_gather(shards[2], ("dp", "fsdp"), axis=0, tiled=True),
        lax.all_gather(shards[3], ("dp", "fsdp"), axis=0, tiled=True),
        lax.all_gather(shards[4], ("dp", "fsdp"), axis=0, tiled=True),
        lax.all_gather(shards[5], ("dp", "fsdp"), axis=0, tiled=True),
        lax.all_gather(shards[6], ("dp", "fsdp"), axis=0, tiled=True),
        lax.all_gather(shards[7], ("dp", "fsdp"), axis=0, tiled=True),
        lax.all_gather(shards[8], ("dp", "fsdp"), axis=0, tiled=True),
        lax.all_gather(shards[9], ("dp", "fsdp"), axis=0, tiled=True),
    )
    (
        query_mat,
        key_mat,
        value_mat,
        output_mat,
        gate_mat,
        up_mat,
        down_mat,
        norm_one,
        norm_two,
        head_norm,
    ) = weights
    tok_rows = tokens.shape[0]
    group_size = lax.axis_size("fsdp")
    member = lax.axis_index("fsdp")
    group_rows = tok_rows * group_size
    group_ratio = H // KV
    score_scale = 1.0 / math.sqrt(HD)
    seq_lengths = lengths[0]
    local_ids = member * tok_rows + jnp.arange(tok_rows, dtype=jnp.int32)
    local_seg, local_pos = seg_start(local_ids, seq_lengths)
    cosines, sine_table = rope_tables(local_pos)
    inputs = tokens.astype(jnp.float32)
    gain_one = norm_one.astype(jnp.float32)
    gain_two = norm_two.astype(jnp.float32)
    gain_heads = head_norm.astype(jnp.float32)
    scale_one = rms_scale(inputs)
    normed = (inputs * scale_one * gain_one).astype(jnp.bfloat16)
    query_raw = jnp.dot(normed, query_mat, preferred_element_type=jnp.float32).reshape(
        tok_rows, H, HD
    )
    key_raw = jnp.dot(normed, key_mat, preferred_element_type=jnp.float32).reshape(tok_rows, KV, HD)
    value_flat = jnp.dot(normed, value_mat, preferred_element_type=jnp.float32).astype(jnp.bfloat16)
    query_scale = rms_scale(query_raw)
    key_scale = rms_scale(key_raw)
    query_rot = rotate(query_raw * query_scale * gain_heads[:HD], cosines, sine_table).astype(
        jnp.bfloat16
    )
    key_rot = rotate(key_raw * key_scale * gain_heads[HD:], cosines, sine_table).astype(
        jnp.bfloat16
    )
    queries = query_rot.reshape(tok_rows, KV, group_ratio, HD).transpose(1, 2, 0, 3)
    key_flat = key_rot.reshape(tok_rows, KV * HD)

    def masked_scores(key_piece, first_key):
        key_count = key_piece.shape[0]
        key_ids = first_key + jnp.arange(key_count, dtype=jnp.int32)
        key_seg, unused = seg_start(key_ids, seq_lengths)
        allowed = (local_seg[:, None] == key_seg[None, :]) & (
            key_ids[None, :] <= local_ids[:, None]
        )
        scores = (
            jnp.einsum(
                "kgqd,nkd->kgqn",
                queries,
                key_piece.reshape(key_count, KV, HD),
                preferred_element_type=jnp.float32,
            )
            * score_scale
        )
        return (jnp.where(allowed, scores, neg_large), allowed)

    run_max = jnp.full((KV, group_ratio, tok_rows), neg_large, jnp.float32)
    key_piece = lax.all_gather(key_flat, "fsdp", axis=0, tiled=True)
    value_piece = lax.all_gather(value_flat, "fsdp", axis=0, tiled=True)
    key_count = key_piece.shape[0]
    scores, allowed = masked_scores(key_piece, jnp.int32(0))
    new_max = jnp.maximum(run_max, jnp.max(scores, axis=-1))
    softmax_rows = jnp.where(allowed, jnp.exp(scores - new_max[..., None]), 0.0)
    run_total = jnp.sum(softmax_rows, axis=-1)
    run_acc = jnp.einsum(
        "kgqn,nkd->kgqd",
        softmax_rows.astype(jnp.bfloat16),
        value_piece.reshape(key_count, KV, HD),
        preferred_element_type=jnp.float32,
    )
    run_max, run_total, run_acc = (new_max, run_total, run_acc)
    attended = run_acc / run_total[..., None]
    log_sum = run_max + jnp.log(run_total)
    attended_low = attended.transpose(2, 0, 1, 3).reshape(tok_rows, H * HD).astype(jnp.bfloat16)
    middle = inputs + jnp.dot(attended_low, output_mat, preferred_element_type=jnp.float32)
    scale_two = rms_scale(middle)
    ffn_in = (middle * scale_two * gain_two).astype(jnp.bfloat16)
    gate_pre = jnp.dot(ffn_in, gate_mat, preferred_element_type=jnp.float32)
    up_pre = jnp.dot(ffn_in, up_mat, preferred_element_type=jnp.float32)
    gate_act, gate_pullback = jax.vjp(gelu_tanh, gate_pre)
    hidden = (gate_act * up_pre).astype(jnp.bfloat16)
    block_out = (middle + jnp.dot(hidden, down_mat, preferred_element_type=jnp.float32)).astype(
        jnp.bfloat16
    )
    weights = (
        lax.all_gather(shards[0], ("dp", "fsdp"), axis=0, tiled=True),
        lax.all_gather(shards[1], ("dp", "fsdp"), axis=0, tiled=True),
        lax.all_gather(shards[2], ("dp", "fsdp"), axis=0, tiled=True),
        lax.all_gather(shards[3], ("dp", "fsdp"), axis=0, tiled=True),
        lax.all_gather(shards[4], ("dp", "fsdp"), axis=0, tiled=True),
        lax.all_gather(shards[5], ("dp", "fsdp"), axis=0, tiled=True),
        lax.all_gather(shards[6], ("dp", "fsdp"), axis=0, tiled=True),
        lax.all_gather(shards[7], ("dp", "fsdp"), axis=0, tiled=True),
        lax.all_gather(shards[8], ("dp", "fsdp"), axis=0, tiled=True),
        lax.all_gather(shards[9], ("dp", "fsdp"), axis=0, tiled=True),
    )
    (
        query_mat,
        key_mat,
        value_mat,
        output_mat,
        gate_mat,
        up_mat,
        down_mat,
        norm_one,
        norm_two,
        head_norm,
    ) = weights
    grad_down = contract_rows(hidden, cotangent)
    d_hidden = times_transposed(cotangent, down_mat)
    d_gate = gate_pullback(d_hidden * up_pre)[0].astype(jnp.bfloat16)
    d_up = (d_hidden * gate_act).astype(jnp.bfloat16)
    grad_gate = contract_rows(ffn_in, d_gate)
    grad_up = contract_rows(ffn_in, d_up)
    d_ffn = times_transposed(d_gate, gate_mat) + times_transposed(d_up, up_mat)
    d_norm_two, grad_two = norm_back(d_ffn, middle, scale_two, gain_two, (0,))
    d_middle = cotangent.astype(jnp.float32) + d_norm_two
    d_branch = d_middle.astype(jnp.bfloat16)
    grad_output = contract_rows(attended_low, d_branch)
    d_attended = (
        times_transposed(d_branch, output_mat)
        .astype(jnp.bfloat16)
        .reshape(tok_rows, KV, group_ratio, HD)
        .transpose(1, 2, 0, 3)
    )
    deltas = jnp.sum(d_attended.astype(jnp.float32) * attended, axis=-1)
    key_all, value_all = (
        lax.all_gather(key_flat, "fsdp", axis=0, tiled=True),
        lax.all_gather(value_flat, "fsdp", axis=0, tiled=True),
    )
    key_block = math.gcd(group_rows, 512)
    block_count = group_rows // key_block
    key_blocks = key_all.reshape(block_count, key_block, KV * HD)
    value_blocks = value_all.reshape(block_count, key_block, KV * HD)
    block_firsts = jnp.arange(block_count, dtype=jnp.int32) * key_block

    def back_block(grad_queries, block_item):
        key_piece, value_piece, first_key = block_item
        scores, allowed = masked_scores(key_piece, first_key)
        softmax_rows = jnp.where(allowed, jnp.exp(scores - log_sum[..., None]), 0.0)
        key_three = key_piece.reshape(key_block, KV, HD)
        d_probs = jnp.einsum(
            "kgqd,nkd->kgqn",
            d_attended,
            value_piece.reshape(key_block, KV, HD),
            preferred_element_type=jnp.float32,
        )
        d_scores = (softmax_rows * (d_probs - deltas[..., None])).astype(jnp.bfloat16)
        grad_queries = (
            grad_queries
            + jnp.einsum("kgqn,nkd->kgqd", d_scores, key_three, preferred_element_type=jnp.float32)
            * score_scale
        )
        d_keys = (
            jnp.einsum("kgqn,kgqd->nkd", d_scores, queries, preferred_element_type=jnp.float32)
            * score_scale
        )
        d_values = jnp.einsum(
            "kgqn,kgqd->nkd",
            softmax_rows.astype(jnp.bfloat16),
            d_attended,
            preferred_element_type=jnp.float32,
        )
        return (
            grad_queries,
            jnp.concatenate(
                [d_keys.reshape(key_block, KV * HD), d_values.reshape(key_block, KV * HD)], axis=-1
            ),
        )

    grad_queries, kv_terms = lax.scan(
        back_block,
        jnp.zeros((KV, group_ratio, tok_rows, HD), jnp.float32),
        (key_blocks, value_blocks, block_firsts),
    )
    kv_sums = lax.psum_scatter(
        kv_terms.reshape(group_rows, 2 * KV * HD).astype(jnp.bfloat16),
        "fsdp",
        scatter_dimension=0,
        tiled=True,
    ).astype(jnp.float32)
    d_query_rot = grad_queries.transpose(2, 0, 1, 3).reshape(tok_rows, H, HD)
    d_query_raw, grad_query_gain = norm_back(
        rotate_back(d_query_rot, cosines, sine_table),
        query_raw,
        query_scale,
        gain_heads[:HD],
        (0, 1),
    )
    d_key_rot = kv_sums[:, : KV * HD].reshape(tok_rows, KV, HD)
    d_key_raw, grad_key_gain = norm_back(
        rotate_back(d_key_rot, cosines, sine_table), key_raw, key_scale, gain_heads[HD:], (0, 1)
    )
    d_query_low = d_query_raw.reshape(tok_rows, H * HD).astype(jnp.bfloat16)
    d_key_low = d_key_raw.reshape(tok_rows, KV * HD).astype(jnp.bfloat16)
    d_value_low = kv_sums[:, KV * HD :].astype(jnp.bfloat16)
    grad_query_mat = contract_rows(normed, d_query_low)
    grad_key_mat = contract_rows(normed, d_key_low)
    grad_value_mat = contract_rows(normed, d_value_low)
    d_normed = (
        times_transposed(d_query_low, query_mat)
        + times_transposed(d_key_low, key_mat)
        + times_transposed(d_value_low, value_mat)
    )
    d_norm_one, grad_one = norm_back(d_normed, inputs, scale_one, gain_one, (0,))
    input_grad = d_middle + d_norm_one
    grad_heads = jnp.concatenate([grad_query_gain, grad_key_gain])
    all_sums = (
        lax.psum_scatter(grad_query_mat, ("dp", "fsdp"), scatter_dimension=0, tiled=True),
        lax.psum_scatter(grad_key_mat, ("dp", "fsdp"), scatter_dimension=0, tiled=True),
        lax.psum_scatter(grad_value_mat, ("dp", "fsdp"), scatter_dimension=0, tiled=True),
        lax.psum_scatter(grad_output, ("dp", "fsdp"), scatter_dimension=0, tiled=True),
        lax.psum_scatter(grad_gate, ("dp", "fsdp"), scatter_dimension=0, tiled=True),
        lax.psum_scatter(grad_up, ("dp", "fsdp"), scatter_dimension=0, tiled=True),
        lax.psum_scatter(grad_down, ("dp", "fsdp"), scatter_dimension=0, tiled=True),
        lax.psum_scatter(grad_one, ("dp", "fsdp"), scatter_dimension=0, tiled=True),
        lax.psum_scatter(grad_two, ("dp", "fsdp"), scatter_dimension=0, tiled=True),
        lax.psum_scatter(grad_heads, ("dp", "fsdp"), scatter_dimension=0, tiled=True),
    )
    (
        sum_query,
        sum_key,
        sum_value,
        sum_output,
        sum_gate,
        sum_up,
        sum_down,
        sum_one,
        sum_two,
        sum_heads,
    ) = all_sums
    return (
        block_out,
        input_grad,
        sum_query,
        sum_key,
        sum_value,
        sum_output,
        sum_gate,
        sum_up,
        sum_down,
        sum_one,
        sum_two,
        sum_heads,
    )


def solution(mesh):
    in_specs = (
        P(("dp", "fsdp"), None),
        P(("dp", "fsdp"), None),
        P(("dp", "fsdp"), None),
        P(("dp", "fsdp"), None),
        P(("dp", "fsdp"), None),
        P(("dp", "fsdp"), None),
        P(("dp", "fsdp"), None),
        P(("dp", "fsdp"), None),
        P(("dp", "fsdp")),
        P(("dp", "fsdp")),
        P(("dp", "fsdp")),
        P("dp", None),
        P(("dp", "fsdp"), None),
    )
    out_specs = (
        P(("dp", "fsdp"), None),
        P(("dp", "fsdp"), None),
        P(("dp", "fsdp"), None),
        P(("dp", "fsdp"), None),
        P(("dp", "fsdp"), None),
        P(("dp", "fsdp"), None),
        P(("dp", "fsdp"), None),
        P(("dp", "fsdp"), None),
        P(("dp", "fsdp"), None),
        P(("dp", "fsdp")),
        P(("dp", "fsdp")),
        P(("dp", "fsdp")),
    )
    return jax.shard_map(body, mesh=mesh, in_specs=in_specs, out_specs=out_specs, check_vma=False)
```

profile of v0, /device:TPU:0, one launch (start us, length us, event | category | flops | bytes accessed | tf_op | source)
XLA Modules:
  0.0 2481.6 jit_solution(17942489905414365557)
XLA Ops:
  8.0 0.7 all-gather.11.cloned.1.call-update
  10.7 1.0 fusion.53
  12.2 0.8 reduce-window.9
  13.2 0.7 fusion.92
  13.9 0.8 dynamic-update-slice
  14.8 0.8 dynamic-update-slice.2
  15.6 0.8 dynamic-update-slice.1
  16.5 68.4 %all-reduce.14 = (bf16[640]{0:T(1024)(128)(2,1)S(1)}, bf16[512]{0:T(512)(128)(2,1)S(1)}, bf16[640]{0:T(1024)(128)(2,1)S(1)}) all-reduce(bf16[640]{0:T(1024)(128)(2,1)S(1)} %dynamic-update-slice, bf16[512]{0:T(512)(128)(2,1)S(1)} %dynamic-update-slice.1, ...), channel_id=1, replica_groups=mesh['dp'=16,'fsdp'=8] {'dp','fsdp'}, use_global_device_ids=true, to_apply=%add | all-reduce | flops 1792 | bytes 7168
  84.9 314.9 %all-gather.1 = bf16[128,5,256]{2,1,0:T(8,128)(2,1)S(1)} all-gather(bf16[1,5,256]{2,1,0:T(8,128)(2,1)} %bitcast.230), channel_id=1, replica_groups=mesh['dp'=16,'fsdp'=8] {'dp','fsdp'}, dimensions={0}, use_global_device_ids=true | all-gather | bytes 330240 | tf_op jit(solution)/shard_map/all_gather | solution.py:101
  399.9 1.4 multiply_reduce_fusion.8
  402.6 312.9 %all-gather.2 = bf16[128,5,256]{2,1,0:T(8,128)(2,1)S(1)} all-gather(bf16[1,5,256]{2,1,0:T(8,128)(2,1)S(1)} %bitcast.231), channel_id=1, replica_groups=mesh['dp'=16,'fsdp'=8] {'dp','fsdp'}, dimensions={0}, use_global_device_ids=true | all-gather | bytes 330240 | tf_op jit(solution)/shard_map/all_gather | solution.py:102
  716.2 0.7 broadcast_in_dim.54
  717.9 29.1 %all_gather.49 = bf16[1024,256]{1,0:T(8,128)(2,1)S(1)} all-gather(bf16[128,256]{1,0:T(8,128)(2,1)S(1)} %pad_maximum_fusion.4), channel_id=1, replica_groups=mesh['dp'=16,'fsdp'=8] {'fsdp'}, dimensions={0}, use_global_device_ids=true | all-gather | bytes 589824 | tf_op jit(solution)/shard_map/all_gather | solution.py:174
  747.2 31.1 %all_gather.51 = bf16[1024,256]{1,0:T(8,128)(2,1)} all-gather(bf16[128,256]{1,0:T(8,128)(2,1)S(1)} %convolution_convert_fusion.1), channel_id=1, replica_groups=mesh['dp'=16,'fsdp'=8] {'fsdp'}, dimensions={0}, use_global_device_ids=true | all-gather | bytes 589824 | tf_op jit(solution)/shard_map/all_gather | solution.py:175
  778.3 2.6 reshape.520
  781.4 1.0 reshape.503
  782.5 1.3 multiply_reduce_fusion.2
  784.3 0.9 copy.136
  785.4 0.9 copy.138
  786.6 0.9 copy.119
  788.0 0.7 fusion.30
  788.7 0.7 fusion.32
  789.5 0.8 copy-done.21
  790.6 1.9 multiply_reduce_fusion.5
  793.7 124.1 %all-gather.17.cloned.1.call-done = bf16[128,5,2048]{2,1,0:T(8,128)(2,1)} async-done(((bf16[1,5,2048]{2,1,0:T(8,128)(2,1)}), bf16[128,5,2048]{2,1,0:T(8,128)(2,1)}) %all-gather.17.cloned.1.call-update) | async-done | bytes 2621456 | tf_op jit(solution)/shard_map/all_gather | solution.py:104
  917.8 4.2 reshape.526
  922.0 304.5 %all-gather.19.cloned.1.call-done = bf16[128,5,2048]{2,1,0:T(8,128)(2,1)} async-done(((bf16[1,5,2048]{2,1,0:T(8,128)(2,1)}), bf16[128,5,2048]{2,1,0:T(8,128)(2,1)}) %all-gather.19.cloned.1.call-update) | async-done | bytes 2621456 | tf_op jit(solution)/shard_map/all_gather | solution.py:105
  1226.5 5.6 reshape.528
  1232.1 3.3 fusion.110
  1235.4 1.6 fusion.109
  1236.9 296.9 %all-gather.13.cloned.1.call-done = bf16[2048,640]{1,0:T(8,128)(2,1)} async-done(((bf16[16,640]{1,0:T(8,128)(2,1)}), bf16[2048,640]{1,0:T(8,128)(2,1)}) %all-gather.13.cloned.1.call-update) | async-done | bytes 2621456 | tf_op jit(solution)/shard_map/all_gather | solution.py:106
  1533.8 4.6 multiply_convert_fusion
  1538.4 0.9 fusion.111
  1539.3 1.1 copy-done
  1540.5 1.1 multiply_reduce_fusion.3
  1541.8 0.7 copy-done.14
  1543.8 12.8 while.15
  1545.4 1.3 fusion.177
  1547.4 1.3 fusion.180
  1549.3 1.0 copy-done.34
  1551.8 1.3 fusion.177
  1553.8 1.3 fusion.180
  1555.6 1.0 copy-done.34
  1556.6 2.4 copy.125
  1560.9 2.1 fusion.101
  1563.0 2.0 fusion.74
  1564.9 3.2 fusion.114
  1568.2 3.2 fusion.113
  1571.4 28.9 %reduce-scatter.3.cloned.1.call-done = bf16[128,512]{1,0:T(8,128)(2,1)} async-done(((bf16[1024,512]{1,0:T(8,128)(2,1)}), bf16[128,512]{1,0:T(8,128)(2,1)}) %reduce-scatter.3.cloned.1.call-update) | async-done | bytes 131088 | tf_op jit(solution)/shard_map/reduce_scatter | solution.py:292
  1600.4 0.8 fusion.85
  1601.9 1.2 fusion.99
  1603.1 2.1 fusion.86
  1605.2 1.0 copy-done.16
  1606.2 3.2 fusion.115
  1609.5 1.2 copy-done.4
  1611.3 3.1 fusion.33
  1615.0 64.0 %all-reduce.12 = (f32[640]{0:T(1024)S(1)}, f32[640]{0:T(1024)S(1)}, f32[512]{0:T(512)S(1)}) all-reduce(f32[640]{0:T(1024)S(1)} %get-tuple-element.289, f32[640]{0:T(1024)S(1)} %get-tuple-element.287, f32[512]{0:T(512)S(1)} %pad_maximum_fusion.5), channel_id=10, replica_groups=mesh['dp'=16,'fsdp'=8] {'dp','fsdp'}, use_global_device_ids=true, to_apply=%region_28.29.clone | all-reduce | flops 1792 | bytes 14336
  1680.8 0.9 fusion.58
  1681.7 146.0 %all-reduce.17.cloned.1.call-done = (f32[640,1024]{1,0:T(8,128)}, f32[640,256]{1,0:T(8,128)}, f32[640,256]{1,0:T(8,128)}, f32[1024,640]{1,0:T(8,128)}, f32[640,2048]{1,0:T(8,128)}, /*index=5*/f32[640,2048]{1,0:T(8,128)}) async-done(((f32[640,1024]{1,0:T(8,128)}, f32[640,256]{1,0:T(8,128)}, f32[640,256]{1,0:T(8,128)}, f32[1024,640]{1,0:T(8,128)}, f32[640,2048]{1,0:T(8,128)}, ...) | async-done | bytes 17039376
  1827.7 1.3 constant_dynamic-slice_fusion.3
  1829.0 1.3 constant_dynamic-slice_fusion.2
  1830.4 1.5 constant_dynamic-slice_fusion.5
  1831.8 1.6 constant_dynamic-slice_fusion
  1833.4 641.4 %reduce-scatter.5.cloned.1.call-done = f32[16,640]{1,0:T(8,128)} async-done(((f32[2048,640]{1,0:T(8,128)}), f32[16,640]{1,0:T(8,128)}) %reduce-scatter.5.cloned.1.call-update) | async-done | bytes 40976 | tf_op jit(solution)/shard_map/reduce_scatter | solution.py:331
  (223 shorter events, 22.3 us)
Async XLA Ops:
  7.2 709.0 %copy-start.58 = (s32[1,2]{1,0:T(1,128)S(1)}, s32[1,2]{1,0:T(1,128)}, u32[]{:S(2)}) copy-start(s32[1,2]{1,0:T(1,128)} %param.26) | copy-start | bytes 28
  7.2 395.4 %copy-start.53 = (bf16[5,256]{1,0:T(8,128)(2,1)S(1)}, bf16[5,256]{1,0:T(8,128)(2,1)}, u32[]{:S(2)}) copy-start(bf16[5,256]{1,0:T(8,128)(2,1)} %param.18) | copy-start | bytes 7684
  7.2 771.1 %all-gather.15.cloned.1.call-start = ((), (), s32[]{:S(2)}) async-start(), calls=%async_computation.6 | async-start | bytes 2113536 | tf_op jit(solution)/shard_map/all_gather | solution.py:100
  7.9 782.6 %all-gather.11.cloned.1.call-start = ((), (), s32[]{:S(2)}) async-start(), calls=%async_computation.2 | async-start | bytes 1320960 | tf_op jit(solution)/shard_map/all_gather | solution.py:103
  8.7 909.1 %all-gather.17.cloned.1.call-start = ((), (), s32[]{:S(2)}) async-start(), calls=%async_computation.7 | async-start | bytes 4227072 | tf_op jit(solution)/shard_map/all_gather | solution.py:104
  9.4 1217.0 %all-gather.19.cloned.1.call-start = ((), (), s32[]{:S(2)}) async-start(), calls=%async_computation.8 | async-start | bytes 4227072 | tf_op jit(solution)/shard_map/all_gather | solution.py:105
  10.0 1523.8 %all-gather.13.cloned.1.call-start = ((), (), s32[]{:S(2)}) async-start(), calls=%async_computation.3 | async-start | bytes 2641920 | tf_op jit(solution)/shard_map/all_gather | solution.py:106
  10.6 1589.8 %reduce-scatter.3.cloned.1.call-start = ((), (), s32[]{:S(2)}) async-start(), calls=%async_computation.4 | async-start | bytes 1179648 | tf_op jit(solution)/shard_map/reduce_scatter | solution.py:292
  10.7 704.9 %copy-start.47 = (f32[128]{0:T(128)}, f32[128]{0:T(128)S(1)}, u32[]{:S(2)}) copy-start(f32[128]{0:T(128)S(1)} %multiply_exponential_fusion) | copy-start | bytes 1540
  13.9 701.6 %copy-start.49 = (f32[128]{0:T(128)}, f32[128]{0:T(128)S(1)}, u32[]{:S(2)}) copy-start(f32[128]{0:T(128)S(1)} %subtract_convert_fusion.3) | copy-start | bytes 1540
  84.8 632.1 %copy-start.39 = (f32[256]{0:T(256)}, f32[256]{0:T(256)S(1)}, u32[]{:S(2)}) copy-start(f32[256]{0:T(256)S(1)} %get-tuple-element.353) | copy-start | bytes 3076
  84.8 701.5 %copy-start.42 = (f32[256]{0:T(256)}, f32[256]{0:T(256)S(1)}, u32[]{:S(2)}) copy-start(f32[256]{0:T(256)S(1)} %get-tuple-element.352) | copy-start | bytes 3076
  399.7 347.2 %copy-start.5 = (bf16[128,640]{1,0:T(8,128)(2,1)S(1)}, bf16[128,640]{1,0:T(8,128)(2,1)}, u32[]{:S(2)}) copy-start(bf16[128,640]{1,0:T(8,128)(2,1)} %param.15) | copy-start | bytes 491524
  399.9 2.7 copy-start.27
  401.3 1.3 copy-start.31
  401.8 379.1 %copy-start.51 = (f32[128]{0:T(128)}, f32[128]{0:T(128)S(1)}, u32[]{:S(2)}) copy-start(f32[128]{0:T(128)S(1)} %get-tuple-element.357) | copy-start | bytes 1540
  402.1 384.3 %copy-start.36 = (f32[128,128]{1,0:T(8,128)}, f32[128,128]{1,0:T(8,128)S(1)}, u32[]{:S(2)}) copy-start(f32[128,128]{1,0:T(8,128)S(1)} %get-tuple-element.351) | copy-start | bytes 196612
  717.6 60.7 %copy-start.29 = (bf16[640,256]{1,0:T(8,128)(2,1)}, bf16[640,256]{1,0:T(8,128)(2,1)S(1)}, u32[]{:S(2)}) copy-start(bf16[640,256]{1,0:T(8,128)(2,1)S(1)} %reshape.524) | copy-start | bytes 983044
  747.0 40.4 %copy-start.9 = (bf16[1024,256]{1,0:T(8,128)(2,1)}, bf16[1024,256]{1,0:T(8,128)(2,1)S(1)}, u32[]{:S(2)}) copy-start(bf16[1024,256]{1,0:T(8,128)(2,1)S(1)} %all_gather.49) | copy-start | bytes 1572868
  781.0 3.3 copy-start.3
  781.4 4.9 copy-start.1
  787.4 1.3 copy-start.11
  790.5 3.1 copy-start.17
  792.5 1.2 copy-start.6
  1538.3 3.2 copy-start.19
  1538.4 3.2 copy-start.23
  1538.4 2.1 copy-start
  1538.4 2.1 copy-start.7
  1538.4 2.1 copy-start.46
  1539.3 2.3 copy-start.35
  1539.3 2.3 copy-start.56
  1540.5 2.0 copy-start.13
  1541.6 1.8 copy-start.22
  1542.5 1.3 copy-start.10
  1542.5 1.3 copy-start.12
  1542.5 1.3 copy-start.44
  1542.5 1.3 copy-start.54
  1542.5 1.3 copy-start.59
  1547.1 2.1 copy-start.33
  1553.5 2.1 copy-start.33
  1556.6 2.4 copy-start.37
  1556.6 2.7 copy-start.2
  1556.6 2.7 copy-start.43
  1559.1 268.6 %all-reduce.17.cloned.1.call-start = ((), (), s32[]{:S(2)}) async-start(), calls=%async_computation.9 | async-start | bytes 34078720
  1559.4 1.0 copy-start.25
  1559.4 1.2 copy-start.26
  1559.4 1.2 copy-start.41
  1560.9 2.1 copy-start.15
  1560.9 2.1 copy-start.18
  1563.0 2.0 copy-start.20
  1564.9 3.2 copy-start.24
  1568.1 33.1 %copy-start.48 = (f32[128]{0:T(128)S(1)}, f32[128]{0:T(128)}, u32[]{:S(2)}) copy-start(f32[128]{0:T(128)} %copy-done.47) | copy-start | bytes 1540
  1568.1 33.1 %copy-start.50 = (f32[128]{0:T(128)S(1)}, f32[128]{0:T(128)}, u32[]{:S(2)}) copy-start(f32[128]{0:T(128)} %copy-done.49) | copy-start | bytes 1540
  1568.1 33.4 %copy-start.32 = (f32[128,256]{1,0:T(8,128)S(1)}, f32[128,256]{1,0:T(8,128)}, u32[]{:S(2)}) copy-start(f32[128,256]{1,0:T(8,128)} %copy-done.31) | copy-start | bytes 393220
  1568.1 33.4 %copy-start.40 = (f32[256]{0:T(256)S(1)}, f32[256]{0:T(256)}, u32[]{:S(2)}) copy-start(f32[256]{0:T(256)} %copy-done.39) | copy-start | bytes 3076
  1568.2 33.4 %copy-start.52 = (f32[128]{0:T(128)S(1)}, f32[128]{0:T(128)}, u32[]{:S(2)}) copy-start(f32[128]{0:T(128)} %copy-done.51) | copy-start | bytes 1540
  1568.2 33.6 %copy-start.57 = (f32[128]{0:T(128)S(1)}, f32[128]{0:T(128)}, u32[]{:S(2)}) copy-start(f32[128]{0:T(128)} %get-tuple-element.356) | copy-start | bytes 1540
  1605.2 869.6 %reduce-scatter.5.cloned.1.call-start = ((), (), s32[]{:S(2)}) async-start(), calls=%async_computation.5 | async-start | bytes 5283840 | tf_op jit(solution)/shard_map/reduce_scatter | solution.py:331
  1609.4 1.3 copy-start.4
  1609.4 1.8 copy-start.8
  1611.3 3.1 copy-start.28
  1611.3 3.4 copy-start.30
  1611.3 3.4 copy-start.38
  1611.3 69.5 %copy-start.55 = (f32[128]{0:T(128)S(1)}, f32[128]{0:T(128)}, u32[]{:S(2)}) copy-start(f32[128]{0:T(128)} %get-tuple-element.354) | copy-start | bytes 1540
  (6 other events, 5.3 us)
Sparse Core Ops, SparseCore 0:
  9.7 302.3 all-gather.14
  313.8 294.5 all-gather.10
  610.0 307.6 all-gather.16
  919.3 307.0 all-gather.18
  1228.0 305.7 all-gather.12
  1559.2 41.1 reduce-scatter.2
  1606.8 220.8 all-reduce.16
  1830.6 644.1 reduce-scatter.4
where the time goes:
time: 2480 us
  waiting for transfers between devices  1540 us (62%)
  blocking collectives  820 us (33%)
  matrix products  45.9 us (2%)
  local copies, waits for them, and re-layouts  40 us (2%)
    reduce_scatter x1, waiting for transfers between devices, body(): lax.psum_scatter(grad_down, ('dp', 'fsdp'), scatter_dimension=0, tiled=True)  641 us
    all_gather x1, blocking collectives, body(): lax.all_gather(shards[1], ('dp', 'fsdp'), axis=0, tiled=True)  315 us
    all_gather x1, blocking collectives, body(): lax.all_gather(shards[2], ('dp', 'fsdp'), axis=0, tiled=True)  313 us
    all_gather x1, waiting for transfers between devices, body(): lax.all_gather(shards[5], ('dp', 'fsdp'), axis=0, tiled=True)  304 us
    all_gather x1, waiting for transfers between devices, body(): lax.all_gather(shards[6], ('dp', 'fsdp'), axis=0, tiled=True)  297 us
    unnamed x9, waiting for transfers between devices  149 us
    unnamed x2, blocking collectives  132 us
    all_gather x1, waiting for transfers between devices, body(): lax.all_gather(shards[4], ('dp', 'fsdp'), axis=0, tiled=True)  124 us
  transfers between devices with their start and end apart: 8, of which 6 were waited for; matrix products, arithmetic and copies ran while one was open for 3% of the time, Pallas kernels for 0%

commit v1 on v0

--- a/solution.py
+++ b/solution.py
@@ -1,14 +1,574 @@
+import functools
 import math
 
 import jax
 import jax.numpy as jnp
 from jax import lax
+from jax.experimental import pallas as pl
+from jax.experimental.pallas import tpu as pltpu
 from jax.sharding import PartitionSpec as P
 
 H = 4
 KV = 1
 HD = 256
 
+MESH = pl.DeviceIdType.MESH
+VMEM_BYTES = 56 * 1024 * 1024
+
+ORDERS = ((0, 1, 2), (1, 2, 0), (2, 0, 1))
+ROWS = (128, 112, 128)
+
+
+def coords():
+    dp = lax.axis_index("dp")
+    fsdp = lax.axis_index("fsdp")
+    return (fsdp // 2, (dp // 2) % 4, (dp // 8) * 2 + fsdp % 2, dp % 2)
+
+
+def device(place):
+    x, y, z, core = place
+    return ((z // 2) * 8 + y * 2 + core, x * 2 + z % 2)
+
+
+def shifted(place, axis, step):
+    moved = list(place)
+    moved[axis] = (place[axis] + step) % 4
+    return tuple(moved)
+
+
+def sibling(place):
+    return place[:3] + (1 - place[3],)
+
+
+def meet(partners):
+    barrier = pltpu.get_barrier_semaphore()
+    for partner in partners:
+        pl.semaphore_signal(barrier, inc=1, device_id=device(partner), device_id_type=MESH)
+    pl.semaphore_wait(barrier, len(partners))
+
+
+def torus_partners(place):
+    partners = [shifted(place, axis, step) for axis in range(3) for step in (1, 2, 3)]
+    return partners + [sibling(place)]
+
+
+def gather_kernel(in0, in1, in2, out0, out1, out2, send, recv, local):
+    place = coords()
+    core = place[3]
+    ins, outs = (in0, in1, in2), (out0, out1, out2)
+    keep = []
+    for s in range(3):
+        ka, kb, kc = (place[axis] for axis in ORDERS[s])
+        copy = pltpu.make_async_copy(ins[s], outs[s].at[core, kc, kb, ka], local.at[s])
+        copy.start()
+        keep.append(copy)
+    meet(torus_partners(place))
+
+    def remote(s, slot, src, dst, to):
+        return pltpu.make_async_remote_copy(
+            src_ref=src,
+            dst_ref=dst,
+            send_sem=send.at[s, slot],
+            recv_sem=recv.at[s, slot],
+            device_id=device(to),
+            device_id_type=MESH,
+        )
+
+    def same(s, slot, ref, to):
+        return remote(s, slot, ref, ref, to)
+
+    sent = []
+    first = []
+    for s in range(3):
+        axis = ORDERS[s][0]
+        ka, kb, kc = (place[a] for a in ORDERS[s])
+        own = outs[s].at[core, kc, kb, ka]
+        copies = [
+            remote(s, step - 1, ins[s], own, shifted(place, axis, step)) for step in (1, 3, 2)
+        ]
+        for copy in copies:
+            copy.start()
+        first.append(copies)
+        sent += copies
+
+    def spread(s, base, axis, whole, part):
+        k = place[axis]
+        right, left = shifted(place, axis, 1), shifted(place, axis, 3)
+        to_right = same(s, base, whole(k), right)
+        to_left = same(s, base + 1, whole(k), left)
+        to_right.start()
+        to_left.start()
+
+        def forward():
+            to_right.wait_recv()
+            on_right = same(s, base + 2, part((k + 3) % 4, 0), right)
+            on_right.start()
+            to_left.wait_recv()
+            on_left = same(s, base + 3, part((k + 1) % 4, 1), left)
+            on_left.start()
+            sent.extend([to_right, to_left, on_right, on_left])
+            return on_right, on_left
+
+        return forward
+
+    forwards = []
+    for s in range(3):
+        keep[s].wait()
+        for copy in first[s]:
+            copy.wait_recv()
+        ka, kb, kc = (place[a] for a in ORDERS[s])
+        out = outs[s]
+        forwards.append(
+            spread(
+                s,
+                3,
+                ORDERS[s][1],
+                lambda k, out=out, kc=kc: out.at[core, kc, k],
+                lambda k, half, out=out, kc=kc: out.at[core, kc, k, pl.ds(2 * half, 2)],
+            )
+        )
+    tails = [forward() for forward in forwards]
+    forwards = []
+    siblings = []
+    for s in range(3):
+        for copy in tails[s]:
+            copy.wait_recv()
+        ka, kb, kc = (place[a] for a in ORDERS[s])
+        out = outs[s]
+        forwards.append(
+            spread(
+                s,
+                7,
+                ORDERS[s][2],
+                lambda k, out=out: out.at[core, k],
+                lambda k, half, out=out: out.at[core, k, pl.ds(2 * half, 2)],
+            )
+        )
+        copy = same(s, 11, out.at[core, kc], sibling(place))
+        copy.start()
+        siblings.append(copy)
+    tails = []
+    for s in range(3):
+        tails.append(forwards[s]())
+        kc = place[ORDERS[s][2]]
+        for slot, k in ((12, (kc + 3) % 4), (13, (kc + 1) % 4)):
+            copy = same(s, slot, outs[s].at[core, k], sibling(place))
+            copy.start()
+            siblings.append(copy)
+    for s in range(3):
+        kc = place[ORDERS[s][2]]
+        for half in range(2):
+            tails[s][half].wait_recv()
+            ref = outs[s].at[core, (kc + 2) % 4, pl.ds(2 * half, 2)]
+            copy = same(s, 14 + half, ref, sibling(place))
+            copy.start()
+            siblings.append(copy)
+    for copy in siblings:
+        copy.wait()
+    for copy in sent:
+        copy.wait_send()
+
+
+def gather_blocks(parts):
+    return pl.pallas_call(
+        gather_kernel,
+        out_shape=[jax.ShapeDtypeStruct((2, 4, 4, 4, rows, 128), jnp.bfloat16) for rows in ROWS],
+        in_specs=[pl.BlockSpec(memory_space=pl.ANY)] * 3,
+        out_specs=[pl.BlockSpec(memory_space=pl.ANY)] * 3,
+        scratch_shapes=[
+            pltpu.SemaphoreType.DMA((3, 16)),
+            pltpu.SemaphoreType.DMA((3, 16)),
+            pltpu.SemaphoreType.DMA((3,)),
+        ],
+        compiler_params=pltpu.CompilerParams(collective_id=0, has_side_effects=True),
+        name="gather_blocks",
+    )(*parts)
+
+
+def add_blocks(total, count, first, *others):
+    def step(i, carry):
+        value = total[first + i].astype(jnp.float32)
+        for other in others:
+            value = value + other(i).astype(jnp.float32)
+        total[first + i] = value.astype(total.dtype)
+        return carry
+
+    lax.fori_loop(0, count, step, 0)
+
+
+def scatter_kernel(in0, in1, in2, out0, out1, out2, *scratch):
+    place = coords()
+    core = place[3]
+    ins, outs = (in0, in1, in2), (out0, out1, out2)
+    own, pair, far, mid, near, send, recv, local = (
+        scratch[0:3],
+        scratch[3:6],
+        scratch[6:9],
+        scratch[9:12],
+        scratch[12:15],
+        scratch[15],
+        scratch[16],
+        scratch[17],
+    )
+    loads = []
+    for s in range(3):
+        copy = pltpu.make_async_copy(ins[s].at[core], own[s], local.at[s])
+        copy.start()
+        loads.append(copy)
+    meet(torus_partners(place))
+    sent = []
+
+    def remote(s, slot, src, dst, to):
+        copy = pltpu.make_async_remote_copy(
+            src_ref=src,
+            dst_ref=dst,
+            send_sem=send.at[s, slot],
+            recv_sem=recv.at[s, slot],
+            device_id=device(to),
+            device_id_type=MESH,
+        )
+        copy.start()
+        sent.append(copy)
+        return copy
+
+    pairs = {}
+    for offset in (2, 1, 3, 0):
+        for s in range(3):
+            kc = place[ORDERS[s][2]]
+            rows = pl.ds(((kc + offset) % 4) * 16, 16)
+            pairs[s, offset] = remote(
+                s, offset, ins[s].at[1 - core, rows], pair[s].at[rows], sibling(place)
+            )
+    for s in range(3):
+        loads[s].wait()
+
+    def reduce_axis(s, axis, base, size, source, inbox, prepare):
+        k = place[axis]
+        right, left = shifted(place, axis, 1), shifted(place, axis, 3)
+        half = size // 2
+
+        def begin():
+            prepare(2)
+            start = ((k + 2) % 4) * size
+            a = remote(s, base, source.at[pl.ds(start, half)], inbox.at[pl.ds(0, half)], right)
+            b = remote(
+                s, base + 1, source.at[pl.ds(start + half, half)], inbox.at[pl.ds(half, half)], left
+            )
+            return a, b
+
+        def middle(pending):
+            a, b = pending
+            prepare(1)
+            start = ((k + 1) % 4) * size
+            a.wait_recv()
+            add_blocks(source, half, start, lambda i: inbox[i])
+            c = remote(
+                s, base + 2, source.at[pl.ds(start, size)], inbox.at[pl.ds(size, size)], right
+            )
+            prepare(3)
+            start = ((k + 3) % 4) * size
+            b.wait_recv()
+            add_blocks(source, half, start + half, lambda i: inbox[half + i])
+            d = remote(
+                s, base + 3, source.at[pl.ds(start, size)], inbox.at[pl.ds(2 * size, size)], left
+            )
+            return c, d
+
+        def end(pending):
+            c, d = pending
+            prepare(0)
+            c.wait_recv()
+            d.wait_recv()
+            add_blocks(
+                source, size, k * size, lambda i: inbox[size + i], lambda i: inbox[2 * size + i]
+            )
+
+        return begin, middle, end
+
+    def prepare_pair(s):
+        def prepare(offset):
+            pairs[s, offset].wait_recv()
+            start = ((place[ORDERS[s][2]] + offset) % 4) * 16
+            add_blocks(own[s], 16, start, lambda i: pair[s][start + i])
+
+        return prepare
+
+    phases = [
+        reduce_axis(s, ORDERS[s][2], 4, 16, own[s], far[s], prepare_pair(s)) for s in range(3)
+    ]
+    state = [phases[s][0]() for s in range(3)]
+    state = [phases[s][1](state[s]) for s in range(3)]
+    for s in range(3):
+        phases[s][2](state[s])
+    phases = [
+        reduce_axis(
+            s,
+            ORDERS[s][1],
+            8,
+            4,
+            own[s].at[pl.ds(place[ORDERS[s][2]] * 16, 16)],
+            mid[s],
+            lambda offset: None,
+        )
+        for s in range(3)
+    ]
+    state = [phases[s][0]() for s in range(3)]
+    state = [phases[s][1](state[s]) for s in range(3)]
+    for s in range(3):
+        phases[s][2](state[s])
+    last = []
+    for s in range(3):
+        axis = ORDERS[s][0]
+        ka, kb, kc = (place[a] for a in ORDERS[s])
+        for step in (1, 3, 2):
+            block = own[s].at[kc * 16 + kb * 4 + (ka + step) % 4]
+            last.append(remote(s, 11 + step, block, near[s].at[step - 1], shifted(place, axis, step)))
+    for s in range(3):
+        ka, kb, kc = (place[a] for a in ORDERS[s])
+        for copy in last[3 * s : 3 * s + 3]:
+            copy.wait_recv()
+        value = own[s][kc * 16 + kb * 4 + ka].astype(jnp.float32)
+        for step in range(3):
+            value = value + near[s][step].astype(jnp.float32)
+        outs[s][...] = value
+    for copy in sent:
+        copy.wait_send()
+
+
+def scatter_blocks(parts):
+    def buffers(count):
+        return [pltpu.VMEM((count, rows, 128), jnp.bfloat16) for rows in ROWS]
+
+    return pl.pallas_call(
+        scatter_kernel,
+        out_shape=[jax.ShapeDtypeStruct((rows, 128), jnp.float32) for rows in ROWS],
+        in_specs=[pl.BlockSpec(memory_space=pl.ANY)] * 3,
+        out_specs=[pl.BlockSpec(memory_space=pltpu.VMEM)] * 3,
+        scratch_shapes=buffers(64)
+        + buffers(64)
+        + buffers(48)
+        + buffers(12)
+        + buffers(3)
+        + [
+            pltpu.SemaphoreType.DMA((3, 15)),
+            pltpu.SemaphoreType.DMA((3, 15)),
+            pltpu.SemaphoreType.DMA((3,)),
+        ],
+        compiler_params=pltpu.CompilerParams(
+            collective_id=1, has_side_effects=True, vmem_limit_bytes=VMEM_BYTES
+        ),
+        name="scatter_blocks",
+    )(*parts)
+
+
+def group_member(place, index):
+    return (index // 2, place[1], (place[2] // 2) * 2 + index % 2, place[3])
+
+
+def group_gather_kernel(block, out, send, recv, local):
+    place = coords()
+    me = lax.axis_index("fsdp")
+    partners = [(lax.axis_index("dp"), (me + step) % 8) for step in range(1, 8)]
+    keep = pltpu.make_async_copy(block, out.at[me], local)
+    keep.start()
+    barrier = pltpu.get_barrier_semaphore()
+    for partner in partners:
+        pl.semaphore_signal(barrier, inc=1, device_id=partner, device_id_type=MESH)
+    pl.semaphore_wait(barrier, 7)
+    copies = []
+    for step in range(7):
+        copy = pltpu.make_async_remote_copy(
+            src_ref=block,
+            dst_ref=out.at[me],
+            send_sem=send.at[step],
+            recv_sem=recv.at[step],
+            device_id=partners[step],
+            device_id_type=MESH,
+        )
+        copy.start()
+        copies.append(copy)
+    keep.wait()
+    for copy in copies:
+        copy.wait()
+
+
+def group_gather(block):
+    return pl.pallas_call(
+        group_gather_kernel,
+        out_shape=jax.ShapeDtypeStruct((8,) + block.shape, block.dtype),
+        in_specs=[pl.BlockSpec(memory_space=pl.ANY)],
+        out_specs=pl.BlockSpec(memory_space=pl.ANY),
+        scratch_shapes=[
+            pltpu.SemaphoreType.DMA((7,)),
+            pltpu.SemaphoreType.DMA((7,)),
+            pltpu.SemaphoreType.DMA,
+        ],
+        compiler_params=pltpu.CompilerParams(collective_id=2, has_side_effects=True),
+        name="group_gather",
+    )(block)
+
+
+def group_scatter_kernel(blocks, out, inbox, send, recv):
+    me = lax.axis_index("fsdp")
+    partners = [(lax.axis_index("dp"), (me + step) % 8) for step in range(1, 8)]
+    barrier = pltpu.get_barrier_semaphore()
+    for partner in partners:
+        pl.semaphore_signal(barrier, inc=1, device_id=partner, device_id_type=MESH)
+    pl.semaphore_wait(barrier, 7)
+    copies = []
+    for step in range(7):
+        copy = pltpu.make_async_remote_copy(
+            src_ref=blocks.at[(me + step + 1) % 8],
+            dst_ref=inbox.at[step],
+            send_sem=send.at[step],
+            recv_sem=recv.at[step],
+            device_id=partners[step],
+            device_id_type=MESH,
+        )
+        copy.start()
+        copies.append(copy)
+    out[...] = blocks[me].astype(jnp.float32)
+    for step in range(7):
+        copies[step].wait_recv()
+        out[...] += inbox[step].astype(jnp.float32)
+    for copy in copies:
+        copy.wait_send()
+
+
+def group_scatter(blocks):
+    rows = blocks.shape[1:]
+    return pl.pallas_call(
+        group_scatter_kernel,
+        out_shape=jax.ShapeDtypeStruct(rows, jnp.float32),
+        in_specs=[pl.BlockSpec(memory_space=pltpu.VMEM)],
+        out_specs=pl.BlockSpec(memory_space=pltpu.VMEM),
+        scratch_shapes=[
+            pltpu.VMEM((7,) + rows, blocks.dtype),
+            pltpu.SemaphoreType.DMA((7,)),
+            pltpu.SemaphoreType.DMA((7,)),
+        ],
+        compiler_params=pltpu.CompilerParams(
+            collective_id=3, has_side_effects=True, vmem_limit_bytes=VMEM_BYTES
+        ),
+        name="group_scatter",
+    )(blocks)
+
+
+def to_devices(blocks, s):
+    rows = blocks.shape[-2]
+    where = {ORDERS[s][0]: 3, ORDERS[s][1]: 2, ORDERS[s][2]: 1}
+    by_place = blocks.transpose(where[2], where[1], 0, where[0], 4, 5)
+    by_place = by_place.reshape(2, 2, 4, 2, 4, rows, 128)
+    return by_place.transpose(0, 2, 3, 4, 1, 5, 6).reshape(128, rows, 128)
+
+
+def from_devices(blocks, s):
+    rows = blocks.shape[-2]
+    by_place = blocks.reshape(2, 4, 2, 4, 2, rows, 128)
+    by_place = by_place.transpose(0, 4, 1, 2, 3, 5, 6).reshape(4, 4, 2, 4, rows, 128)
+    where = {2: 0, 1: 1, 0: 3}
+    a, b, c = (where[axis] for axis in ORDERS[s])
+    return by_place.transpose(2, c, b, a, 4, 5).reshape(2, 64, rows, 128)
+
+
+def lines(block, rows=None):
+    flat = block.reshape(-1)
+    count = -(-flat.shape[0] // 128) if rows is None else rows
+    return jnp.pad(flat, (0, count * 128 - flat.shape[0])).reshape(count, 128)
+
+
+def column_lines(block):
+    r, columns = block.shape
+    return block.reshape(r, columns // 128, 128).transpose(1, 0, 2).reshape(-1, 128)
+
+
+def column_blocks(blocks, r):
+    devices, count, _ = blocks.shape
+    n = count // r
+    return (
+        blocks.reshape(devices, n, r, 128).transpose(0, 2, 1, 3).reshape(devices * r, 128 * n)
+    )
+
+
+def split_columns(matrix, devices):
+    r, n = matrix.shape[0] // devices, matrix.shape[1] // 128
+    return matrix.reshape(devices, r, n, 128).transpose(0, 2, 1, 3).reshape(devices, n * r, 128)
+
+
+def gather_weights(shards):
+    query, key, value, output, gate, up, down, norm_one, norm_two, head_norm = shards
+    vectors = jnp.concatenate([norm_one, norm_two, head_norm])
+    parts = (
+        jnp.concatenate([lines(gate), lines(query), lines(vectors, 8)]),
+        jnp.concatenate([lines(up), lines(key), lines(value), jnp.zeros((12, 128), up.dtype)]),
+        jnp.concatenate([column_lines(down), column_lines(output), jnp.zeros((8, 128), up.dtype)]),
+    )
+    first, second, third = (to_devices(b, s) for s, b in enumerate(gather_blocks(parts)))
+    flat = first[:, 120, :]
+    return (
+        first[:, 80:120].reshape(640, 1024),
+        second[:, 80:90].reshape(640, 256),
+        second[:, 90:100].reshape(640, 256),
+        column_blocks(third[:, 80:120], 8),
+        first[:, :80].reshape(640, 2048),
+        second[:, :80].reshape(640, 2048),
+        column_blocks(third[:, :80], 16),
+        flat[:, 0:5].reshape(640),
+        flat[:, 5:10].reshape(640),
+        flat[:, 10:14].reshape(512),
+    )
+
+
+def scatter_gradients(grads):
+    query, key, value, output, gate, up, down, norm_one, norm_two, head_norm = (
+        grad.astype(jnp.bfloat16) for grad in grads
+    )
+    vectors = jnp.concatenate(
+        [norm_one.reshape(128, 5), norm_two.reshape(128, 5), head_norm.reshape(128, 4)], axis=1
+    )
+    vectors = jnp.pad(vectors, ((0, 0), (0, 114)))[:, None, :]
+    parts = (
+        jnp.concatenate(
+            [
+                gate.reshape(128, 80, 128),
+                query.reshape(128, 40, 128),
+                vectors,
+                jnp.zeros((128, 7, 128), jnp.bfloat16),
+            ],
+            axis=1,
+        ),
+        jnp.concatenate(
+            [
+                up.reshape(128, 80, 128),
+                key.reshape(128, 10, 128),
+                value.reshape(128, 10, 128),
+                jnp.zeros((128, 12, 128), jnp.bfloat16),
+            ],
+            axis=1,
+        ),
+        jnp.concatenate(
+            [
+                split_columns(down, 128),
+                split_columns(output, 128),
+                jnp.zeros((128, 8, 128), jnp.bfloat16),
+            ],
+            axis=1,
+        ),
+    )
+    first, second, third = scatter_blocks([from_devices(p, s) for s, p in enumerate(parts)])
+    flat = first[120]
+    return (
+        first[80:120].reshape(5, 1024),
+        second[80:90].reshape(5, 256),
+        second[90:100].reshape(5, 256),
+        column_blocks(third[None, 80:120], 8),
+        first[:80].reshape(5, 2048),
+        second[:80].reshape(5, 2048),
+        column_blocks(third[None, :80], 16),
+        flat[0:5],
+        flat[5:10],
+        flat[10:14],
+    )
 
 eps_norm = 1e-05
 rope_base = 1000000.0
@@ -96,18 +656,7 @@
     cotangent,
 ):
     shards = (w_query, w_key, w_value, w_out, w_gate, w_up, w_down, attn_gain, ffn_gain, head_gains)
-    weights = (
-        lax.all_gather(shards[0], ("dp", "fsdp"), axis=0, tiled=True),
-        lax.all_gather(shards[1], ("dp", "fsdp"), axis=0, tiled=True),
-        lax.all_gather(shards[2], ("dp", "fsdp"), axis=0, tiled=True),
-        lax.all_gather(shards[3], ("dp", "fsdp"), axis=0, tiled=True),
-        lax.all_gather(shards[4], ("dp", "fsdp"), axis=0, tiled=True),
-        lax.all_gather(shards[5], ("dp", "fsdp"), axis=0, tiled=True),
-        lax.all_gather(shards[6], ("dp", "fsdp"), axis=0, tiled=True),
-        lax.all_gather(shards[7], ("dp", "fsdp"), axis=0, tiled=True),
-        lax.all_gather(shards[8], ("dp", "fsdp"), axis=0, tiled=True),
-        lax.all_gather(shards[9], ("dp", "fsdp"), axis=0, tiled=True),
-    )
+    weights = gather_weights(shards)
     (
         query_mat,
         key_mat,
@@ -171,8 +720,9 @@
         return (jnp.where(allowed, scores, neg_large), allowed)
 
     run_max = jnp.full((KV, group_ratio, tok_rows), neg_large, jnp.float32)
-    key_piece = lax.all_gather(key_flat, "fsdp", axis=0, tiled=True)
-    value_piece = lax.all_gather(value_flat, "fsdp", axis=0, tiled=True)
+    group_kv = group_gather(jnp.concatenate([key_flat, value_flat], axis=1))
+    group_kv = group_kv.reshape(group_rows, 2 * KV * HD)
+    key_piece, value_piece = group_kv[:, : KV * HD], group_kv[:, KV * HD :]
     key_count = key_piece.shape[0]
     scores, allowed = masked_scores(key_piece, jnp.int32(0))
     new_max = jnp.maximum(run_max, jnp.max(scores, axis=-1))
@@ -198,30 +748,6 @@
     block_out = (middle + jnp.dot(hidden, down_mat, preferred_element_type=jnp.float32)).astype(
         jnp.bfloat16
     )
-    weights = (
-        lax.all_gather(shards[0], ("dp", "fsdp"), axis=0, tiled=True),
-        lax.all_gather(shards[1], ("dp", "fsdp"), axis=0, tiled=True),
-        lax.all_gather(shards[2], ("dp", "fsdp"), axis=0, tiled=True),
-        lax.all_gather(shards[3], ("dp", "fsdp"), axis=0, tiled=True),
-        lax.all_gather(shards[4], ("dp", "fsdp"), axis=0, tiled=True),
-        lax.all_gather(shards[5], ("dp", "fsdp"), axis=0, tiled=True),
-        lax.all_gather(shards[6], ("dp", "fsdp"), axis=0, tiled=True),
-        lax.all_gather(shards[7], ("dp", "fsdp"), axis=0, tiled=True),
-        lax.all_gather(shards[8], ("dp", "fsdp"), axis=0, tiled=True),
-        lax.all_gather(shards[9], ("dp", "fsdp"), axis=0, tiled=True),
-    )
-    (
-        query_mat,
-        key_mat,
-        value_mat,
-        output_mat,
-        gate_mat,
-        up_mat,
-        down_mat,
-        norm_one,
-        norm_two,
-        head_norm,
-    ) = weights
     grad_down = contract_rows(hidden, cotangent)
     d_hidden = times_transposed(cotangent, down_mat)
     d_gate = gate_pullback(d_hidden * up_pre)[0].astype(jnp.bfloat16)
@@ -240,10 +766,7 @@
         .transpose(1, 2, 0, 3)
     )
     deltas = jnp.sum(d_attended.astype(jnp.float32) * attended, axis=-1)
-    key_all, value_all = (
-        lax.all_gather(key_flat, "fsdp", axis=0, tiled=True),
-        lax.all_gather(value_flat, "fsdp", axis=0, tiled=True),
-    )
+    key_all, value_all = key_piece, value_piece
     key_block = math.gcd(group_rows, 512)
     block_count = group_rows // key_block
     key_blocks = key_all.reshape(block_count, key_block, KV * HD)
@@ -289,12 +812,9 @@
         jnp.zeros((KV, group_ratio, tok_rows, HD), jnp.float32),
         (key_blocks, value_blocks, block_firsts),
     )
-    kv_sums = lax.psum_scatter(
-        kv_terms.reshape(group_rows, 2 * KV * HD).astype(jnp.bfloat16),
-        "fsdp",
-        scatter_dimension=0,
-        tiled=True,
-    ).astype(jnp.float32)
+    kv_sums = group_scatter(
+        kv_terms.reshape(group_size, tok_rows, 2 * KV * HD).astype(jnp.bfloat16)
+    )
     d_query_rot = grad_queries.transpose(2, 0, 1, 3).reshape(tok_rows, H, HD)
     d_query_raw, grad_query_gain = norm_back(
         rotate_back(d_query_rot, cosines, sine_table),
@@ -321,17 +841,19 @@
     d_norm_one, grad_one = norm_back(d_normed, inputs, scale_one, gain_one, (0,))
     input_grad = d_middle + d_norm_one
     grad_heads = jnp.concatenate([grad_query_gain, grad_key_gain])
-    all_sums = (
-        lax.psum_scatter(grad_query_mat, ("dp", "fsdp"), scatter_dimension=0, tiled=True),
-        lax.psum_scatter(grad_key_mat, ("dp", "fsdp"), scatter_dimension=0, tiled=True),
-        lax.psum_scatter(grad_value_mat, ("dp", "fsdp"), scatter_dimension=0, tiled=True),
-        lax.psum_scatter(grad_output, ("dp", "fsdp"), scatter_dimension=0, tiled=True),
-        lax.psum_scatter(grad_gate, ("dp", "fsdp"), scatter_dimension=0, tiled=True),
-        lax.psum_scatter(grad_up, ("dp", "fsdp"), scatter_dimension=0, tiled=True),
-        lax.psum_scatter(grad_down, ("dp", "fsdp"), scatter_dimension=0, tiled=True),
-        lax.psum_scatter(grad_one, ("dp", "fsdp"), scatter_dimension=0, tiled=True),
-        lax.psum_scatter(grad_two, ("dp", "fsdp"), scatter_dimension=0, tiled=True),
-        lax.psum_scatter(grad_heads, ("dp", "fsdp"), scatter_dimension=0, tiled=True),
+    all_sums = scatter_gradients(
+        (
+            grad_query_mat,
+            grad_key_mat,
+            grad_value_mat,
+            grad_output,
+            grad_gate,
+            grad_up,
+            grad_down,
+            grad_one,
+            grad_two,
+            grad_heads,
+        )
     )
     (
         sum_query,

time: 2480 us -> 283 us (0.11)
  waiting for transfers between devices: 1540 us -> 0 us
  blocking collectives: 820 us -> 0 us
  Pallas kernels: 0 us -> 124 us
  local copies, waits for them, and re-layouts: 40 us -> 92.7 us
    all_gather x5 -> x0, waiting for transfers between devices: 725 us -> none  [the longest x1 304 us: body(): lax.all_gather(shards[5], ('dp', 'fsdp'), axis=0, tiled=True)]
    all_gather x4 -> x0, blocking collectives: 688 us -> none  [the longest x1 315 us: body(): lax.all_gather(shards[1], ('dp', 'fsdp'), axis=0, tiled=True)]
    reduce_scatter x2 -> x0, waiting for transfers between devices: 670 us -> none  [the longest x1 641 us: body(): lax.psum_scatter(grad_down, ('dp', 'fsdp'), scatter_dimension=0, tiled=True)]
    unnamed x9 -> x0, waiting for transfers between devices: 149 us -> none
    unnamed x2 -> x0, blocking collectives: 132 us -> none
    pallas_call x0 -> x4, Pallas kernels: none -> 124 us  [the longest x1 44.4 us: scatter_blocks(): pl.pallas_call(scatter_kernel, out_shape=[jax.ShapeDtypeStruct((rows, 128...]
    reshape x1 -> x23, local copies, waits for them, and re-layouts: 1.04 us -> 32.4 us  [the longest x3 7.67 us: to_devices(): by_place = by_place.reshape(2, 2, 4, 2, 4, rows, 128)]
  transfers between devices with their start and end apart: 8 -> 0, of which waited for: 6 -> 0; matrix products, arithmetic and copies ran while one was open for 3% -> 0% of each run, Pallas kernels for 0% -> 0%
where the time goes in v1:
time: 283 us; the launch traced here: 281 us
  Pallas kernels  124 us (44%)
  local copies, waits for them, and re-layouts  92.7 us (33%)
  matrix products  34.4 us (12%)
  other arithmetic  27.7 us (10%)
    pallas_call x1, Pallas kernels, scatter_blocks(): pl.pallas_call(scatter_kernel, out_shape=[jax.ShapeDtypeStruct((rows, 128...  44.4 us
    pallas_call x1, Pallas kernels, gather_blocks(): pl.pallas_call(gather_kernel, out_shape=[jax.ShapeDtypeStruct((2, 4, 4, 4...  42.9 us
    pallas_call x1, Pallas kernels, group_scatter(): pl.pallas_call(group_scatter_kernel, out_shape=jax.ShapeDtypeStruct(rows,...  20.4 us
    pallas_call x1, Pallas kernels, group_gather(): pl.pallas_call(group_gather_kernel, out_shape=jax.ShapeDtypeStruct((8,) +...  16.3 us
    unnamed x140, local copies, waits for them, and re-layouts  12.1 us
    dot_general x7, matrix products, times_transposed(): lax.dot_general(left, right, (((1,), (1,)), ((), ())), preferred_element_...  8.79 us
    dot_general x7, matrix products, contract_rows(): lax.dot_general(left, right, (((0,), (0,)), ((), ())), preferred_element_...  8.07 us
    reshape x3, local copies, waits for them, and re-layouts, to_devices(): by_place = by_place.reshape(2, 2, 4, 2, 4, rows, 128)  7.67 us

profile of v1, /device:TPU:0, one launch (start us, length us, event | category | flops | bytes accessed | tf_op | source)
XLA Modules:
  0.0 280.9 jit_solution(2769657050536513937)
XLA Ops:
  6.4 1.4 pad_maximum_fusion.5
  10.8 42.9 %gather_blocks.1 = (bf16[2,4,4,4,128,128]{5,4,3,2,1,0:T(8,128)(2,1)}, bf16[2,4,4,4,112,128]{5,4,3,2,1,0:T(8,128)(2,1)}, bf16[2,4,4,4,128,128]{5,4,3,2,1,0:T(8,128)(2,1)}) custom-call(bf16[128,128]{1,0:T(8,128)(2,1)} %get-tuple-element.378.in0, bf16[112,128]{1,0:T(8,128)(2,1)} %maximum_maximum_fusion.1.in1, bf16[128,128]{1,0:T(8,128)(2,1)} %get-tuple-element.379.in2), custom_call_target="tpu_custom_call" | custom-call | tf_op jit(solution)/shard_map/gather_blocks/pallas_call | solution.py:173
  53.7 2.4 copy.157
  56.2 1.8 copy-done.4
  58.4 2.6 copy.155
  61.1 2.0 copy-done.3
  67.3 16.3 %group_gather.1 = bf16[8,128,512]{2,1,0:T(8,128)(2,1)} custom-call(bf16[128,512]{1,0:T(8,128)(2,1)} %pad_maximum_fusion.3.block), custom_call_target="tpu_custom_call" | custom-call | tf_op jit(solution)/shard_map/group_gather/pallas_call | solution.py:396
  83.6 1.5 slice.169
  88.4 1.8 fusion.36
  92.8 2.6 copy.159
  95.4 2.0 copy-done.2
  99.1 3.4 %slice.183 = bf16[128,80,128]{2,1,0:T(8,128)(2,1)} slice(bf16[128,128,128]{2,1,0:T(8,128)(2,1)} %bitcast.299), slice={[0:128], [0:80], [0:128]} | slice | bytes 5242880 | tf_op jit(solution)/shard_map/slice | solution.py:513
  102.6 3.8 %reshape.714 = bf16[640,2048]{1,0:T(8,128)(2,1)S(1)} reshape(bf16[128,80,128]{2,1,0:T(8,128)(2,1)} %slice.183) | data formatting | bytes 5242880 | tf_op jit(solution)/shard_map/reshape | solution.py:513
  106.4 1.6 fusion.132
  108.3 1.5 copy-done.5
  109.8 1.7 slice.184
  111.5 4.0 %reshape.715 = bf16[640,2048]{1,0:T(8,128)(2,1)S(1)} reshape(bf16[128,80,128]{2,1,0:T(8,128)(2,1)} %slice.184) | data formatting | bytes 5242880 | tf_op jit(solution)/shard_map/reshape | solution.py:514
  116.1 1.9 slice.185
  118.0 1.7 copy.160
  119.7 1.6 multiply_convert_fusion
  121.4 1.3 fusion.45
  122.7 1.0 copy-done.1
  123.7 0.9 fusion.134
  124.7 1.6 multiply_reduce_fusion.4
  127.2 1.4 broadcast_in_dim.105
  128.5 2.3 fusion.129
  132.3 1.9 convolution_convert_fusion.7
  134.8 17.9 %while.15 = (s32[]{:T(128)}, f32[1,4,128,256]{3,2,1,0:T(8,128)S(1)}, bf16[2,512,512]{1,2,0:T(8,128)(2,1)}, s32[128]{0:T(128)S(1)}, s32[2]{0:T(128)}, /*index=5*/...) while((s32[]{:T(128)}, ...), condition=%wide.region_15.16_spmd.clone, body=%wide.region_13.15_spmd.clone.sunk | while | flops 675089536 | bytes 19808032 | solution.py:810
  134.9 1.3 dynamic_slice.39
  137.7 1.4 fusion.193
  139.5 1.5 fusion.195
  141.4 1.3 fusion.196
  142.7 1.0 copy-done.32
  143.8 1.3 dynamic_slice.39
  146.7 1.4 fusion.193
  148.4 1.5 fusion.195
  150.3 1.3 fusion.196
  151.7 1.0 copy-done.32
  152.7 1.0 multiply_add_fusion
  154.6 1.0 subtract_convert_fusion
  155.8 1.3 fusion.135
  157.1 2.4 copy.167
  159.5 20.4 %group_scatter.1 = f32[128,512]{1,0:T(8,128)} custom-call(bf16[8,128,512]{2,1,0:T(8,128)(2,1)} %bitcast.309), custom_call_target="tpu_custom_call" | custom-call | tf_op jit(solution)/shard_map/group_scatter/pallas_call | solution.py:440
  181.8 1.3 fusion.72
  185.4 1.4 concatenate.112
  186.9 2.4 convolution_convert_fusion.2
  189.2 3.9 %concatenate.111 = bf16[2,4,2,4,2,80,128]{6,5,4,3,2,1,0:T(8,128)(2,1)S(1)} reshape(bf16[640,2048]{1,0:T(8,128)(2,1)} %convolution_convert_fusion.2) | data formatting | bytes 5242880 | tf_op jit(solution)/shard_map/concatenate | solution.py:531
  193.2 2.7 maximum_bitcast_fusion.1
  195.9 2.3 copy.169
  198.6 1.0 concatenate.121
  199.9 1.0 concatenate.120
  201.0 1.9 convolution_convert_fusion.1
  202.9 3.1 %concatenate.119 = bf16[2,4,2,4,2,80,128]{6,5,4,3,2,1,0:T(8,128)(2,1)} reshape(bf16[640,2048]{1,0:T(8,128)(2,1)S(1)} %convolution_convert_fusion.1) | data formatting | bytes 5242880 | tf_op jit(solution)/shard_map/concatenate | solution.py:540
  206.0 2.7 maximum_bitcast_fusion.3
  208.7 2.3 copy.170
  211.0 1.6 convolution_convert_fusion.3
  213.5 4.3 %reshape.727 = bf16[128,16,5,128]{3,2,1,0:T(8,128)(2,1)} reshape(bf16[2048,640]{1,0:T(8,128)(2,1)S(1)} %convolution_convert_fusion) | data formatting | bytes 5242880 | tf_op jit(solution)/shard_map/reshape | solution.py:495
  217.8 2.8 %copy.171 = bf16[128,5,16,128]{3,2,1,0:T(8,128)(2,1)S(1)} copy(bf16[128,5,16,128]{3,1,2,0:T(8,128)(2,1)} %bitcast.296) | data formatting | bytes 5242880 | tf_op jit(solution)/shard_map/transpose | solution.py:495
  220.7 1.3 maximum_bitcast_fusion.2
  222.6 2.3 copy.173
  224.9 44.4 %scatter_blocks.1 = (f32[128,128]{1,0:T(8,128)}, f32[112,128]{1,0:T(8,128)}, f32[128,128]{1,0:T(8,128)}) custom-call(bf16[2,64,128,128]{3,2,1,0:T(8,128)(2,1)} %bitcast.293, bf16[2,64,112,128]{3,2,1,0:T(8,128)(2,1)} %bitcast.302, bf16[2,64,128,128]{3,2,1,0:T(8,128)(2,1)} %bitcast.294), custom_call_target="tpu_custom_call" | custom-call | tf_op jit(solution)/shard_map/scatter_blocks/pallas_call | solution.py:342
  272.7 1.3 slice_bitcast_fusion.4
  278.3 1.3 slice_bitcast_fusion.6
  279.7 1.3 slice_bitcast_fusion.5
  (259 shorter events, 44.0 us)
Async XLA Ops:
  5.6 50.6 %copy-start.64 = (bf16[128]{0:T(256)(128)(2,1)}, bf16[128]{0:T(256)(128)(2,1)S(1)}, u32[]{:S(2)}) copy-start(bf16[128]{0:T(256)(128)(2,1)S(1)} %pad.38.clone) | copy-start | bytes 772
  10.1 46.1 %copy-start.66 = (bf16[112]{0:T(256)(128)(2,1)}, bf16[112]{0:T(256)(128)(2,1)S(1)}, u32[]{:S(2)}) copy-start(bf16[112]{0:T(256)(128)(2,1)S(1)} %pad.42.clone) | copy-start | bytes 676
  56.2 1.8 copy-start.4
  58.4 5.7 %copy-start.26 = (bf16[640,256]{1,0:T(8,128)(2,1)}, bf16[640,256]{1,0:T(8,128)(2,1)S(1)}, u32[]{:S(2)}) copy-start(bf16[640,256]{1,0:T(8,128)(2,1)S(1)} %reshape.708) | copy-start | bytes 983044
  58.4 5.0 %copy-start.8 = (bf16[128,640]{1,0:T(8,128)(2,1)S(1)}, bf16[128,640]{1,0:T(8,128)(2,1)}, u32[]{:S(2)}) copy-start(bf16[128,640]{1,0:T(8,128)(2,1)} %param.15) | copy-start | bytes 491524
  61.1 2.0 copy-start.3
  64.1 22.3 %copy-start.44 = (f32[128]{0:T(128)}, f32[128]{0:T(128)S(1)}, u32[]{:S(2)}) copy-start(f32[128]{0:T(128)S(1)} %get-tuple-element.363) | copy-start | bytes 1540
  64.6 18.9 %copy-start.24 = (bf16[640,256]{1,0:T(8,128)(2,1)}, bf16[640,256]{1,0:T(8,128)(2,1)S(1)}, u32[]{:S(2)}) copy-start(bf16[640,256]{1,0:T(8,128)(2,1)S(1)} %reshape.707) | copy-start | bytes 983044
  65.0 18.6 %copy-start.29 = (f32[128,256]{1,0:T(8,128)}, f32[128,256]{1,0:T(8,128)S(1)}, u32[]{:S(2)}) copy-start(f32[128,256]{1,0:T(8,128)S(1)} %get-tuple-element.371) | copy-start | bytes 393220
  65.2 20.5 %copy-start.46 = (f32[256]{0:T(256)}, f32[256]{0:T(256)S(1)}, u32[]{:S(2)}) copy-start(f32[256]{0:T(256)S(1)} %slice.137) | copy-start | bytes 3076
  65.8 17.8 %copy-start.58 = (f32[128]{0:T(128)}, f32[128]{0:T(128)S(1)}, u32[]{:S(2)}) copy-start(f32[128]{0:T(128)S(1)} %multiply_exponential_fusion) | copy-start | bytes 1540
  66.3 17.3 %copy-start.61 = (f32[128]{0:T(128)}, f32[128]{0:T(128)S(1)}, u32[]{:S(2)}) copy-start(f32[128]{0:T(128)S(1)} %subtract_convert_fusion.3) | copy-start | bytes 1540
  85.7 2.3 copy-start.6
  85.7 2.3 copy-start.59
  85.7 2.3 copy-start.62
  87.2 3.0 %copy-start.48 = (f32[256]{0:T(256)}, f32[256]{0:T(256)S(1)}, u32[]{:S(2)}) copy-start(f32[256]{0:T(256)S(1)} %slice.132) | copy-start | bytes 3076
  88.0 2.3 copy-start.39
  88.3 2.6 copy-start.36
  88.4 2.6 copy-start.40
  88.4 2.6 copy-start.42
  88.4 2.6 copy-start.15
  92.8 2.6 copy-start.16
  95.4 2.0 copy-start.2
  106.4 1.9 copy-start
  106.4 3.4 %copy-start.5 = (bf16[2,2,4,2,4,112,128]{6,5,1,4,3,2,0:T(8,128)(2,1)S(1)}, bf16[2,2,4,2,4,112,128]{6,5,1,4,3,2,0:T(8,128)(2,1)}, u32[]{:S(2)}) copy-start(bf16[2,2,4,2,4,112,128]{6,5,1,4,3,2,0:T(8,128)(2,1)} %copy-done.4) | copy-start | bytes 11010052
  118.0 1.7 copy-start.33
  118.0 1.7 copy-start.34
  121.3 3.3 %copy-start.21 = (bf16[128,2048]{1,0:T(8,128)(2,1)}, bf16[128,2048]{1,0:T(8,128)(2,1)S(1)}, u32[]{:S(2)}) copy-start(bf16[128,2048]{1,0:T(8,128)(2,1)S(1)} %get-tuple-element.338) | copy-start | bytes 1572868
  121.3 3.3 %copy-start.37 = (bf16[128,2048]{1,0:T(8,128)(2,1)}, bf16[128,2048]{1,0:T(8,128)(2,1)S(1)}, u32[]{:S(2)}) copy-start(bf16[128,2048]{1,0:T(8,128)(2,1)S(1)} %get-tuple-element.339) | copy-start | bytes 1572868
  121.4 3.3 %copy-start.18 = (bf16[128,2048]{1,0:T(8,128)(2,1)}, bf16[128,2048]{1,0:T(8,128)(2,1)S(1)}, u32[]{:S(2)}) copy-start(bf16[128,2048]{1,0:T(8,128)(2,1)S(1)} %get-tuple-element.337) | copy-start | bytes 1572868
  121.4 2.4 copy-start.1
  122.7 2.0 copy-start.55
  126.3 4.5 %copy-start.41 = (bf16[128,1,4,128]{3,0,2,1:T(8,128)(2,1)S(1)}, bf16[128,1,4,128]{3,0,2,1:T(8,128)(2,1)}, u32[]{:S(2)}) copy-start(bf16[128,1,4,128]{3,0,2,1:T(8,128)(2,1)} %copy-done.40) | copy-start | bytes 393220
  126.3 4.5 %copy-start.43 = (bf16[128,1,4,128]{3,0,2,1:T(8,128)(2,1)S(1)}, bf16[128,1,4,128]{3,0,2,1:T(8,128)(2,1)}, u32[]{:S(2)}) copy-start(bf16[128,1,4,128]{3,0,2,1:T(8,128)(2,1)} %copy-done.42) | copy-start | bytes 393220
  126.3 5.4 %copy-start.51 = (f32[4,128]{1,0:T(4,128)S(1)}, f32[4,128]{1,0:T(4,128)}, u32[]{:S(2)}) copy-start(f32[4,128]{1,0:T(4,128)} %copy-done.50) | copy-start | bytes 6148
  126.3 5.4 %copy-start.53 = (f32[4,128]{1,0:T(4,128)S(1)}, f32[4,128]{1,0:T(4,128)}, u32[]{:S(2)}) copy-start(f32[4,128]{1,0:T(4,128)} %copy-done.52) | copy-start | bytes 6148
  126.5 7.8 %copy-start.13 = (f32[128,640]{1,0:T(8,128)}, f32[128,640]{1,0:T(8,128)S(1)}, u32[]{:S(2)}) copy-start(f32[128,640]{1,0:T(8,128)S(1)} %subtract_add_fusion) | copy-start | bytes 983044
  130.8 3.9 %copy-start.20 = (f32[1,4,128,256]{3,2,1,0:T(8,128)S(1)}, f32[1,4,128,256]{3,2,1,0:T(8,128)}, u32[]{:S(2)}) copy-start(f32[1,4,128,256]{3,2,1,0:T(8,128)} %copy-done.19) | copy-start | bytes 1572868
  134.8 4.3 %copy-start.9 = (bf16[2,512,256]{2,1,0:T(8,128)(2,1)S(1)}, bf16[2,512,256]{2,1,0:T(8,128)(2,1)}, u32[]{:S(2)}) copy-start(bf16[2,512,256]{2,1,0:T(8,128)(2,1)} %get-tuple-element.498) | copy-start | bytes 1572868 | tf_op jit(solution)/shard_map/while
  139.5 3.2 %copy-start.31 = (bf16[2,512,512]{1,2,0:T(8,128)(2,1)S(1)}, bf16[2,512,512]{1,2,0:T(8,128)(2,1)}, u32[]{:S(2)}) copy-start(bf16[2,512,512]{1,2,0:T(8,128)(2,1)} %get-tuple-element.476) | copy-start | bytes 3145732 | tf_op jit(solution)/shard_map/while
  143.8 4.3 %copy-start.9 = (bf16[2,512,256]{2,1,0:T(8,128)(2,1)S(1)}, bf16[2,512,256]{2,1,0:T(8,128)(2,1)}, u32[]{:S(2)}) copy-start(bf16[2,512,256]{2,1,0:T(8,128)(2,1)} %get-tuple-element.498) | copy-start | bytes 1572868 | tf_op jit(solution)/shard_map/while
  148.4 3.2 %copy-start.31 = (bf16[2,512,512]{1,2,0:T(8,128)(2,1)S(1)}, bf16[2,512,512]{1,2,0:T(8,128)(2,1)}, u32[]{:S(2)}) copy-start(bf16[2,512,512]{1,2,0:T(8,128)(2,1)} %get-tuple-element.476) | copy-start | bytes 3145732 | tf_op jit(solution)/shard_map/while
  152.7 3.1 %copy-start.7 = (bf16[640,1024]{1,0:T(8,128)(2,1)S(1)}, bf16[640,1024]{1,0:T(8,128)(2,1)}, u32[]{:S(2)}) copy-start(bf16[640,1024]{1,0:T(8,128)(2,1)} %copy-done.6) | copy-start | bytes 3932164
  155.8 25.0 %copy-start.60 = (f32[128]{0:T(128)S(1)}, f32[128]{0:T(128)}, u32[]{:S(2)}) copy-start(f32[128]{0:T(128)} %copy-done.58) | copy-start | bytes 1540
  155.8 25.0 %copy-start.63 = (f32[128]{0:T(128)S(1)}, f32[128]{0:T(128)}, u32[]{:S(2)}) copy-start(f32[128]{0:T(128)} %copy-done.61) | copy-start | bytes 1540
  155.8 25.4 %copy-start.30 = (f32[128,256]{1,0:T(8,128)S(1)}, f32[128,256]{1,0:T(8,128)}, u32[]{:S(2)}) copy-start(f32[128,256]{1,0:T(8,128)} %copy-done.29) | copy-start | bytes 393220
  155.8 25.4 %copy-start.47 = (f32[256]{0:T(256)S(1)}, f32[256]{0:T(256)}, u32[]{:S(2)}) copy-start(f32[256]{0:T(256)} %copy-done.46) | copy-start | bytes 3076
  155.8 25.4 %copy-start.57 = (f32[128]{0:T(128)S(1)}, f32[128]{0:T(128)}, u32[]{:S(2)}) copy-start(f32[128]{0:T(128)} %copy-done.56) | copy-start | bytes 1540
  155.8 25.5 %copy-start.70 = (f32[128]{0:T(128)S(1)}, f32[128]{0:T(128)}, u32[]{:S(2)}) copy-start(f32[128]{0:T(128)} %get-tuple-element.364) | copy-start | bytes 1540
  157.1 24.4 %copy-start.25 = (bf16[640,256]{1,0:T(8,128)(2,1)S(1)}, bf16[640,256]{1,0:T(8,128)(2,1)}, u32[]{:S(2)}) copy-start(bf16[640,256]{1,0:T(8,128)(2,1)} %copy-done.24) | copy-start | bytes 983044
  157.1 24.4 %copy-start.28 = (f32[128,640]{1,0:T(8,128)S(1)}, f32[128,640]{1,0:T(8,128)}, u32[]{:S(2)}) copy-start(f32[128,640]{1,0:T(8,128)} %fusion.135) | copy-start | bytes 983044
  157.1 24.6 %copy-start.27 = (bf16[640,256]{1,0:T(8,128)(2,1)S(1)}, bf16[640,256]{1,0:T(8,128)(2,1)}, u32[]{:S(2)}) copy-start(bf16[640,256]{1,0:T(8,128)(2,1)} %copy-done.26) | copy-start | bytes 983044
  157.1 24.6 %copy-start.45 = (f32[128]{0:T(128)S(1)}, f32[128]{0:T(128)}, u32[]{:S(2)}) copy-start(f32[128]{0:T(128)} %copy-done.44) | copy-start | bytes 1540
  159.5 23.6 %copy-start.14 = (f32[128,640]{1,0:T(8,128)S(1)}, f32[128,640]{1,0:T(8,128)}, u32[]{:S(2)}) copy-start(f32[128,640]{1,0:T(8,128)} %copy-done.13) | copy-start | bytes 983044
  159.5 23.6 %copy-start.68 = (f32[128]{0:T(128)S(1)}, f32[128]{0:T(128)}, u32[]{:S(2)}) copy-start(f32[128]{0:T(128)} %get-tuple-element.362) | copy-start | bytes 1540
  179.9 4.3 %copy-start.49 = (bf16[640]{0:T(1024)(128)(2,1)S(1)}, bf16[640]{0:T(1024)(128)(2,1)}, u32[]{:S(2)}) copy-start(bf16[640]{0:T(1024)(128)(2,1)} %get-tuple-element.301) | copy-start | bytes 3844
  184.0 2.9 %copy-start.22 = (bf16[128,2048]{1,0:T(8,128)(2,1)S(1)}, bf16[128,2048]{1,0:T(8,128)(2,1)}, u32[]{:S(2)}) copy-start(bf16[128,2048]{1,0:T(8,128)(2,1)} %copy-done.21) | copy-start | bytes 1572868
  195.9 2.3 copy-start.23
  202.9 3.1 %copy-start.67 = (bf16[112]{0:T(256)(128)(2,1)S(1)}, bf16[112]{0:T(256)(128)(2,1)}, u32[]{:S(2)}) copy-start(bf16[112]{0:T(256)(128)(2,1)} %copy-done.66) | copy-start | bytes 676
  208.7 2.3 copy-start.17
  208.7 3.9 %copy-start.35 = (bf16[128,640]{1,0:T(8,128)(2,1)S(1)}, bf16[128,640]{1,0:T(8,128)(2,1)}, u32[]{:S(2)}) copy-start(bf16[128,640]{1,0:T(8,128)(2,1)} %param.27) | copy-start | bytes 491524
  208.7 3.9 %copy-start.38 = (bf16[128,2048]{1,0:T(8,128)(2,1)S(1)}, bf16[128,2048]{1,0:T(8,128)(2,1)}, u32[]{:S(2)}) copy-start(bf16[128,2048]{1,0:T(8,128)(2,1)} %copy-done.37) | copy-start | bytes 1572868
  217.8 2.9 %copy-start.12 = (bf16[1024,640]{1,0:T(8,128)(2,1)S(1)}, bf16[1024,640]{1,0:T(8,128)(2,1)}, u32[]{:S(2)}) copy-start(bf16[1024,640]{1,0:T(8,128)(2,1)} %convolution_convert_fusion.3) | copy-start | bytes 3932164
  217.8 2.9 %copy-start.65 = (bf16[128]{0:T(256)(128)(2,1)S(1)}, bf16[128]{0:T(256)(128)(2,1)}, u32[]{:S(2)}) copy-start(bf16[128]{0:T(256)(128)(2,1)} %copy-done.64) | copy-start | bytes 772
  (10 other events, 10.5 us)

commit v2 on v0

v2 whole, which is shorter than its diff:
```python
import math

import jax
import jax.numpy as jnp
from jax import lax
from jax.experimental import pallas as pl
from jax.experimental.pallas import tpu as pltpu
from jax.sharding import PartitionSpec as P

H = 4
HD = 256
D = 640
FF = 2048
TOK = 128
GROUP = 8
KEYS = TOK * GROUP
EPS = 1e-05
ROPE_BASE = 1000000.0
NEG = -1e30
SCORE_SCALE = 1.0 / math.sqrt(HD)
F32 = jnp.float32
BF16 = jnp.bfloat16

MESH = pl.DeviceIdType.MESH
VMEM_BYTES = 60 * 1024 * 1024

ORDERS = ((0, 1, 2), (1, 2, 0), (2, 0, 1))
ROWS = ((48, 32, 48), (80, 80, 80))
GAIN_ROW = 40


def coords():
    dp = lax.axis_index("dp")
    fsdp = lax.axis_index("fsdp")
    return (fsdp // 2, (dp // 2) % 4, (dp // 8) * 2 + fsdp % 2, dp % 2)


def device(place):
    x, y, z, core = place
    return ((z // 2) * 8 + y * 2 + core, x * 2 + z % 2)


def shifted(place, axis, step):
    moved = list(place)
    moved[axis] = (place[axis] + step) % 4
    return tuple(moved)


def sibling(place):
    return place[:3] + (1 - place[3],)


def group_partner(step):
    return (lax.axis_index("dp"), (lax.axis_index("fsdp") + step) % GROUP)


def meet(place):
    partners = [device(shifted(place, axis, step)) for axis in range(3) for step in (1, 2, 3)]
    partners.append(device(sibling(place)))
    x, y, z, core = place
    flipped = (x, y, (z // 2) * 2 + (1 - z % 2), core)
    partners += [device(shifted(flipped, 0, step)) for step in (1, 2, 3)]
    barrier = pltpu.get_barrier_semaphore()
    for partner in partners:
        pl.semaphore_signal(barrier, inc=1, device_id=partner, device_id_type=MESH)
    pl.semaphore_wait(barrier, len(partners))


def remote(src, dst, send, recv, to):
    copy = pltpu.make_async_remote_copy(
        src_ref=src, dst_ref=dst, send_sem=send, recv_sem=recv, device_id=to, device_id_type=MESH
    )
    copy.start()
    return copy


class Gather:
    def __init__(self, place, bufs, send, recv):
        self.place, self.bufs, self.send, self.recv = place, bufs, send, recv
        self.sent, self.pair = [], []
        self.kept = [None] * 3

    def copy(self, s, slot, ref, to, keep=None):
        copy = remote(ref, ref, self.send.at[s, slot], self.recv.at[s, slot], device(to))
        (self.sent if keep is None else keep).append(copy)
        return copy

    def at(self, s):
        return tuple(self.place[axis] for axis in ORDERS[s])

    def blocks(self, s, first, count):
        return self.bufs[s].at[self.place[3], pl.ds(first, count)]

    def own(self):
        for s in range(3):
            ka, kb, kc = self.at(s)
            ref = self.blocks(s, kc * 16 + kb * 4 + ka, 1)
            axis = ORDERS[s][0]
            self.kept[s] = [
                self.copy(s, step - 1, ref, shifted(self.place, axis, step)) for step in (1, 3, 2)
            ]

    def to_both(self, s, slot, axis, ref):
        return [
            self.copy(s, slot, ref, shifted(self.place, axis, 1)),
            self.copy(s, slot + 1, ref, shifted(self.place, axis, 3)),
        ]

    def second(self):
        for s in range(3):
            for copy in self.kept[s]:
                copy.wait_recv()
            ka, kb, kc = self.at(s)
            self.kept[s] = self.to_both(s, 3, ORDERS[s][1], self.blocks(s, kc * 16 + kb * 4, 4))

    def second_on(self):
        for s in range(3):
            ka, kb, kc = self.at(s)
            axis = ORDERS[s][1]
            from_left, from_right = self.kept[s]
            from_left.wait_recv()
            right = self.copy(
                s, 5, self.blocks(s, kc * 16 + (kb + 3) % 4 * 4, 2), shifted(self.place, axis, 1)
            )
            from_right.wait_recv()
            left = self.copy(
                s,
                6,
                self.blocks(s, kc * 16 + (kb + 1) % 4 * 4 + 2, 2),
                shifted(self.place, axis, 3),
            )
            self.kept[s] = [right, left]

    def third(self):
        for s in range(3):
            for copy in self.kept[s]:
                copy.wait_recv()
            ka, kb, kc = self.at(s)
            ref = self.blocks(s, kc * 16, 16)
            self.kept[s] = self.to_both(s, 7, ORDERS[s][2], ref)
            self.copy(s, 11, ref, sibling(self.place), self.pair)

    def third_on(self):
        for s in range(3):
            ka, kb, kc = self.at(s)
            axis = ORDERS[s][2]
            from_left, from_right = self.kept[s]
            from_left.wait_recv()
            start = (kc + 3) % 4 * 16
            right = self.copy(s, 9, self.blocks(s, start, 8), shifted(self.place, axis, 1))
            self.copy(s, 12, self.blocks(s, start, 16), sibling(self.place), self.pair)
            from_right.wait_recv()
            start = (kc + 1) % 4 * 16
            left = self.copy(s, 10, self.blocks(s, start + 8, 8), shifted(self.place, axis, 3))
            self.copy(s, 13, self.blocks(s, start, 16), sibling(self.place), self.pair)
            self.kept[s] = [right, left]

    def last(self):
        for s in range(3):
            ka, kb, kc = self.at(s)
            for half in range(2):
                self.kept[s][half].wait_recv()
                ref = self.blocks(s, (kc + 2) % 4 * 16 + 8 * half, 8)
                self.copy(s, 14 + half, ref, sibling(self.place), self.pair)

    def finish(self):
        for copy in self.pair:
            copy.wait()
        for copy in self.sent:
            copy.wait_send()


def add_blocks(total, count, first, other):
    def step(i, carry):
        total[first + i] = total[first + i] + other(i)
        return carry

    lax.fori_loop(0, count, step, 0, unroll=4)


def add_two(total, count, first, one, two):
    def step(i, carry):
        value = total[first + i].astype(F32) + one(i).astype(F32) + two(i).astype(F32)
        total[first + i] = value.astype(BF16)
        return carry

    lax.fori_loop(0, count, step, 0, unroll=4)


class Scatter:
    def __init__(self, place, bufs, pair, far, mid, near, outs, send, recv):
        self.place, self.bufs, self.pair_in = place, bufs, pair
        self.far_in, self.mid_in, self.near_in, self.outs = far, mid, near, outs
        self.send, self.recv = send, recv
        self.sent, self.pairs = [], {}
        self.kept = [None] * 3

    def copy(self, s, slot, src, dst, to):
        copy = remote(src, dst, self.send.at[s, slot], self.recv.at[s, slot], device(to))
        self.sent.append(copy)
        return copy

    def at(self, s):
        return tuple(self.place[axis] for axis in ORDERS[s])

    def own(self, s):
        return self.bufs[s].at[self.place[3]]

    def to_pair(self, streams=(0, 1, 2)):
        core = self.place[3]
        for offset in (2, 1, 3, 0):
            for s in streams:
                rows = pl.ds((self.at(s)[2] + offset) % 4 * 16, 16)
                self.pairs[s, offset] = self.copy(
                    s,
                    offset,
                    self.bufs[s].at[1 - core, rows],
                    self.pair_in[s].at[rows],
                    sibling(self.place),
                )

    def add_pair(self, s, offset):
        self.pairs[s, offset].wait_recv()
        start = (self.at(s)[2] + offset) % 4 * 16
        pair = self.pair_in[s]
        add_blocks(self.own(s), 16, start, lambda i: pair[start + i])

    def level(self, s, far):
        ka, kb, kc = self.at(s)
        if far:
            return ORDERS[s][2], kc, 0, 16, 4, self.far_in[s]
        return ORDERS[s][1], kb, kc * 16, 4, 8, self.mid_in[s]

    def begin(self, far):
        for s in range(3):
            axis, k, base, size, slot, inbox = self.level(s, far)
            half = size // 2
            if far:
                self.add_pair(s, 2)
            start = base + (k + 2) % 4 * size
            own = self.own(s)
            self.kept[s] = (
                self.copy(
                    s,
                    slot,
                    own.at[pl.ds(start, half)],
                    inbox.at[pl.ds(0, half)],
                    shifted(self.place, axis, 1),
                ),
                self.copy(
                    s,
                    slot + 1,
                    own.at[pl.ds(start + half, half)],
                    inbox.at[pl.ds(half, half)],
                    shifted(self.place, axis, 3),
                ),
            )

    def middle(self, far):
        for s in range(3):
            axis, k, base, size, slot, inbox = self.level(s, far)
            half = size // 2
            own = self.own(s)
            if far:
                self.add_pair(s, 1)
            start = base + (k + 1) % 4 * size
            self.kept[s][0].wait_recv()
            add_blocks(own, half, start, lambda i: inbox[i])
            right = self.copy(
                s,
                slot + 2,
                own.at[pl.ds(start, size)],
                inbox.at[pl.ds(size, size)],
                shifted(self.place, axis, 1),
            )
            if far:
                self.add_pair(s, 3)
            start = base + (k + 3) % 4 * size
            self.kept[s][1].wait_recv()
            add_blocks(own, half, start + half, lambda i: inbox[half + i])
            left = self.copy(
                s,
                slot + 3,
                own.at[pl.ds(start, size)],
                inbox.at[pl.ds(2 * size, size)],
                shifted(self.place, axis, 3),
            )
            self.kept[s] = (right, left)

    def end(self, far):
        for s in range(3):
            axis, k, base, size, slot, inbox = self.level(s, far)
            if far:
                self.add_pair(s, 0)
            for copy in self.kept[s]:
                copy.wait_recv()
            add_two(
                self.own(s),
                size,
                base + k * size,
                lambda i: inbox[size + i],
                lambda i: inbox[2 * size + i],
            )

    def to_owners(self):
        for s in range(3):
            ka, kb, kc = self.at(s)
            axis = ORDERS[s][0]
            own = self.own(s)
            self.kept[s] = [
                self.copy(
                    s,
                    11 + step,
                    own.at[kc * 16 + kb * 4 + (ka + step) % 4],
                    self.near_in[s].at[step - 1],
                    shifted(self.place, axis, step),
                )
                for step in (1, 3, 2)
            ]

    def finish(self):
        for s in range(3):
            ka, kb, kc = self.at(s)
            for copy in self.kept[s]:
                copy.wait_recv()
            value = self.own(s)[kc * 16 + kb * 4 + ka].astype(F32)
            for step in range(3):
                value = value + self.near_in[s][step].astype(F32)
            self.outs[s][...] = value
        for copy in self.sent:
            copy.wait_send()


def one_hot(rows, columns, pick):
    i = lax.broadcasted_iota(jnp.int32, (rows, columns), 0)
    j = lax.broadcasted_iota(jnp.int32, (rows, columns), 1)
    return jnp.where(pick(i) == j, 1.0, 0.0)


def dot(left, right):
    return jnp.dot(left, right, preferred_element_type=F32)


def dot_nt(left, right):
    return lax.dot_general(left, right, (((1,), (1,)), ((), ())), preferred_element_type=F32)


def dot_tn(left, right):
    return lax.dot_general(left, right, (((0,), (0,)), ((), ())), preferred_element_type=F32)


def stack_columns(shard):
    r, columns = shard.shape
    value = shard.astype(F32)
    pad = [jnp.zeros((8 - r, 128), F32)] if r < 8 else []
    pieces = []
    for c in range(columns // 128):
        pieces += [value[:, c * 128 : (c + 1) * 128]] + pad
    return jnp.concatenate(pieces, axis=0)


def row_order(rows, n):
    shift = n.bit_length() - 1
    return one_hot(rows, 8 * n, lambda i: jnp.where(i < 5 * n, (i & (n - 1)) * 8 + (i >> shift), -1))


def block_index(s, g, d):
    z_hi, y = g // 4, g % 4
    core, x, z_lo = d // 8, (d // 2) % 4, d % 2
    place = (x, y, z_hi * 2 + z_lo)
    a, b, c = (place[axis] for axis in ORDERS[s])
    return core, c * 16 + b * 4 + a


def rms(value):
    return lax.rsqrt(jnp.mean(value * value, axis=-1, keepdims=True) + EPS)


def rotate(value, cosines, sines):
    half = HD // 2
    u, w = value[:, :half], value[:, half:]
    return jnp.concatenate([u * cosines - w * sines, w * cosines + u * sines], axis=1)


def norm_back(grad, value, scale, gain):
    scaled = grad * gain
    back = scale * scaled - value * scale**3 * jnp.mean(scaled * value, axis=-1, keepdims=True)
    return back, jnp.sum(grad * value * scale, axis=0, keepdims=True)


def split_dot_nt(value, matrix):
    high = value.astype(BF16)
    low = (value - high.astype(F32)).astype(BF16)
    return dot_nt(high, matrix) + dot_nt(low, matrix)


def block_kernel(
    tokens,
    cotangent,
    lengths,
    w_query,
    w_key,
    w_value,
    w_out,
    w_gate,
    w_up,
    w_down,
    gains,
    block_out,
    input_grad,
    sum_a0,
    sum_a1,
    sum_a2,
    sum_b0,
    sum_b1,
    sum_b2,
    a0,
    a1,
    a2,
    b0,
    b1,
    b2,
    *scratch,
):
    it = iter(scratch)

    def take(count):
        return [next(it) for _ in range(count)]

    pair_a, pair_b = take(3), take(3)
    far_a, far_b = take(3), take(3)
    mid_a, mid_b = take(3), take(3)
    near_a, near_b = take(3), take(3)
    q_mat, kv_mat, o_mat, g_mat, u_mat, d_mat = take(6)
    perm, flip, pick, gain_cols, gain_rows = take(5)
    cos_ref, sin_ref, allowed_ref = take(3)
    normed, ffn_in, middle = take(3)
    q_raw, kv_raw, queries, kv_all = take(4)
    probs, attended, attended_low, d_attended, d_scores = take(5)
    hidden, d_gate, d_up, d_acc = take(4)
    d_kv, kv_in, d_q_low, d_kv_low = take(4)
    gather_send, gather_recv, scatter_send, scatter_recv = take(4)
    kv_send, kv_recv, dkv_send, dkv_recv = take(4)

    place = coords()
    core = place[3]
    me = lax.axis_index("fsdp")
    bufs_a, bufs_b = (a0, a1, a2), (b0, b1, b2)

    def own_ref(bufs, s):
        ka, kb, kc = (place[axis] for axis in ORDERS[s])
        return bufs[s].at[core, kc * 16 + kb * 4 + ka]

    packed = dot(row_order(48, 8).astype(BF16), stack_columns(w_query[...]).astype(BF16))
    packed = jnp.concatenate([packed[:GAIN_ROW], gains[...]], axis=0)
    own_ref(bufs_a, 0)[...] = packed.astype(BF16)
    both = jnp.concatenate([stack_columns(w_key[...]), stack_columns(w_value[...])], axis=0)
    own_ref(bufs_a, 1)[...] = dot(row_order(32, 4).astype(BF16), both.astype(BF16)).astype(BF16)
    packed = jnp.concatenate([stack_columns(w_out[...]), jnp.zeros((8, 128), F32)], axis=0)
    own_ref(bufs_a, 2)[...] = packed.astype(BF16)
    order = row_order(80, 16).astype(BF16)
    own_ref(bufs_b, 0)[...] = dot(order, stack_columns(w_gate[...]).astype(BF16)).astype(BF16)
    own_ref(bufs_b, 1)[...] = dot(order, stack_columns(w_up[...]).astype(BF16)).astype(BF16)
    down = w_down[...]
    own_ref(bufs_b, 2)[...] = jnp.concatenate(
        [down[:, c * 128 : (c + 1) * 128] for c in range(5)], axis=0
    )

    meet(place)
    ga = Gather(place, bufs_a, gather_send.at[0], gather_recv.at[0])
    gb = Gather(place, bufs_b, gather_send.at[1], gather_recv.at[1])
    sa = Scatter(
        place,
        bufs_a,
        pair_a,
        far_a,
        mid_a,
        near_a,
        (sum_a0, sum_a1, sum_a2),
        scatter_send.at[0],
        scatter_recv.at[0],
    )
    sb = Scatter(
        place,
        bufs_b,
        pair_b,
        far_b,
        mid_b,
        near_b,
        (sum_b0, sum_b1, sum_b2),
        scatter_send.at[1],
        scatter_recv.at[1],
    )

    ga.own()
    gb.own()

    perm[...] = one_hot(256, 256, lambda i: (i & 15) * 16 + (i >> 4)).astype(BF16)
    flip[...] = one_hot(
        256, 256, lambda i: ((i & 127) >> 3) * 16 + (i >> 7) * 8 + (i & 7)
    ).astype(BF16)
    row = lax.broadcasted_iota(jnp.int32, (D, D), 0)
    column = lax.broadcasted_iota(jnp.int32, (D, D), 1)
    pick[...] = jnp.where(row == 5 * (column & 127) + (column >> 7), 1.0, 0.0).astype(BF16)
    ga.second()
    first_len, second_len = lengths[0, 0], lengths[0, 1]
    first_end, second_end = first_len, first_len + second_len

    def segment(ids):
        past_one = jnp.where(ids >= first_end, 1, 0)
        past_two = jnp.where(ids >= second_end, 1, 0)
        return past_one + past_two, ids - past_one * first_len - past_two * second_len

    ids = me * TOK + lax.broadcasted_iota(jnp.int32, (TOK, HD // 2), 0)
    lane = lax.broadcasted_iota(jnp.int32, (TOK, HD // 2), 1).astype(F32)
    angles = segment(ids)[1].astype(F32) * jnp.exp(lane * (2.0 / HD) * (-math.log(ROPE_BASE)))
    cos_ref[...] = jnp.cos(angles)
    sin_ref[...] = jnp.sin(angles)
    ga.second_on()
    row_ids = me * TOK + lax.broadcasted_iota(jnp.int32, (TOK, KEYS), 0)
    key_ids = lax.broadcasted_iota(jnp.int32, (TOK, KEYS), 1)
    same = segment(row_ids)[0] == segment(key_ids)[0]
    allowed_ref[...] = jnp.where(same & (key_ids <= row_ids), 1.0, 0.0)
    ga.third()
    gb.second()
    inputs = tokens[...].astype(F32)
    scale_one = rms(inputs)
    ga.third_on()
    ga.last()
    gb.second_on()
    ga.finish()

    def slab(bufs, s, g, j):
        tiles = []
        for d in range(16):
            c, index = block_index(s, g, d)
            tiles.append(bufs[s][c, index, pl.ds(j * 16, 16), :])
        return jnp.concatenate(tiles, axis=0)

    def turn(matrix, parts):
        out = dot(matrix, jnp.concatenate(parts, axis=1)).astype(BF16)
        return [out[:, i * 128 : (i + 1) * 128] for i in range(len(parts))]

    def tiles_wide(block, first, count):
        return jnp.concatenate(
            [block[(first + i) * 16 : (first + i + 1) * 16] for i in range(count)], axis=1
        )

    def unpack_a(g, carry):
        at = pl.ds(pl.multiple_of(g * 16, 16), 16)

        def rows(r):
            return pl.ds(pl.multiple_of(r * 128 + g * 16, 16), 16)

        q0, q1 = turn(perm[...], [slab(bufs_a, 0, g, 0), slab(bufs_a, 0, g, 1)])
        q2, kv0 = turn(perm[...], [slab(bufs_a, 0, g, 2), slab(bufs_a, 1, g, 0)])
        (kv1,) = turn(perm[...], [slab(bufs_a, 1, g, 1)])
        for r, (block, first) in enumerate(((q0, 0), (q0, 8), (q1, 0), (q1, 8), (q2, 0))):
            q_mat[rows(r), :] = tiles_wide(block, first, 8)
        gain_cols[at, :] = q2[8 * 16 : 9 * 16].astype(F32)
        for r in range(4):
            kv_mat[rows(r), :] = tiles_wide(kv0, 4 * r, 4)
        kv_mat[rows(4), :] = tiles_wide(kv1, 0, 4)
        return carry

    lax.fori_loop(0, 8, unpack_a, 0)

    def unpack_out(g, carry):
        o0, o1 = turn(flip[...], [slab(bufs_a, 2, g, 0), slab(bufs_a, 2, g, 1)])
        (o2,) = turn(flip[...], [slab(bufs_a, 2, g, 2)])
        o_mat[pl.ds(pl.multiple_of(g * 128, 128), 128), :] = jnp.concatenate(
            [o0[:128], o0[128:], o1[:128], o1[128:], o2[:128]], axis=1
        )
        return carry

    turned = gain_cols[...].T

    def natural(first, count):
        spread = jnp.concatenate([turned[first + i : first + i + 1] for i in range(count)], axis=1)
        return spread.astype(BF16)

    gain_rows[0:1, :] = dot_nt(natural(0, 5), pick[...])
    gain_rows[1:2, :] = dot_nt(natural(5, 5), pick[...])
    head_row = lax.broadcasted_iota(jnp.int32, (512, 512), 0)
    head_column = lax.broadcasted_iota(jnp.int32, (512, 512), 1)
    head_pick = jnp.where(
        head_row == 4 * (head_column & 127) + (head_column >> 7), 1.0, 0.0
    ).astype(BF16)
    gain_rows[2:3, 0:512] = dot_nt(natural(10, 4), head_pick)

    normed_nat = (inputs * scale_one * gain_rows[0:1, :]).astype(BF16)
    normed[...] = dot(normed_nat, pick[...]).astype(BF16)
    kv_raw[...] = dot(normed[...], kv_mat[...])
    key_gain = gain_rows[2:3, HD : 2 * HD]
    query_gain = gain_rows[2:3, 0:HD]
    cosines, sines = cos_ref[...], sin_ref[...]
    key_raw = kv_raw[:, 0:HD]
    key_rot = rotate(key_raw * rms(key_raw) * key_gain, cosines, sines)
    mine = pl.ds(pl.multiple_of(me * TOK, TOK), TOK)
    kv_all[mine, :] = jnp.concatenate([key_rot, kv_raw[:, HD:]], axis=1).astype(BF16)
    kv_copies = [
        remote(
            kv_all.at[mine],
            kv_all.at[mine],
            kv_send.at[step - 1],
            kv_recv.at[step - 1],
            group_partner(step),
        )
        for step in range(1, GROUP)
    ]
    gb.third()
    q_raw[...] = dot(normed[...], q_mat[...])
    for h in range(H):
        raw = q_raw[:, h * HD : (h + 1) * HD]
        rot = rotate(raw * rms(raw) * query_gain, cosines, sines)
        queries[h * TOK : (h + 1) * TOK, :] = rot.astype(BF16)
    lax.fori_loop(0, 8, unpack_out, 0)
    for copy in kv_copies:
        copy.wait()
    gb.third_on()

    def attend(h, carry):
        rows = pl.ds(pl.multiple_of(h * TOK, TOK), TOK)
        allowed = allowed_ref[...]
        scores = dot_nt(queries[rows, :], kv_all[:, 0:HD]) * SCORE_SCALE
        scores = jnp.where(allowed > 0.0, scores, NEG)
        peak = jnp.max(scores, axis=-1, keepdims=True)
        expd = jnp.exp(scores - peak) * allowed
        low = (expd * (1.0 / jnp.sum(expd, axis=-1, keepdims=True))).astype(BF16)
        probs[rows, :] = low
        value = dot(low, kv_all[:, HD : 2 * HD])
        attended[rows, :] = value
        attended_low[:, pl.ds(pl.multiple_of(h * HD, HD), HD)] = value.astype(BF16)
        return carry

    lax.fori_loop(0, H, attend, 0)
    gb.last()
    middle[...] = inputs + dot(attended_low[...], o_mat[...])
    scale_two = rms(middle[...])
    ffn_nat = (middle[...] * scale_two * gain_rows[1:2, :]).astype(BF16)
    ffn_in[...] = dot(ffn_nat, pick[...]).astype(BF16)
    gb.finish()

    def unpack_b(g, carry):
        for mat, s in ((g_mat, 0), (u_mat, 1)):
            slabs = [slab(bufs_b, s, g, j) for j in range(5)]
            turned_slabs = turn(perm[...], slabs[0:2])
            turned_slabs += turn(perm[...], slabs[2:4])
            turned_slabs += turn(perm[...], slabs[4:5])
            for r in range(5):
                mat[pl.ds(pl.multiple_of(r * 128 + g * 16, 16), 16), :] = tiles_wide(
                    turned_slabs[r], 0, 16
                )
        for d in range(16):
            c, index = block_index(2, g, d)
            block = bufs_b[2][c, index]
            d_mat[pl.ds(pl.multiple_of(g * 256 + d * 16, 16), 16), :] = tiles_wide(block, 0, 5)
        return carry

    lax.fori_loop(0, 8, unpack_b, 0)

    block_out[...] = middle[...]
    d_acc[...] = jnp.zeros_like(d_acc)
    root = math.sqrt(2.0 / math.pi)

    def feed(n, carry):
        at = pl.ds(pl.multiple_of(n * 512, 512), 512)
        gate = dot(ffn_in[...], g_mat[:, at])
        up = dot(ffn_in[...], u_mat[:, at])
        d_hidden = dot_nt(cotangent[...], d_mat[at, :])
        square = gate * gate
        tanh = jnp.tanh(root * gate * (1.0 + 0.044715 * square))
        lift = 0.5 * (1.0 + tanh)
        act = gate * lift
        slope = lift + 0.5 * gate * (1.0 - tanh * tanh) * root * (1.0 + 3 * 0.044715 * square)
        hid = (act * up).astype(BF16)
        dg = (d_hidden * up * slope).astype(BF16)
        du = (d_hidden * act).astype(BF16)
        hidden[:, at] = hid
        d_gate[:, at] = dg
        d_up[:, at] = du
        block_out[...] += dot(hid, d_mat[at, :])
        d_acc[...] += dot_nt(dg, g_mat[:, at]) + dot_nt(du, u_mat[:, at])
        return carry

    lax.fori_loop(0, 4, feed, 0)

    def put(bufs, s, g, j, block):
        for d in range(16):
            c, index = block_index(s, g, d)
            bufs[s][c, index, pl.ds(j * 16, 16), :] = block[d * 16 : (d + 1) * 16]

    def down_grads(g, carry):
        at = pl.ds(pl.multiple_of(g * 256, 256), 256)
        grad = dot_tn(hidden[:, at], cotangent[...]).astype(BF16)
        for d in range(16):
            c, index = block_index(2, g, d)
            rows = grad[d * 16 : (d + 1) * 16]
            bufs_b[2][c, index] = jnp.concatenate(
                [rows[:, i * 128 : (i + 1) * 128] for i in range(5)], axis=0
            )
        return carry

    def stack(grad, g, count):
        rows = grad[g * 16 : (g + 1) * 16]
        return [rows[:, i * 128 : (i + 1) * 128] for i in range(count)]

    def wide_grads(s, source):
        def step(r, carry):
            at = pl.ds(pl.multiple_of(r * 128, 128), 128)
            grad = dot_tn(ffn_in[:, at], source[...]).astype(BF16)
            for g in range(0, 8, 2):
                one, two = turn(
                    perm[...],
                    [jnp.concatenate(stack(grad, g + i, 16), axis=0) for i in range(2)],
                )
                put(bufs_b, s, g, r, one)
                put(bufs_b, s, g + 1, r, two)
            return carry

        lax.fori_loop(0, 5, step, 0)

    lax.fori_loop(0, 8, down_grads, 0)
    sb.to_pair((2,))
    wide_grads(0, d_gate)
    sb.to_pair((0,))
    wide_grads(1, d_up)
    sb.to_pair((1,))

    d_ffn = split_dot_nt(d_acc[...], pick[...])
    d_norm, grad_two = norm_back(d_ffn, middle[...], scale_two, gain_rows[1:2, :])
    d_middle = cotangent[...].astype(F32) + d_norm
    input_grad[...] = d_middle
    d_branch = d_middle.astype(BF16)
    d_attended_flat = dot_nt(d_branch, o_mat[...]).astype(BF16)
    for h in range(H):
        d_attended[h * TOK : (h + 1) * TOK, :] = d_attended_flat[:, h * HD : (h + 1) * HD]
    sb.begin(True)

    def scores_back(h, carry):
        rows = pl.ds(pl.multiple_of(h * TOK, TOK), TOK)
        upstream = d_attended[rows, :]
        delta = jnp.sum(upstream.astype(F32) * attended[rows, :], axis=-1, keepdims=True)
        d_probs = dot_nt(upstream, kv_all[:, HD : 2 * HD])
        d_scores[rows, :] = (probs[rows, :].astype(F32) * (d_probs - delta)).astype(BF16)
        return carry

    lax.fori_loop(0, H, scores_back, 0)

    def keys_back(n, carry):
        at = pl.ds(pl.multiple_of(n * 256, 256), 256)
        d_keys = dot_tn(d_scores[:, at], queries[...]) * SCORE_SCALE
        d_values = dot_tn(probs[:, at], d_attended[...])
        d_kv[at, :] = jnp.concatenate([d_keys, d_values], axis=1).astype(BF16)
        return carry

    lax.fori_loop(0, KEYS // 256, keys_back, 0)
    dkv_copies = [
        remote(
            d_kv.at[pl.ds(pl.multiple_of((me + step) % GROUP * TOK, TOK), TOK)],
            kv_in.at[step - 1],
            dkv_send.at[step - 1],
            dkv_recv.at[step - 1],
            group_partner(step),
        )
        for step in range(1, GROUP)
    ]
    sb.middle(True)

    def back_rotated(grad):
        return rotate(grad, cosines, -sines)

    query_gain_grad = jnp.zeros((1, HD), F32)
    for h in range(H):
        rows = slice(h * TOK, (h + 1) * TOK)
        d_rot = dot(d_scores[rows, :], kv_all[:, 0:HD]) * SCORE_SCALE
        raw = q_raw[:, h * HD : (h + 1) * HD]
        d_raw, gain_grad = norm_back(back_rotated(d_rot), raw, rms(raw), query_gain)
        query_gain_grad = query_gain_grad + gain_grad
        d_q_low[:, h * HD : (h + 1) * HD] = d_raw.astype(BF16)

    def out_grads(g, carry):
        at = pl.ds(pl.multiple_of(g * 128, 128), 128)
        grad = dot_tn(attended_low[:, at], d_branch).astype(BF16)
        cols = [grad[:, i * 128 : (i + 1) * 128] for i in range(5)]
        slabs = [
            jnp.concatenate(cols[0:2], axis=0),
            jnp.concatenate(cols[2:4], axis=0),
            jnp.concatenate([cols[4], jnp.zeros((128, 128), BF16)], axis=0),
        ]
        turned_back = dot_tn(flip[...], jnp.concatenate(slabs, axis=1)).astype(BF16)
        for j in range(3):
            put(bufs_a, 2, g, j, turned_back[:, j * 128 : (j + 1) * 128])
        return carry

    lax.fori_loop(0, 8, out_grads, 0)
    sa.to_pair((2,))
    sb.end(True)
    sb.begin(False)

    total = d_kv[mine, :].astype(F32)
    for step in range(GROUP - 1):
        dkv_copies[step].wait_recv()
        total = total + kv_in[step].astype(F32)
    key_raw = kv_raw[:, 0:HD]
    d_key_raw, key_gain_grad = norm_back(
        back_rotated(total[:, 0:HD]), key_raw, rms(key_raw), key_gain
    )
    d_kv_low[...] = jnp.concatenate([d_key_raw, total[:, HD:]], axis=1).astype(BF16)
    sb.middle(False)
    d_normed = split_dot_nt(
        dot_nt(d_q_low[...], q_mat[...]) + dot_nt(d_kv_low[...], kv_mat[...]), pick[...]
    )
    d_norm, grad_one = norm_back(d_normed, inputs, scale_one, gain_rows[0:1, :])
    input_grad[...] += d_norm

    def by_device(row, count, matrix):
        turned_row = dot(row.astype(BF16), matrix)
        return [turned_row[:, i * 128 : (i + 1) * 128] for i in range(count)]

    heads = jnp.concatenate([query_gain_grad, key_gain_grad], axis=1)
    gain_parts = by_device(grad_one, 5, pick[...]) + by_device(grad_two, 5, pick[...])
    gain_parts += by_device(heads, 4, head_pick)
    gain_parts.append(jnp.zeros((114, 128), F32))
    gain_cols[...] = jnp.concatenate(gain_parts, axis=0).T

    def grads_a(g, carry):
        at = pl.ds(pl.multiple_of(g * 16, 16), 16)
        q_rows, kv_rows = [], []
        for r in range(5):
            rows = pl.ds(pl.multiple_of(r * 128 + g * 16, 16), 16)
            q_row, kv_row = q_mat[rows, :], kv_mat[rows, :]
            q_rows += [q_row[:, i * 128 : (i + 1) * 128] for i in range(8)]
            kv_rows += [kv_row[:, i * 128 : (i + 1) * 128] for i in range(4)]
        zero = jnp.zeros((16, 128), BF16)
        q_rows += [gain_cols[at, :].astype(BF16)] + [zero] * 7
        kv_rows += [zero] * 12
        slabs = [jnp.concatenate(q_rows[i * 16 : (i + 1) * 16], axis=0) for i in range(3)]
        slabs += [jnp.concatenate(kv_rows[i * 16 : (i + 1) * 16], axis=0) for i in range(2)]
        out = turn(perm[...], slabs[0:2]) + turn(perm[...], slabs[2:4]) + turn(perm[...], slabs[4:5])
        for j in range(3):
            put(bufs_a, 0, g, j, out[j])
        for j in range(2):
            put(bufs_a, 1, g, j, out[3 + j])
        return carry

    q_mat[...] = dot_tn(normed[...], d_q_low[...]).astype(BF16)
    kv_mat[...] = dot_tn(normed[...], d_kv_low[...]).astype(BF16)
    lax.fori_loop(0, 8, grads_a, 0)
    sa.to_pair((0, 1))
    sb.end(False)
    sb.to_owners()
    sa.begin(True)
    sa.middle(True)
    sb.finish()
    sa.end(True)
    sa.begin(False)
    sa.middle(False)
    sa.end(False)
    sa.to_owners()
    for copy in dkv_copies:
        copy.wait_send()
    sa.finish()


def finish_kernel(a0, a1, a2, b0, b1, b2, out, grad, block_out, input_grad, *outs):
    query, key, value, output, gate, up, down, vectors = outs
    block_out[...] = out[...].astype(BF16)
    input_grad[...] = grad[...]

    def exact(order, block):
        return lax.dot_general(
            order,
            block,
            (((0,), (0,)), ((), ())),
            precision=lax.Precision.HIGHEST,
            preferred_element_type=F32,
        )

    def spread(ref, stacked, first, count):
        for c in range(count):
            ref[:, c * 128 : (c + 1) * 128] = stacked[(first + c) * 8 : (first + c) * 8 + 5]

    spread(query, exact(row_order(48, 8), a0[...]), 0, 8)
    stacked = exact(row_order(32, 4), a1[...])
    spread(key, stacked, 0, 2)
    spread(value, stacked, 2, 2)
    for c in range(5):
        output[:, c * 128 : (c + 1) * 128] = a2[c * 8 : (c + 1) * 8]
        down[:, c * 128 : (c + 1) * 128] = b2[c * 16 : (c + 1) * 16]
    order = row_order(80, 16)
    spread(gate, exact(order, b0[...]), 0, 16)
    spread(up, exact(order, b1[...]), 0, 16)
    vectors[...] = a0[GAIN_ROW : GAIN_ROW + 8]


def vmem_specs(count):
    return [pl.BlockSpec(memory_space=pltpu.VMEM)] * count


def body(
    tokens,
    w_query,
    w_key,
    w_value,
    w_out,
    w_gate,
    w_up,
    w_down,
    attn_gain,
    ffn_gain,
    head_gains,
    lengths,
    cotangent,
):
    gains = jnp.concatenate([attn_gain, ffn_gain, head_gains]).astype(F32)
    gains = jnp.pad(gains[None, :], ((0, 7), (0, 114)))

    def low(*shape):
        return pltpu.VMEM(shape, BF16)

    def full(*shape):
        return pltpu.VMEM(shape, F32)

    phases = [[low(2, 64, rows, 128) for rows in phase] for phase in ROWS]
    inboxes = [
        [low(count, rows, 128) for rows in phase] for count in (64, 48, 12, 3) for phase in ROWS
    ]
    scratch = sum(phases, []) + sum(inboxes, [])
    scratch += [low(D, 1024), low(D, 512), low(1024, D), low(D, FF), low(D, FF), low(FF, D)]
    scratch += [low(256, 256), low(256, 256), low(D, D), full(128, 128), full(8, D)]
    scratch += [full(TOK, 128), full(TOK, 128), full(TOK, KEYS)]
    scratch += [low(TOK, D), low(TOK, D), full(TOK, D)]
    scratch += [full(TOK, 1024), full(TOK, 512), low(H * TOK, HD), low(KEYS, 2 * HD)]
    scratch += [low(H * TOK, KEYS), full(H * TOK, HD), low(TOK, 1024), low(H * TOK, HD)]
    scratch += [low(H * TOK, KEYS), low(TOK, FF), low(TOK, FF), low(TOK, FF), full(TOK, D)]
    scratch += [low(KEYS, 2 * HD), low(GROUP - 1, TOK, 2 * HD), low(TOK, 1024), low(TOK, 512)]
    dma = pltpu.SemaphoreType.DMA
    scratch += [dma((2, 3, 16)), dma((2, 3, 16)), dma((2, 3, 15)), dma((2, 3, 15))]
    scratch += [dma((7,)), dma((7,)), dma((7,)), dma((7,))]
    out, grad, *sums = pl.pallas_call(
        block_kernel,
        out_shape=[jax.ShapeDtypeStruct((TOK, D), F32)] * 2
        + [jax.ShapeDtypeStruct((rows, 128), F32) for phase in ROWS for rows in phase],
        in_specs=vmem_specs(2) + [pl.BlockSpec(memory_space=pltpu.SMEM)] + vmem_specs(8),
        out_specs=vmem_specs(8),
        scratch_shapes=scratch,
        compiler_params=pltpu.CompilerParams(
            collective_id=0, has_side_effects=True, vmem_limit_bytes=VMEM_BYTES
        ),
        name="block",
    )(
        tokens,
        cotangent,
        lengths,
        w_query,
        w_key,
        w_value,
        w_out,
        w_gate,
        w_up,
        w_down,
        gains,
    )
    shards = [
        jax.ShapeDtypeStruct(shape, F32)
        for shape in ((5, 1024), (5, 256), (5, 256), (8, D), (5, FF), (5, FF), (16, D), (8, 128))
    ]
    *results, vectors = pl.pallas_call(
        finish_kernel,
        out_shape=[jax.ShapeDtypeStruct((TOK, D), BF16), jax.ShapeDtypeStruct((TOK, D), F32)]
        + shards,
        in_specs=vmem_specs(8),
        out_specs=vmem_specs(10),
        name="finish",
    )(*sums, out, grad)
    flat = vectors[0]
    return (*results, flat[0:5], flat[5:10], flat[10:14])


def solution(mesh):
    rows = P(("dp", "fsdp"), None)
    vector = P(("dp", "fsdp"))
    return jax.shard_map(
        body,
        mesh=mesh,
        in_specs=(rows,) * 8 + (vector,) * 3 + (P("dp", None), rows),
        out_specs=(rows,) * 9 + (vector,) * 3,
        check_vma=False,
    )
```

time: 2480 us -> 155 us (0.06)
  waiting for transfers between devices: 1540 us -> 0 us
  blocking collectives: 820 us -> 0 us
  Pallas kernels: 0 us -> 150 us
  matrix products: 45.9 us -> 0 us
  local copies, waits for them, and re-layouts: 40 us -> 3.25 us
    all_gather x5 -> x0, waiting for transfers between devices: 725 us -> none  [the longest x1 304 us: body(): lax.all_gather(shards[5], ('dp', 'fsdp'), axis=0, tiled=True)]
    all_gather x4 -> x0, blocking collectives: 688 us -> none  [the longest x1 315 us: body(): lax.all_gather(shards[1], ('dp', 'fsdp'), axis=0, tiled=True)]
    reduce_scatter x2 -> x0, waiting for transfers between devices: 670 us -> none  [the longest x1 641 us: body(): lax.psum_scatter(grad_down, ('dp', 'fsdp'), scatter_dimension=0, tiled=True)]
    pallas_call x0 -> x2, Pallas kernels: none -> 150 us  [the longest x1 148 us: body(): pl.pallas_call(block_kernel, out_shape=[jax.ShapeDtypeStruct((TOK, D), F3...]
    unnamed x9 -> x0, waiting for transfers between devices: 149 us -> none
    unnamed x2 -> x0, blocking collectives: 132 us -> none
    dot_general x33 -> x0, matrix products: 45.9 us -> none  [the longest x7 17 us: contract_rows(): lax.dot_general(left, right, (((0,), (0,)), ((), ())), preferred_element_...]
    unnamed x142 -> x6, local copies, waits for them, and re-layouts: 32.1 us -> 0.66 us
  transfers between devices with their start and end apart: 8 -> 0, of which waited for: 6 -> 0; matrix products, arithmetic and copies ran while one was open for 3% -> 0% of each run, Pallas kernels for 0% -> 0%
where the time goes in v2:
time: 155 us
  Pallas kernels  150 us (97%)
  local copies, waits for them, and re-layouts  3.25 us (2%)
    pallas_call x1, Pallas kernels, body(): pl.pallas_call(block_kernel, out_shape=[jax.ShapeDtypeStruct((TOK, D), F3...  148 us

profile of v2, /device:TPU:0, one launch (start us, length us, event | category | flops | bytes accessed | tf_op | source)
XLA Modules:
  0.0 154.7 jit_solution(776598391021422604)
XLA Ops:
  0.6 0.0 copy-start
  0.7 0.0 copy-start.1
  0.7 0.0 copy-start.2
  0.7 0.6 copy-done
  1.3 0.0 copy-done.1
  1.3 0.0 copy-done.2
  1.3 0.7 fusion.9.gains
  2.0 147.8 %block.1 = (f32[128,640]{1,0:T(8,128)}, f32[128,640]{1,0:T(8,128)}, f32[48,128]{1,0:T(8,128)}, f32[32,128]{1,0:T(8,128)}, f32[48,128]{1,0:T(8,128)}, /*index=5*/...) custom-call(bf16[128,640]{1,0:T(8,128)(2,1)} %tokens.1, bf16[128,640]{1,0:T(8,128)(2,1)} %cotangent.1, ...), custom_call_target="tpu_custom_call" | custom-call | tf_op jit(solution)/shard_map/block/pallas_call | solution.py:941
  149.8 2.3 %finish.1 = (bf16[128,640]{1,0:T(8,128)(2,1)}, f32[128,640]{1,0:T(8,128)}, f32[5,1024]{1,0:T(8,128)}, f32[5,256]{1,0:T(8,128)}, f32[5,256]{1,0:T(8,128)}, /*inde...) custom-call(f32[48,128]{1,0:T(8,128)} %get-tuple-element.30.a0, ...), custom_call_target="tpu_custom_call" | custom-call | tf_op jit(solution)/shard_map/finish/pallas_call | solution.py:969
  152.1 1.3 slice_bitcast_fusion
  153.3 1.3 slice_bitcast_fusion.1
Async XLA Ops:
  0.6 0.7 copy-start
  0.7 0.7 copy-start.1
  0.7 0.7 copy-start.2

commit v3 on v2

v3 whole, which is shorter than its diff:
```python
import math

import jax
import jax.numpy as jnp
from jax import lax
from jax.experimental import pallas as pl
from jax.experimental.pallas import tpu as pltpu
from jax.sharding import PartitionSpec as P

H = 4
HD = 256
D = 640
FF = 2048
TOK = 128
GROUP = 8
KEYS = TOK * GROUP
EPS = 1e-05
ROPE_BASE = 1000000.0
NEG = -1e30
SCORE_SCALE = 1.0 / math.sqrt(HD)
F32 = jnp.float32
BF16 = jnp.bfloat16

MESH = pl.DeviceIdType.MESH
VMEM_BYTES = 60 * 1024 * 1024

ORDERS = ((0, 1, 2), (1, 2, 0), (2, 0, 1))
ROWS = ((32, 32, 48), (80, 80, 80))
GAIN_ROW = 28


def coords():
    dp = lax.axis_index("dp")
    fsdp = lax.axis_index("fsdp")
    return (fsdp // 2, (dp // 2) % 4, (dp // 8) * 2 + fsdp % 2, dp % 2)


def device(place):
    x, y, z, core = place
    return ((z // 2) * 8 + y * 2 + core, x * 2 + z % 2)


def shifted(place, axis, step):
    moved = list(place)
    moved[axis] = (place[axis] + step) % 4
    return tuple(moved)


def sibling(place):
    return place[:3] + (1 - place[3],)


def group_partner(step):
    return (lax.axis_index("dp"), (lax.axis_index("fsdp") + step) % GROUP)


def greet(place):
    partners = [device(shifted(place, axis, step)) for axis in range(3) for step in (1, 2, 3)]
    partners.append(device(sibling(place)))
    x, y, z, core = place
    flipped = (x, y, (z // 2) * 2 + (1 - z % 2), core)
    partners += [device(shifted(flipped, 0, step)) for step in (1, 2, 3)]
    barrier = pltpu.get_barrier_semaphore()
    for partner in partners:
        pl.semaphore_signal(barrier, inc=1, device_id=partner, device_id_type=MESH)
    return lambda: pl.semaphore_wait(barrier, len(partners))


def remote(src, dst, send, recv, to):
    copy = pltpu.make_async_remote_copy(
        src_ref=src, dst_ref=dst, send_sem=send, recv_sem=recv, device_id=to, device_id_type=MESH
    )
    copy.start()
    return copy


class Gather:
    def __init__(self, place, s, buf, send, recv):
        self.place, self.buf, self.send, self.recv = place, buf, send, recv
        self.axes = ORDERS[s]
        self.at = tuple(place[axis] for axis in self.axes)
        self.sent, self.pair, self.kept = [], [], []

    def copy(self, slot, first, count, to, keep):
        ref = self.buf.at[self.place[3], pl.ds(first, count)]
        copy = remote(ref, ref, self.send.at[slot], self.recv.at[slot], device(to))
        keep.append(copy)

    def to_line(self, level, first, count):
        self.kept = []
        for step in (2, 1, 3):
            to = shifted(self.place, self.axes[level], step)
            self.copy(3 * level + step - 1, first, count, to, self.kept)
        self.sent += self.kept

    def arrive(self):
        for copy in self.kept:
            copy.wait_recv()

    def first(self):
        ka, kb, kc = self.at
        self.to_line(0, kc * 16 + kb * 4 + ka, 1)

    def second(self):
        self.arrive()
        ka, kb, kc = self.at
        self.to_line(1, kc * 16 + kb * 4, 4)

    def third(self):
        self.arrive()
        kc = self.at[2]
        self.to_line(2, kc * 16, 16)
        self.copy(9, kc * 16, 16, sibling(self.place), self.pair)

    def to_pair(self):
        kc = self.at[2]
        for step, copy in zip((2, 1, 3), self.kept):
            copy.wait_recv()
        for step in (1, 2, 3):
            self.copy(9 + step, (kc - step + 4) % 4 * 16, 16, sibling(self.place), self.pair)

    def finish(self):
        for copy in self.pair:
            copy.wait()
        for copy in self.sent:
            copy.wait_send()


def add_blocks(total, count, first, *others):
    def step(i, carry):
        value = total[first + i].astype(F32)
        for other in others:
            value = value + other(i).astype(F32)
        total[first + i] = value.astype(BF16)
        return carry

    lax.fori_loop(0, count, step, 0, unroll=4)


class Scatter:
    def __init__(self, place, s, buf, pair, far, mid, near, out, send, recv):
        self.place, self.buf, self.pair_in = place, buf, pair
        self.inbox, self.out = (near, mid, far), out
        self.send, self.recv = send, recv
        self.axes = ORDERS[s]
        self.at = tuple(place[axis] for axis in self.axes)
        self.own = buf.at[place[3]]
        self.sent, self.pairs, self.kept = [], {}, []

    def copy(self, slot, src, dst, to):
        copy = remote(src, dst, self.send.at[slot], self.recv.at[slot], device(to))
        self.sent.append(copy)
        return copy

    def to_pair(self):
        other = self.buf.at[1 - self.place[3]]
        for offset in (2, 1, 3, 0):
            rows = pl.ds((self.at[2] + offset) % 4 * 16, 16)
            self.pairs[offset] = self.copy(
                offset, other.at[rows], self.pair_in.at[rows], sibling(self.place)
            )

    def add_pair(self, offset):
        self.pairs[offset].wait_recv()
        start = (self.at[2] + offset) % 4 * 16
        add_blocks(self.own, 16, start, lambda i: self.pair_in[start + i])

    def to_line(self, level, base, size, prepare=None):
        inbox = self.inbox[level]
        self.kept = []
        for step in (2, 1, 3):
            if prepare is not None:
                prepare(step)
            first = base + (self.at[level] + step) % 4 * size
            copy = self.copy(
                4 + 3 * level + step - 1,
                self.own.at[pl.ds(first, size)],
                inbox.at[pl.ds((step - 1) * size, size)],
                shifted(self.place, self.axes[level], step),
            )
            self.kept.append(copy)

    def total(self, level, base, size):
        for copy in self.kept:
            copy.wait_recv()
        inbox = self.inbox[level]
        add_blocks(
            self.own,
            size,
            base + self.at[level] * size,
            *[lambda i, n=n: inbox[n * size + i] for n in range(3)],
        )

    def far(self):
        self.to_line(2, 0, 16, self.add_pair)

    def mid(self):
        self.add_pair(0)
        self.total(2, 0, 16)
        self.to_line(1, self.at[2] * 16, 4)

    def near(self):
        self.total(1, self.at[2] * 16, 4)
        self.to_line(0, self.at[2] * 16 + self.at[1] * 4, 1)

    def finish(self):
        for copy in self.kept:
            copy.wait_recv()
        ka, kb, kc = self.at
        value = self.own[kc * 16 + kb * 4 + ka].astype(F32)
        for step in range(3):
            value = value + self.inbox[0][step].astype(F32)
        self.out[...] = value
        for copy in self.sent:
            copy.wait_send()


def one_hot(rows, columns, pick):
    i = lax.broadcasted_iota(jnp.int32, (rows, columns), 0)
    j = lax.broadcasted_iota(jnp.int32, (rows, columns), 1)
    return jnp.where(pick(i) == j, 1.0, 0.0)


def dot(left, right):
    return jnp.dot(left, right, preferred_element_type=F32)


def dot_nt(left, right):
    return lax.dot_general(left, right, (((1,), (1,)), ((), ())), preferred_element_type=F32)


def dot_tn(left, right):
    return lax.dot_general(left, right, (((0,), (0,)), ((), ())), preferred_element_type=F32)


def stack_columns(shard):
    r, columns = shard.shape
    value = shard.astype(F32)
    pad = [jnp.zeros((8 - r, 128), F32)] if r < 8 else []
    pieces = []
    for c in range(columns // 128):
        pieces += [value[:, c * 128 : (c + 1) * 128]] + pad
    return jnp.concatenate(pieces, axis=0)


def query_order():
    return one_hot(32, 64, lambda i: (i & 7) * 8 + (i >> 3))


def mixed_order():
    def pick(i):
        rest = jnp.where(i < 28, 32 + (i - 20) * 8 + 4, -1)
        return jnp.where(i < 20, (i & 3) * 8 + (i >> 2), rest)

    return one_hot(32, 96, pick)


def wide_order():
    return one_hot(80, 128, lambda i: (i & 15) * 8 + (i >> 4))


def block_index(s, g, d):
    z_hi, y = g // 4, g % 4
    core, x, z_lo = d // 8, (d // 2) % 4, d % 2
    place = (x, y, z_hi * 2 + z_lo)
    a, b, c = (place[axis] for axis in ORDERS[s])
    return core, c * 16 + b * 4 + a


def rms(value):
    return lax.rsqrt(jnp.mean(value * value, axis=-1, keepdims=True) + EPS)


def rotate(value, cosines, sines):
    half = HD // 2
    u, w = value[:, :half], value[:, half:]
    return jnp.concatenate([u * cosines - w * sines, w * cosines + u * sines], axis=1)


def norm_back(grad, value, scale, gain):
    scaled = grad * gain
    back = scale * scaled - value * scale**3 * jnp.mean(scaled * value, axis=-1, keepdims=True)
    return back, jnp.sum(grad * value * scale, axis=0, keepdims=True)


def split_dot_nt(value, matrix):
    high = value.astype(BF16)
    low = (value - high.astype(F32)).astype(BF16)
    return dot_nt(high, matrix) + dot_nt(low, matrix)


def block_kernel(
    tokens,
    cotangent,
    lengths,
    w_query,
    w_key,
    w_value,
    w_out,
    w_gate,
    w_up,
    w_down,
    gains,
    block_out,
    input_grad,
    sum_a0,
    sum_a1,
    sum_a2,
    sum_b0,
    sum_b1,
    sum_b2,
    a0,
    a1,
    a2,
    b0,
    b1,
    b2,
    *scratch,
):
    it = iter(scratch)

    def take(count):
        return [next(it) for _ in range(count)]

    pair_in, far_in, mid_in, near_in = take(6), take(6), take(6), take(6)
    q_mat, kv_mat, o_mat, g_mat, u_mat, d_mat, q_grad, kv_grad = take(8)
    perm, flip, pick, head_pick, gain_cols, gain_rows = take(6)
    cos_ref, sin_ref, allowed_ref = take(3)
    tok_all, scaled, normed, ffn_in, middle = take(5)
    q_raw, kv_raw, queries, kv_all = take(4)
    probs, attended, attended_low, d_attended, d_scores = take(5)
    hidden, d_gate, d_up, d_acc = take(4)
    d_kv_low, kv_in, d_q_low = take(3)
    gather_send, gather_recv, scatter_send, scatter_recv = take(4)
    tok_send, tok_recv, dkv_send, dkv_recv = take(4)

    place = coords()
    core = place[3]
    met = greet(place)
    me = lax.axis_index("fsdp")
    mine = pl.ds(pl.multiple_of(me * TOK, TOK), TOK)
    bufs = (a0, a1, a2, b0, b1, b2)
    outs = (sum_a0, sum_a1, sum_a2, sum_b0, sum_b1, sum_b2)

    def own_ref(n):
        ka, kb, kc = (place[axis] for axis in ORDERS[n % 3])
        return bufs[n].at[core, kc * 16 + kb * 4 + ka]

    query_stack = stack_columns(w_query[...]).astype(BF16)
    own_ref(0)[...] = dot(query_order().astype(BF16), query_stack).astype(BF16)
    mixed = jnp.concatenate(
        [
            stack_columns(w_key[...]).astype(BF16),
            stack_columns(w_value[...]).astype(BF16),
            query_stack,
        ],
        axis=0,
    )
    packed = dot(mixed_order().astype(BF16), mixed)
    own_ref(1)[...] = jnp.concatenate([packed[:24], packed[24:] + gains[...]], axis=0).astype(BF16)
    packed = jnp.concatenate([stack_columns(w_out[...]), jnp.zeros((8, 128), F32)], axis=0)
    own_ref(2)[...] = packed.astype(BF16)
    order = wide_order().astype(BF16)
    own_ref(3)[...] = dot(order, stack_columns(w_gate[...]).astype(BF16)).astype(BF16)
    own_ref(4)[...] = dot(order, stack_columns(w_up[...]).astype(BF16)).astype(BF16)
    down = w_down[...]
    own_ref(5)[...] = jnp.concatenate(
        [down[:, c * 128 : (c + 1) * 128] for c in range(5)], axis=0
    )
    tok_all[mine, :] = tokens[...]

    ga = [
        Gather(place, n % 3, bufs[n], gather_send.at[n], gather_recv.at[n]) for n in range(6)
    ]
    sc = [
        Scatter(
            place,
            n % 3,
            bufs[n],
            pair_in[n],
            far_in[n],
            mid_in[n],
            near_in[n],
            outs[n],
            scatter_send.at[n],
            scatter_recv.at[n],
        )
        for n in range(6)
    ]
    met()
    for n in (1, 0, 2, 3, 4, 5):
        ga[n].first()

    perm[...] = one_hot(256, 256, lambda i: (i & 15) * 16 + (i >> 4)).astype(BF16)
    flip[...] = one_hot(
        256, 256, lambda i: ((i & 127) >> 3) * 16 + (i >> 7) * 8 + (i & 7)
    ).astype(BF16)
    row = lax.broadcasted_iota(jnp.int32, (D, D), 0)
    column = lax.broadcasted_iota(jnp.int32, (D, D), 1)
    pick[...] = jnp.where(row == 5 * (column & 127) + (column >> 7), 1.0, 0.0).astype(BF16)
    row = lax.broadcasted_iota(jnp.int32, (2 * HD, 2 * HD), 0)
    column = lax.broadcasted_iota(jnp.int32, (2 * HD, 2 * HD), 1)
    head_pick[...] = jnp.where(row == 4 * (column & 127) + (column >> 7), 1.0, 0.0).astype(BF16)
    for n in (1, 0, 2):
        ga[n].second()
    tok_copies = [
        remote(
            tok_all.at[mine],
            tok_all.at[mine],
            tok_send.at[step - 1],
            tok_recv.at[step - 1],
            group_partner(step),
        )
        for step in range(1, GROUP)
    ]
    first_len, second_len = lengths[0, 0], lengths[0, 1]
    first_end, second_end = first_len, first_len + second_len

    def segment(ids):
        past_one = jnp.where(ids >= first_end, 1, 0)
        past_two = jnp.where(ids >= second_end, 1, 0)
        return past_one + past_two, ids - past_one * first_len - past_two * second_len

    lane = lax.broadcasted_iota(jnp.int32, (TOK, HD // 2), 1).astype(F32)
    frequencies = jnp.exp(lane * (2.0 / HD) * (-math.log(ROPE_BASE)))

    def tables(m, carry):
        ids = m * TOK + lax.broadcasted_iota(jnp.int32, (TOK, HD // 2), 0)
        angles = segment(ids)[1].astype(F32) * frequencies
        rows = pl.ds(pl.multiple_of(m * TOK, TOK), TOK)
        cos_ref[rows, :] = jnp.cos(angles)
        sin_ref[rows, :] = jnp.sin(angles)
        return carry

    lax.fori_loop(0, GROUP, tables, 0)
    for n in (1, 0, 2):
        ga[n].third()
    row_ids = me * TOK + lax.broadcasted_iota(jnp.int32, (TOK, KEYS), 0)
    key_ids = lax.broadcasted_iota(jnp.int32, (TOK, KEYS), 1)
    same = segment(row_ids)[0] == segment(key_ids)[0]
    allowed_ref[...] = jnp.where(same & (key_ids <= row_ids), 1.0, 0.0)
    for n in (3, 4, 5):
        ga[n].second()
    inputs = tokens[...].astype(F32)
    scale_one = rms(inputs)
    for n in (1, 0):
        ga[n].to_pair()
    for copy in tok_copies:
        copy.wait()

    def scale_tokens(m, carry):
        rows = pl.ds(pl.multiple_of(m * TOK, TOK), TOK)
        value = tok_all[rows, :]
        scaled[rows, :] = dot(value, pick[...]) * rms(value.astype(F32))
        return carry

    lax.fori_loop(0, GROUP, scale_tokens, 0)
    for n in (3, 4, 5):
        ga[n].third()
    ga[1].finish()
    ga[0].finish()

    def slab(n, g, j):
        tiles = []
        for d in range(16):
            c, index = block_index(n % 3, g, d)
            tiles.append(bufs[n][c, index, pl.ds(j * 16, 16), :])
        return jnp.concatenate(tiles, axis=0)

    def turn(matrix, parts):
        out = dot(matrix, jnp.concatenate(parts, axis=1)).astype(BF16)
        return [out[:, i * 128 : (i + 1) * 128] for i in range(len(parts))]

    def tiles_wide(block, first, count):
        return jnp.concatenate(
            [block[(first + i) * 16 : (first + i + 1) * 16] for i in range(count)], axis=1
        )

    def unpack_a(g, carry):
        at = pl.ds(pl.multiple_of(g * 16, 16), 16)

        def rows(r):
            return pl.ds(pl.multiple_of(r * 128 + g * 16, 16), 16)

        kv0, kv1 = turn(perm[...], [slab(1, g, 0), slab(1, g, 1)])
        q0, q1 = turn(perm[...], [slab(0, g, 0), slab(0, g, 1)])
        for r, (block, first) in enumerate(((q0, 0), (q0, 8), (q1, 0), (q1, 8), (kv1, 4))):
            q_mat[rows(r), :] = tiles_wide(block, first, 8)
        gain_cols[at, :] = kv1[12 * 16 : 13 * 16].astype(F32)
        for r in range(4):
            kv_mat[rows(r), :] = tiles_wide(kv0, 4 * r, 4)
        kv_mat[rows(4), :] = tiles_wide(kv1, 0, 4)
        return carry

    lax.fori_loop(0, 8, unpack_a, 0)

    def unpack_out(g, carry):
        o0, o1 = turn(flip[...], [slab(2, g, 0), slab(2, g, 1)])
        (o2,) = turn(flip[...], [slab(2, g, 2)])
        o_mat[pl.ds(pl.multiple_of(g * 128, 128), 128), :] = jnp.concatenate(
            [o0[:128], o0[128:], o1[:128], o1[128:], o2[:128]], axis=1
        )
        return carry

    turned = gain_cols[...].T

    def by_column(first, count):
        return jnp.concatenate([turned[first + i : first + i + 1] for i in range(count)], axis=1)

    gain_rows[2:3, 0 : 2 * HD] = dot_nt(by_column(10, 4).astype(BF16), head_pick[...])

    key_gain = gain_rows[2:3, HD : 2 * HD]
    query_gain = gain_rows[2:3, 0:HD]
    turned_gain = by_column(0, 5)

    def keys_forward(m, carry):
        rows = pl.ds(pl.multiple_of(m * 256, 256), 256)
        normed_rows = (scaled[rows, :] * turned_gain).astype(BF16)
        normed[rows, :] = normed_rows
        raw = dot(normed_rows, kv_mat[...])
        kv_raw[rows, :] = raw
        key_raw = raw[:, 0:HD]
        key_rot = rotate(key_raw * rms(key_raw) * key_gain, cos_ref[rows, :], sin_ref[rows, :])
        kv_all[rows, :] = jnp.concatenate([key_rot, raw[:, HD:]], axis=1).astype(BF16)
        return carry

    lax.fori_loop(0, KEYS // 256, keys_forward, 0)
    cosines, sines = cos_ref[mine, :], sin_ref[mine, :]
    q_raw[...] = dot(normed[mine, :], q_mat[...])
    for h in range(H):
        raw = q_raw[:, h * HD : (h + 1) * HD]
        rot = rotate(raw * rms(raw) * query_gain, cosines, sines)
        queries[h * TOK : (h + 1) * TOK, :] = rot.astype(BF16)
    ga[2].to_pair()

    def attend(h, carry):
        rows = pl.ds(pl.multiple_of(h * TOK, TOK), TOK)
        allowed = allowed_ref[...]
        scores = dot_nt(queries[rows, :], kv_all[:, 0:HD]) * SCORE_SCALE
        scores = jnp.where(allowed > 0.0, scores, NEG)
        peak = jnp.max(scores, axis=-1, keepdims=True)
        expd = jnp.exp(scores - peak) * allowed
        low = (expd * (1.0 / jnp.sum(expd, axis=-1, keepdims=True))).astype(BF16)
        probs[rows, :] = low
        value = dot(low, kv_all[:, HD : 2 * HD])
        attended[rows, :] = value
        attended_low[:, pl.ds(pl.multiple_of(h * HD, HD), HD)] = value.astype(BF16)
        return carry

    lax.fori_loop(0, H, attend, 0)
    for n in (3, 4, 5):
        ga[n].to_pair()
    ga[2].finish()
    lax.fori_loop(0, 8, unpack_out, 0)
    gain_rows[0:1, :] = dot_nt(by_column(0, 5).astype(BF16), pick[...])
    gain_rows[1:2, :] = dot_nt(by_column(5, 5).astype(BF16), pick[...])
    middle[...] = inputs + dot(attended_low[...], o_mat[...])
    scale_two = rms(middle[...])
    ffn_nat = (middle[...] * scale_two * gain_rows[1:2, :]).astype(BF16)
    ffn_in[...] = dot(ffn_nat, pick[...]).astype(BF16)
    for n in (3, 4, 5):
        ga[n].finish()

    def unpack_b(g, carry):
        for mat, n in ((g_mat, 3), (u_mat, 4)):
            slabs = [slab(n, g, j) for j in range(5)]
            turned_slabs = turn(perm[...], slabs[0:2])
            turned_slabs += turn(perm[...], slabs[2:4])
            turned_slabs += turn(perm[...], slabs[4:5])
            for r in range(5):
                mat[pl.ds(pl.multiple_of(r * 128 + g * 16, 16), 16), :] = tiles_wide(
                    turned_slabs[r], 0, 16
                )
        for d in range(16):
            c, index = block_index(2, g, d)
            block = bufs[5][c, index]
            d_mat[pl.ds(pl.multiple_of(g * 256 + d * 16, 16), 16), :] = tiles_wide(block, 0, 5)
        return carry

    lax.fori_loop(0, 8, unpack_b, 0)

    block_out[...] = middle[...]
    d_acc[...] = jnp.zeros_like(d_acc)
    root = math.sqrt(2.0 / math.pi)

    def feed(n, carry):
        at = pl.ds(pl.multiple_of(n * 512, 512), 512)
        gate = dot(ffn_in[...], g_mat[:, at])
        up = dot(ffn_in[...], u_mat[:, at])
        d_hidden = dot_nt(cotangent[...], d_mat[at, :])
        square = gate * gate
        tanh = jnp.tanh(root * gate * (1.0 + 0.044715 * square))
        lift = 0.5 * (1.0 + tanh)
        act = gate * lift
        slope = lift + 0.5 * gate * (1.0 - tanh * tanh) * root * (1.0 + 3 * 0.044715 * square)
        hid = (act * up).astype(BF16)
        dg = (d_hidden * up * slope).astype(BF16)
        du = (d_hidden * act).astype(BF16)
        hidden[:, at] = hid
        d_gate[:, at] = dg
        d_up[:, at] = du
        block_out[...] += dot(hid, d_mat[at, :])
        d_acc[...] += dot_nt(dg, g_mat[:, at]) + dot_nt(du, u_mat[:, at])
        return carry

    lax.fori_loop(0, 4, feed, 0)

    def put(n, g, j, block):
        for d in range(16):
            c, index = block_index(n % 3, g, d)
            bufs[n][c, index, pl.ds(j * 16, 16), :] = block[d * 16 : (d + 1) * 16]

    def down_grads(g, carry):
        at = pl.ds(pl.multiple_of(g * 256, 256), 256)
        grad = dot_tn(hidden[:, at], cotangent[...]).astype(BF16)
        for d in range(16):
            c, index = block_index(2, g, d)
            rows = grad[d * 16 : (d + 1) * 16]
            bufs[5][c, index] = jnp.concatenate(
                [rows[:, i * 128 : (i + 1) * 128] for i in range(5)], axis=0
            )
        return carry

    def stack(grad, g, count):
        rows = grad[g * 16 : (g + 1) * 16]
        return [rows[:, i * 128 : (i + 1) * 128] for i in range(count)]

    def wide_grads(n, source):
        def step(r, carry):
            at = pl.ds(pl.multiple_of(r * 128, 128), 128)
            grad = dot_tn(ffn_in[:, at], source[...]).astype(BF16)
            for g in range(0, 8, 2):
                one, two = turn(
                    perm[...],
                    [jnp.concatenate(stack(grad, g + i, 16), axis=0) for i in range(2)],
                )
                put(n, g, r, one)
                put(n, g + 1, r, two)
            return carry

        lax.fori_loop(0, 5, step, 0)

    lax.fori_loop(0, 8, down_grads, 0)
    sc[5].to_pair()
    wide_grads(3, d_gate)
    sc[3].to_pair()
    sc[5].far()
    wide_grads(4, d_up)
    sc[4].to_pair()
    sc[3].far()

    d_ffn = split_dot_nt(d_acc[...], pick[...])
    d_norm, grad_two = norm_back(d_ffn, middle[...], scale_two, gain_rows[1:2, :])
    d_middle = cotangent[...].astype(F32) + d_norm
    input_grad[...] = d_middle
    d_branch = d_middle.astype(BF16)
    d_attended_flat = dot_nt(d_branch, o_mat[...]).astype(BF16)
    for h in range(H):
        d_attended[h * TOK : (h + 1) * TOK, :] = d_attended_flat[:, h * HD : (h + 1) * HD]
    sc[4].far()

    def out_grads(g, carry):
        at = pl.ds(pl.multiple_of(g * 128, 128), 128)
        grad = dot_tn(attended_low[:, at], d_branch).astype(BF16)
        cols = [grad[:, i * 128 : (i + 1) * 128] for i in range(5)]
        slabs = [
            jnp.concatenate(cols[0:2], axis=0),
            jnp.concatenate(cols[2:4], axis=0),
            jnp.concatenate([cols[4], jnp.zeros((128, 128), BF16)], axis=0),
        ]
        turned_back = dot_tn(flip[...], jnp.concatenate(slabs, axis=1)).astype(BF16)
        for j in range(3):
            put(2, g, j, turned_back[:, j * 128 : (j + 1) * 128])
        return carry

    lax.fori_loop(0, 8, out_grads, 0)
    sc[2].to_pair()

    def scores_back(h, carry):
        rows = pl.ds(pl.multiple_of(h * TOK, TOK), TOK)
        upstream = d_attended[rows, :]
        delta = jnp.sum(upstream.astype(F32) * attended[rows, :], axis=-1, keepdims=True)
        d_probs = dot_nt(upstream, kv_all[:, HD : 2 * HD])
        d_scores[rows, :] = (probs[rows, :].astype(F32) * (d_probs - delta)).astype(BF16)
        return carry

    lax.fori_loop(0, H, scores_back, 0)
    sc[5].mid()

    def keys_back(n, key_gain_grad):
        at = pl.ds(pl.multiple_of(n * 256, 256), 256)
        d_keys = dot_tn(d_scores[:, at], queries[...]) * SCORE_SCALE
        d_values = dot_tn(probs[:, at], d_attended[...])
        d_rot = rotate(d_keys, cos_ref[at, :], -sin_ref[at, :])
        raw = kv_raw[at, 0:HD]
        d_raw, gain_grad = norm_back(d_rot, raw, rms(raw), key_gain)
        d_kv_low[at, :] = jnp.concatenate([d_raw, d_values], axis=1).astype(BF16)
        return key_gain_grad + gain_grad

    key_gain_grad = lax.fori_loop(0, KEYS // 256, keys_back, jnp.zeros((1, HD), F32))
    sc[2].far()
    sc[3].mid()

    query_gain_grad = jnp.zeros((1, HD), F32)
    for h in range(H):
        rows = slice(h * TOK, (h + 1) * TOK)
        d_rot = dot(d_scores[rows, :], kv_all[:, 0:HD]) * SCORE_SCALE
        raw = q_raw[:, h * HD : (h + 1) * HD]
        d_raw, gain_grad = norm_back(
            rotate(d_rot, cosines, -sines), raw, rms(raw), query_gain
        )
        query_gain_grad = query_gain_grad + gain_grad
        d_q_low[:, h * HD : (h + 1) * HD] = d_raw.astype(BF16)
    kv_grad[...] = dot_tn(normed[...], d_kv_low[...]).astype(BF16)
    q_grad[...] = dot_tn(normed[mine, :], d_q_low[...]).astype(BF16)
    sc[4].mid()

    d_key_total = jnp.zeros((1, D), F32)
    d_normed_q = dot_nt(d_q_low[...], q_mat[...])

    def norm_one_grad(n, total):
        at = pl.ds(pl.multiple_of(n * 256, 256), 256)
        return total + jnp.sum(
            dot_nt(d_kv_low[at, :], kv_mat[...]) * scaled[at, :], axis=0, keepdims=True
        )

    grad_one = lax.fori_loop(0, KEYS // 256, norm_one_grad, d_key_total)
    grad_one = grad_one + jnp.sum(d_normed_q * scaled[mine, :], axis=0, keepdims=True)

    def by_device(row, count, matrix):
        turned_row = dot(row.astype(BF16), matrix)
        return [turned_row[:, i * 128 : (i + 1) * 128] for i in range(count)]

    heads = jnp.concatenate([query_gain_grad, key_gain_grad], axis=1)
    gain_parts = [grad_one[:, i * 128 : (i + 1) * 128] for i in range(5)]
    gain_parts += by_device(grad_two, 5, pick[...]) + by_device(heads, 4, head_pick[...])
    gain_parts.append(jnp.zeros((114, 128), F32))
    gain_cols[...] = jnp.concatenate(gain_parts, axis=0).T

    def grads_a(g, carry):
        at = pl.ds(pl.multiple_of(g * 16, 16), 16)
        q_tiles, kv_tiles = [], []
        for r in range(5):
            rows = pl.ds(pl.multiple_of(r * 128 + g * 16, 16), 16)
            q_row, kv_row = q_grad[rows, :], kv_grad[rows, :]
            q_tiles += [q_row[:, i * 128 : (i + 1) * 128] for i in range(8)]
            kv_tiles += [kv_row[:, i * 128 : (i + 1) * 128] for i in range(4)]
        kv_tiles += q_tiles[32:40] + [gain_cols[at, :].astype(BF16)]
        kv_tiles += [jnp.zeros((16, 128), BF16)] * 3
        slabs = [
            jnp.concatenate(tiles[i : i + 16], axis=0)
            for tiles in (q_tiles, kv_tiles)
            for i in (0, 16)
        ]
        out = turn(perm[...], slabs[0:2]) + turn(perm[...], slabs[2:4])
        for n in range(2):
            for j in range(2):
                put(n, g, j, out[2 * n + j])
        return carry

    lax.fori_loop(0, 8, grads_a, 0)
    sc[1].to_pair()
    sc[0].to_pair()
    sc[1].far()
    sc[0].far()
    dkv_copies = [
        remote(
            d_kv_low.at[pl.ds(pl.multiple_of((me + step) % GROUP * TOK, TOK), TOK)],
            kv_in.at[step - 1],
            dkv_send.at[step - 1],
            dkv_recv.at[step - 1],
            group_partner(step),
        )
        for step in range(1, GROUP)
    ]
    sc[5].near()
    sc[3].near()
    sc[4].near()
    sc[2].mid()
    sc[1].mid()
    sc[0].mid()
    sc[5].finish()
    sc[3].finish()
    sc[4].finish()
    sc[2].near()
    sc[1].near()
    sc[0].near()

    total = d_kv_low[mine, :].astype(F32)
    for step in range(GROUP - 1):
        dkv_copies[step].wait()
        total = total + kv_in[step].astype(F32)
    d_normed = d_normed_q + dot_nt(total.astype(BF16), kv_mat[...])
    d_normed = split_dot_nt(d_normed, pick[...])
    d_norm, _ = norm_back(d_normed, inputs, scale_one, gain_rows[0:1, :])
    input_grad[...] += d_norm
    sc[2].finish()
    sc[1].finish()
    sc[0].finish()


def finish_kernel(a0, a1, a2, b0, b1, b2, out, grad, block_out, input_grad, *outs):
    query, key, value, output, gate, up, down, norm_one, norm_two, heads = outs
    block_out[...] = out[...].astype(BF16)
    input_grad[...] = grad[...]

    def exact(order, block):
        return lax.dot_general(
            order,
            block,
            (((0,), (0,)), ((), ())),
            precision=lax.Precision.HIGHEST,
            preferred_element_type=F32,
        )

    def spread(ref, stacked, first, count):
        for c in range(count):
            ref[:, c * 128 : (c + 1) * 128] = stacked[(first + c) * 8 : (first + c) * 8 + 5]

    stacked = exact(mixed_order(), a1[...])
    spread(query, exact(query_order(), a0[...]) + stacked[32:], 0, 8)
    spread(key, stacked, 0, 2)
    spread(value, stacked, 2, 2)
    for c in range(5):
        output[:, c * 128 : (c + 1) * 128] = a2[c * 8 : (c + 1) * 8]
        down[:, c * 128 : (c + 1) * 128] = b2[c * 16 : (c + 1) * 16]
    order = wide_order()
    spread(gate, exact(order, b0[...]), 0, 16)
    spread(up, exact(order, b1[...]), 0, 16)
    row = a1[GAIN_ROW]
    norm_one[...] = row[0:5]
    norm_two[...] = row[5:10]
    heads[...] = row[10:14]


def vmem_specs(count):
    return [pl.BlockSpec(memory_space=pltpu.VMEM)] * count


def body(
    tokens,
    w_query,
    w_key,
    w_value,
    w_out,
    w_gate,
    w_up,
    w_down,
    attn_gain,
    ffn_gain,
    head_gains,
    lengths,
    cotangent,
):
    gains = jnp.concatenate([attn_gain, ffn_gain, head_gains]).astype(F32)
    gains = jnp.pad(gains[None, :], ((GAIN_ROW - 24, 31 - GAIN_ROW), (0, 114)))

    def low(*shape):
        return pltpu.VMEM(shape, BF16)

    def full(*shape):
        return pltpu.VMEM(shape, F32)

    streams = [rows for phase in ROWS for rows in phase]
    scratch = [low(2, 64, rows, 128) for rows in streams]
    scratch += [low(count, rows, 128) for count in (64, 48, 12, 3) for rows in streams]
    scratch += [low(D, 1024), low(D, 512), low(1024, D), low(D, FF), low(D, FF), low(FF, D)]
    scratch += [low(D, 1024), low(D, 512)]
    scratch += [low(256, 256), low(256, 256), low(D, D), low(512, 512)]
    scratch += [full(128, 128), full(8, D)]
    scratch += [full(KEYS, 128), full(KEYS, 128), full(TOK, KEYS)]
    scratch += [low(KEYS, D), full(KEYS, D), low(KEYS, D), low(TOK, D), full(TOK, D)]
    scratch += [full(TOK, 1024), full(KEYS, 512), low(H * TOK, HD), low(KEYS, 2 * HD)]
    scratch += [low(H * TOK, KEYS), full(H * TOK, HD), low(TOK, 1024), low(H * TOK, HD)]
    scratch += [low(H * TOK, KEYS), low(TOK, FF), low(TOK, FF), low(TOK, FF), full(TOK, D)]
    scratch += [low(KEYS, 2 * HD), low(GROUP - 1, TOK, 2 * HD), low(TOK, 1024)]
    dma = pltpu.SemaphoreType.DMA
    scratch += [dma((6, 13)), dma((6, 13)), dma((6, 13)), dma((6, 13))]
    scratch += [dma((7,)), dma((7,)), dma((7,)), dma((7,))]
    out, grad, *sums = pl.pallas_call(
        block_kernel,
        out_shape=[jax.ShapeDtypeStruct((TOK, D), F32)] * 2
        + [jax.ShapeDtypeStruct((rows, 128), F32) for phase in ROWS for rows in phase],
        in_specs=vmem_specs(2) + [pl.BlockSpec(memory_space=pltpu.SMEM)] + vmem_specs(8),
        out_specs=vmem_specs(8),
        scratch_shapes=scratch,
        compiler_params=pltpu.CompilerParams(
            collective_id=0, has_side_effects=True, vmem_limit_bytes=VMEM_BYTES
        ),
        name="block",
    )(
        tokens,
        cotangent,
        lengths,
        w_query,
        w_key,
        w_value,
        w_out,
        w_gate,
        w_up,
        w_down,
        gains,
    )
    shards = [
        jax.ShapeDtypeStruct(shape, F32)
        for shape in ((5, 1024), (5, 256), (5, 256), (8, D), (5, FF), (5, FF), (16, D))
    ]
    shards += [jax.ShapeDtypeStruct((count,), F32) for count in (5, 5, 4)]
    return pl.pallas_call(
        finish_kernel,
        out_shape=[jax.ShapeDtypeStruct((TOK, D), BF16), jax.ShapeDtypeStruct((TOK, D), F32)]
        + shards,
        in_specs=vmem_specs(8),
        out_specs=vmem_specs(12),
        name="finish",
    )(*sums, out, grad)


def solution(mesh):
    rows = P(("dp", "fsdp"), None)
    vector = P(("dp", "fsdp"))
    return jax.shard_map(
        body,
        mesh=mesh,
        in_specs=(rows,) * 8 + (vector,) * 3 + (P("dp", None), rows),
        out_specs=(rows,) * 9 + (vector,) * 3,
        check_vma=False,
    )
```

time: 155 us -> 136 us (0.88)
  Pallas kernels: 150 us -> 134 us
  local copies, waits for them, and re-layouts: 3.25 us -> 0.66 us
    pallas_call x1, Pallas kernels: 148 us -> 132 us  [body(): pl.pallas_call(block_kernel, out_shape=[jax.ShapeDtypeStruct((TOK, D), F3...]
    slice x2 -> x0, local copies, waits for them, and re-layouts: 2.59 us -> none  [body(): return (*results, flat[0:5], flat[5:10], flat[10:14])]
where the time goes in v3:
time: 136 us
  Pallas kernels  134 us (99%)
    pallas_call x1, Pallas kernels, body(): pl.pallas_call(block_kernel, out_shape=[jax.ShapeDtypeStruct((TOK, D), F3...  132 us

profile of v3, /device:TPU:0, one launch (start us, length us, event | category | flops | bytes accessed | tf_op | source)
XLA Modules:
  0.0 135.9 jit_solution(13713088716868516598)
XLA Ops:
  0.6 0.0 copy-start
  0.7 0.0 copy-start.1
  0.7 0.0 copy-start.2
  0.7 0.6 copy-done
  1.3 0.0 copy-done.1
  1.3 0.0 copy-done.2
  1.3 0.7 fusion.2.gains
  2.0 131.5 %block.1 = (f32[128,640]{1,0:T(8,128)}, f32[128,640]{1,0:T(8,128)}, f32[32,128]{1,0:T(8,128)}, f32[32,128]{1,0:T(8,128)}, f32[48,128]{1,0:T(8,128)}, /*index=5*/...) custom-call(bf16[128,640]{1,0:T(8,128)(2,1)} %tokens.1, bf16[128,640]{1,0:T(8,128)(2,1)} %cotangent.1, ...), custom_call_target="tpu_custom_call" | custom-call | tf_op jit(solution)/shard_map/block/pallas_call | solution.py:880
  133.5 2.3 %finish.1 = (bf16[128,640]{1,0:T(8,128)(2,1)}, f32[128,640]{1,0:T(8,128)}, f32[5,1024]{1,0:T(8,128)}, f32[5,256]{1,0:T(8,128)}, f32[5,256]{1,0:T(8,128)}, /*inde...) custom-call(f32[32,128]{1,0:T(8,128)} %get-tuple-element.20.a0, ...), custom_call_target="tpu_custom_call" | custom-call | tf_op jit(solution)/shard_map/finish/pallas_call | solution.py:909
Async XLA Ops:
  0.6 0.7 copy-start
  0.7 0.7 copy-start.1
  0.7 0.7 copy-start.2

commit v4 on v3

--- a/solution.py
+++ b/solution.py
@@ -50,16 +50,14 @@
     return place[:3] + (1 - place[3],)
 
 
-def group_partner(step):
-    return (lax.axis_index("dp"), (lax.axis_index("fsdp") + step) % GROUP)
+def beside(place):
+    x, y, z, core = place
+    return (x, y, (z // 2) * 2 + (1 - z % 2), core)
 
 
 def greet(place):
     partners = [device(shifted(place, axis, step)) for axis in range(3) for step in (1, 2, 3)]
     partners.append(device(sibling(place)))
-    x, y, z, core = place
-    flipped = (x, y, (z // 2) * 2 + (1 - z % 2), core)
-    partners += [device(shifted(flipped, 0, step)) for step in (1, 2, 3)]
     barrier = pltpu.get_barrier_semaphore()
     for partner in partners:
         pl.semaphore_signal(barrier, inc=1, device_id=partner, device_id_type=MESH)
@@ -213,6 +211,115 @@
         self.out[...] = value
         for copy in self.sent:
             copy.wait_send()
+
+
+class GroupGather:
+    def __init__(self, place, me, buf, send, recv):
+        self.place, self.me, self.buf, self.send, self.recv = place, me, buf, send, recv
+        self.sent, self.along, self.across = [], [], []
+
+    def copy(self, slot, ref, to, keep):
+        copy = remote(ref, ref, self.send.at[slot], self.recv.at[slot], device(to))
+        keep.append(copy)
+        self.sent.append(copy)
+
+    def half(self, member, bottom, count=1):
+        rows = TOK // 2
+        return self.buf.at[pl.ds(member, count), pl.ds(bottom * rows, rows)]
+
+    def first(self):
+        for step in (2, 1, 3):
+            to = shifted(self.place, 0, step)
+            self.copy(step - 1, self.half(self.me, 0), to, self.along)
+        self.copy(3, self.half(self.me, 1), beside(self.place), self.across)
+        self.copy(4, self.half(self.me, 0), beside(self.place), self.across)
+
+    def second(self):
+        x = self.place[0]
+        self.across[0].wait_recv()
+        for step in (2, 1, 3):
+            to = shifted(self.place, 0, step)
+            self.copy(7 + step, self.half(2 * x, 1, 2), to, self.across)
+        for step, copy in zip((2, 1, 3), list(self.along)):
+            copy.wait_recv()
+            member = (x - step + 4) % 4 * 2 + self.me % 2
+            self.copy(4 + step, self.half(member, 0), beside(self.place), self.across)
+
+    def finish(self):
+        for copy in self.across[1:]:
+            copy.wait_recv()
+        for copy in self.sent:
+            copy.wait_send()
+
+
+class GroupScatter:
+    def __init__(self, place, buf, inbox, send, recv):
+        self.place, self.buf, self.inbox, self.send, self.recv = place, buf, inbox, send, recv
+        self.sent = []
+
+    def copy(self, slot, src, dst, to):
+        copy = remote(src, dst, self.send.at[slot], self.recv.at[slot], device(to))
+        self.sent.append(copy)
+        return copy
+
+    def first(self):
+        x, z = self.place[0], self.place[2] % 2
+        by_x, by_z = self.inbox[0], self.inbox[1]
+        half = TOK // 2
+        self.along = [
+            self.copy(
+                step - 1,
+                self.buf.at[pl.ds(0, 2), (x + step) % 4, pl.ds(0, half)],
+                by_x.at[step - 1],
+                shifted(self.place, 0, step),
+            )
+            for step in (2, 1, 3)
+        ]
+        self.across = self.copy(
+            3, self.buf.at[1 - z, pl.ds(0, 4), pl.ds(half, half)], by_z, beside(self.place)
+        )
+
+    def second(self):
+        x, z = self.place[0], self.place[2] % 2
+        by_x, by_z, last_x, last_z = self.inbox
+        half = TOK // 2
+        top, bottom = pl.ds(0, half), pl.ds(half, half)
+        self.across.wait_recv()
+        for k in range(4):
+            value = self.buf[z, k, bottom, :].astype(F32) + by_z[k].astype(F32)
+            self.buf[z, k, bottom, :] = value.astype(BF16)
+        self.last = [
+            self.copy(
+                3 + step,
+                self.buf.at[z, (x + step) % 4, bottom],
+                last_x.at[step - 1],
+                shifted(self.place, 0, step),
+            )
+            for step in (2, 1, 3)
+        ]
+        for copy in self.along:
+            copy.wait_recv()
+        for k in range(2):
+            value = self.buf[k, x, top, :].astype(F32)
+            for step in range(3):
+                value = value + by_x[step, k].astype(F32)
+            self.buf[k, x, top, :] = value.astype(BF16)
+        self.last.append(self.copy(7, self.buf.at[1 - z, x, top], last_z, beside(self.place)))
+
+    def finish(self):
+        x, z = self.place[0], self.place[2] % 2
+        last_x, last_z = self.inbox[2:]
+        half = TOK // 2
+        for copy in self.last:
+            copy.wait_recv()
+        value = self.buf[z, x].astype(F32)
+        upper = value[:half] + last_z[...].astype(F32)
+        lower = value[half:]
+        for step in range(3):
+            lower = lower + last_x[step].astype(F32)
+        for copy in self.sent:
+            copy.wait_send()
+        return jnp.concatenate([upper, lower], axis=0)
 
 
 def one_hot(rows, columns, pick):
@@ -330,7 +437,7 @@
     q_raw, kv_raw, queries, kv_all = take(4)
     probs, attended, attended_low, d_attended, d_scores = take(5)
     hidden, d_gate, d_up, d_acc = take(4)
-    d_kv_low, kv_in, d_q_low = take(3)
+    d_kv_low, d_kv, d_q_low, *d_kv_in = take(7)
     gather_send, gather_recv, scatter_send, scatter_recv = take(4)
     tok_send, tok_recv, dkv_send, dkv_recv = take(4)
 
@@ -367,7 +474,7 @@
     own_ref(5)[...] = jnp.concatenate(
         [down[:, c * 128 : (c + 1) * 128] for c in range(5)], axis=0
     )
-    tok_all[mine, :] = tokens[...]
+    tok_all[me] = tokens[...]
 
     ga = [
         Gather(place, n % 3, bufs[n], gather_send.at[n], gather_recv.at[n]) for n in range(6)
@@ -387,9 +494,12 @@
         )
         for n in range(6)
     ]
+    tg = GroupGather(place, me, tok_all, tok_send, tok_recv)
+    ds = GroupScatter(place, d_kv, d_kv_in, dkv_send, dkv_recv)
     met()
     for n in (1, 0, 2, 3, 4, 5):
         ga[n].first()
+    tg.first()
 
     perm[...] = one_hot(256, 256, lambda i: (i & 15) * 16 + (i >> 4)).astype(BF16)
     flip[...] = one_hot(
@@ -401,18 +511,9 @@
     row = lax.broadcasted_iota(jnp.int32, (2 * HD, 2 * HD), 0)
     column = lax.broadcasted_iota(jnp.int32, (2 * HD, 2 * HD), 1)
     head_pick[...] = jnp.where(row == 4 * (column & 127) + (column >> 7), 1.0, 0.0).astype(BF16)
-    for n in (1, 0, 2):
+    for n in (1, 0, 2, 3, 4, 5):
         ga[n].second()
-    tok_copies = [
-        remote(
-            tok_all.at[mine],
-            tok_all.at[mine],
-            tok_send.at[step - 1],
-            tok_recv.at[step - 1],
-            group_partner(step),
-        )
-        for step in range(1, GROUP)
-    ]
+    tg.second()
     first_len, second_len = lengths[0, 0], lengths[0, 1]
     first_end, second_end = first_len, first_len + second_len
 
@@ -433,30 +534,25 @@
         return carry
 
     lax.fori_loop(0, GROUP, tables, 0)
-    for n in (1, 0, 2):
+    for n in (1, 0, 2, 3, 4, 5):
         ga[n].third()
     row_ids = me * TOK + lax.broadcasted_iota(jnp.int32, (TOK, KEYS), 0)
     key_ids = lax.broadcasted_iota(jnp.int32, (TOK, KEYS), 1)
     same = segment(row_ids)[0] == segment(key_ids)[0]
     allowed_ref[...] = jnp.where(same & (key_ids <= row_ids), 1.0, 0.0)
-    for n in (3, 4, 5):
-        ga[n].second()
     inputs = tokens[...].astype(F32)
     scale_one = rms(inputs)
+    tg.finish()
+
+    def scale_tokens(m, carry):
+        rows = pl.ds(pl.multiple_of(m * TOK, TOK), TOK)
+        value = tok_all[m]
+        scaled[rows, :] = dot(value, pick[...]) * rms(value.astype(F32))
+        return carry
+
+    lax.fori_loop(0, GROUP, scale_tokens, 0)
     for n in (1, 0):
         ga[n].to_pair()
-    for copy in tok_copies:
-        copy.wait()
-
-    def scale_tokens(m, carry):
-        rows = pl.ds(pl.multiple_of(m * TOK, TOK), TOK)
-        value = tok_all[rows, :]
-        scaled[rows, :] = dot(value, pick[...]) * rms(value.astype(F32))
-        return carry
-
-    lax.fori_loop(0, GROUP, scale_tokens, 0)
-    for n in (3, 4, 5):
-        ga[n].third()
     ga[1].finish()
     ga[0].finish()
 
@@ -685,7 +781,6 @@
         return carry
 
     lax.fori_loop(0, H, scores_back, 0)
-    sc[5].mid()
 
     def keys_back(n, key_gain_grad):
         at = pl.ds(pl.multiple_of(n * 256, 256), 256)
@@ -694,12 +789,15 @@
         d_rot = rotate(d_keys, cos_ref[at, :], -sin_ref[at, :])
         raw = kv_raw[at, 0:HD]
         d_raw, gain_grad = norm_back(d_rot, raw, rms(raw), key_gain)
-        d_kv_low[at, :] = jnp.concatenate([d_raw, d_values], axis=1).astype(BF16)
+        low = jnp.concatenate([d_raw, d_values], axis=1).astype(BF16)
+        d_kv_low[at, :] = low
+        d_kv[0, n] = low[:TOK]
+        d_kv[1, n] = low[TOK:]
         return key_gain_grad + gain_grad
 
     key_gain_grad = lax.fori_loop(0, KEYS // 256, keys_back, jnp.zeros((1, HD), F32))
+    ds.first()
     sc[2].far()
-    sc[3].mid()
 
     query_gain_grad = jnp.zeros((1, HD), F32)
     for h in range(H):
@@ -713,7 +811,6 @@
         d_q_low[:, h * HD : (h + 1) * HD] = d_raw.astype(BF16)
     kv_grad[...] = dot_tn(normed[...], d_kv_low[...]).astype(BF16)
     q_grad[...] = dot_tn(normed[mine, :], d_q_low[...]).astype(BF16)
-    sc[4].mid()
 
     d_key_total = jnp.zeros((1, D), F32)
     d_normed_q = dot_nt(d_q_low[...], q_mat[...])
@@ -763,40 +860,19 @@
     sc[0].to_pair()
     sc[1].far()
     sc[0].far()
-    dkv_copies = [
-        remote(
-            d_kv_low.at[pl.ds(pl.multiple_of((me + step) % GROUP * TOK, TOK), TOK)],
-            kv_in.at[step - 1],
-            dkv_send.at[step - 1],
-            dkv_recv.at[step - 1],
-            group_partner(step),
-        )
-        for step in range(1, GROUP)
-    ]
-    sc[5].near()
-    sc[3].near()
-    sc[4].near()
-    sc[2].mid()
-    sc[1].mid()
-    sc[0].mid()
-    sc[5].finish()
-    sc[3].finish()
-    sc[4].finish()
-    sc[2].near()
-    sc[1].near()
-    sc[0].near()
-
-    total = d_kv_low[mine, :].astype(F32)
-    for step in range(GROUP - 1):
-        dkv_copies[step].wait()
-        total = total + kv_in[step].astype(F32)
+    ds.second()
+    for n in (5, 3, 4, 2, 1, 0):
+        sc[n].mid()
+    for n in (5, 3, 4, 2, 1, 0):
+        sc[n].near()
+
+    total = ds.finish()
     d_normed = d_normed_q + dot_nt(total.astype(BF16), kv_mat[...])
     d_normed = split_dot_nt(d_normed, pick[...])
     d_norm, _ = norm_back(d_normed, inputs, scale_one, gain_rows[0:1, :])
     input_grad[...] += d_norm
-    sc[2].finish()
-    sc[1].finish()
-    sc[0].finish()
+    for n in (5, 3, 4, 2, 1, 0):
+        sc[n].finish()
 
 
 def finish_kernel(a0, a1, a2, b0, b1, b2, out, grad, block_out, input_grad, *outs):
@@ -869,14 +945,18 @@
     scratch += [low(256, 256), low(256, 256), low(D, D), low(512, 512)]
     scratch += [full(128, 128), full(8, D)]
     scratch += [full(KEYS, 128), full(KEYS, 128), full(TOK, KEYS)]
-    scratch += [low(KEYS, D), full(KEYS, D), low(KEYS, D), low(TOK, D), full(TOK, D)]
+    scratch += [low(GROUP, TOK, D), full(KEYS, D), low(KEYS, D)]
+    scratch += [low(TOK, D), full(TOK, D)]
     scratch += [full(TOK, 1024), full(KEYS, 512), low(H * TOK, HD), low(KEYS, 2 * HD)]
     scratch += [low(H * TOK, KEYS), full(H * TOK, HD), low(TOK, 1024), low(H * TOK, HD)]
     scratch += [low(H * TOK, KEYS), low(TOK, FF), low(TOK, FF), low(TOK, FF), full(TOK, D)]
-    scratch += [low(KEYS, 2 * HD), low(GROUP - 1, TOK, 2 * HD), low(TOK, 1024)]
+    scratch += [low(KEYS, 2 * HD), low(2, 4, TOK, 2 * HD), low(TOK, 1024)]
+    half = TOK // 2
+    scratch += [low(3, 2, half, 2 * HD), low(4, half, 2 * HD)]
+    scratch += [low(3, half, 2 * HD), low(half, 2 * HD)]
     dma = pltpu.SemaphoreType.DMA
     scratch += [dma((6, 13)), dma((6, 13)), dma((6, 13)), dma((6, 13))]
-    scratch += [dma((7,)), dma((7,)), dma((7,)), dma((7,))]
+    scratch += [dma((11,)), dma((11,)), dma((8,)), dma((8,))]
     out, grad, *sums = pl.pallas_call(
         block_kernel,
         out_shape=[jax.ShapeDtypeStruct((TOK, D), F32)] * 2

time: 136 us -> 121 us (0.89)
  Pallas kernels: 134 us -> 118 us
    pallas_call x1, Pallas kernels: 132 us -> 116 us  [body(): pl.pallas_call(block_kernel, out_shape=[jax.ShapeDtypeStruct((TOK, D), F3...]
where the time goes in v4:
time: 121 us; the launch traced here: 120 us
  Pallas kernels  118 us (98%)
    pallas_call x1, Pallas kernels, body(): pl.pallas_call(block_kernel, out_shape=[jax.ShapeDtypeStruct((TOK, D), F3...  116 us

profile of v4, /device:TPU:0, one launch (start us, length us, event | category | flops | bytes accessed | tf_op | source)
XLA Modules:
  0.0 120.3 jit_solution(3684388093358649959)
XLA Ops:
  0.6 0.0 copy-start
  0.7 0.0 copy-start.1
  0.7 0.0 copy-start.2
  0.7 0.6 copy-done
  1.3 0.0 copy-done.1
  1.3 0.0 copy-done.2
  1.3 0.7 fusion.2.gains
  2.0 115.9 %block.1 = (f32[128,640]{1,0:T(8,128)}, f32[128,640]{1,0:T(8,128)}, f32[32,128]{1,0:T(8,128)}, f32[32,128]{1,0:T(8,128)}, f32[48,128]{1,0:T(8,128)}, /*index=5*/...) custom-call(bf16[128,640]{1,0:T(8,128)(2,1)} %tokens.1, bf16[128,640]{1,0:T(8,128)(2,1)} %cotangent.1, ...), custom_call_target="tpu_custom_call" | custom-call | tf_op jit(solution)/shard_map/block/pallas_call | solution.py:960
  117.9 2.3 %finish.1 = (bf16[128,640]{1,0:T(8,128)(2,1)}, f32[128,640]{1,0:T(8,128)}, f32[5,1024]{1,0:T(8,128)}, f32[5,256]{1,0:T(8,128)}, f32[5,256]{1,0:T(8,128)}, /*inde...) custom-call(f32[32,128]{1,0:T(8,128)} %get-tuple-element.20.a0, ...), custom_call_target="tpu_custom_call" | custom-call | tf_op jit(solution)/shard_map/finish/pallas_call | solution.py:989
Async XLA Ops:
  0.6 0.7 copy-start
  0.7 0.7 copy-start.1
  0.7 0.7 copy-start.2

commit v5 on v4

--- a/solution.py
+++ b/solution.py
@@ -533,7 +533,7 @@
         sin_ref[rows, :] = jnp.sin(angles)
         return carry
 
-    lax.fori_loop(0, GROUP, tables, 0)
+    lax.fori_loop(0, GROUP, tables, 0, unroll=2)
     for n in (1, 0, 2, 3, 4, 5):
         ga[n].third()
     row_ids = me * TOK + lax.broadcasted_iota(jnp.int32, (TOK, KEYS), 0)
@@ -550,7 +550,7 @@
         scaled[rows, :] = dot(value, pick[...]) * rms(value.astype(F32))
         return carry
 
-    lax.fori_loop(0, GROUP, scale_tokens, 0)
+    lax.fori_loop(0, GROUP, scale_tokens, 0, unroll=2)
     for n in (1, 0):
         ga[n].to_pair()
     ga[1].finish()
@@ -588,7 +588,7 @@
         kv_mat[rows(4), :] = tiles_wide(kv1, 0, 4)
         return carry
 
-    lax.fori_loop(0, 8, unpack_a, 0)
+    lax.fori_loop(0, 8, unpack_a, 0, unroll=8)
 
     def unpack_out(g, carry):
         o0, o1 = turn(flip[...], [slab(2, g, 0), slab(2, g, 1)])
@@ -620,14 +620,15 @@
         kv_all[rows, :] = jnp.concatenate([key_rot, raw[:, HD:]], axis=1).astype(BF16)
         return carry
 
-    lax.fori_loop(0, KEYS // 256, keys_forward, 0)
+    lax.fori_loop(0, KEYS // 256, keys_forward, 0, unroll=4)
     cosines, sines = cos_ref[mine, :], sin_ref[mine, :]
     q_raw[...] = dot(normed[mine, :], q_mat[...])
     for h in range(H):
         raw = q_raw[:, h * HD : (h + 1) * HD]
         rot = rotate(raw * rms(raw) * query_gain, cosines, sines)
         queries[h * TOK : (h + 1) * TOK, :] = rot.astype(BF16)
-    ga[2].to_pair()
+    for n in (2, 3, 4, 5):
+        ga[n].to_pair()
 
     def attend(h, carry):
         rows = pl.ds(pl.multiple_of(h * TOK, TOK), TOK)
@@ -643,11 +644,9 @@
         attended_low[:, pl.ds(pl.multiple_of(h * HD, HD), HD)] = value.astype(BF16)
         return carry
 
-    lax.fori_loop(0, H, attend, 0)
-    for n in (3, 4, 5):
-        ga[n].to_pair()
+    lax.fori_loop(0, H, attend, 0, unroll=4)
     ga[2].finish()
-    lax.fori_loop(0, 8, unpack_out, 0)
+    lax.fori_loop(0, 8, unpack_out, 0, unroll=8)
     gain_rows[0:1, :] = dot_nt(by_column(0, 5).astype(BF16), pick[...])
     gain_rows[1:2, :] = dot_nt(by_column(5, 5).astype(BF16), pick[...])
     middle[...] = inputs + dot(attended_low[...], o_mat[...])
@@ -673,7 +672,7 @@
             d_mat[pl.ds(pl.multiple_of(g * 256 + d * 16, 16), 16), :] = tiles_wide(block, 0, 5)
         return carry
 
-    lax.fori_loop(0, 8, unpack_b, 0)
+    lax.fori_loop(0, 8, unpack_b, 0, unroll=8)
 
     block_out[...] = middle[...]
     d_acc[...] = jnp.zeros_like(d_acc)
@@ -699,7 +698,7 @@
         d_acc[...] += dot_nt(dg, g_mat[:, at]) + dot_nt(du, u_mat[:, at])
         return carry
 
-    lax.fori_loop(0, 4, feed, 0)
+    lax.fori_loop(0, 4, feed, 0, unroll=2)
 
     def put(n, g, j, block):
         for d in range(16):
@@ -722,7 +721,7 @@
         return [rows[:, i * 128 : (i + 1) * 128] for i in range(count)]
 
     def wide_grads(n, source):
-        def step(r, carry):
+        def loop_r(r, carry):
             at = pl.ds(pl.multiple_of(r * 128, 128), 128)
             grad = dot_tn(ffn_in[:, at], source[...]).astype(BF16)
             for g in range(0, 8, 2):
@@ -734,9 +733,9 @@
                 put(n, g + 1, r, two)
             return carry
 
-        lax.fori_loop(0, 5, step, 0)
-
-    lax.fori_loop(0, 8, down_grads, 0)
+        lax.fori_loop(0, 5, loop_r, 0, unroll=5)
+
+    lax.fori_loop(0, 8, down_grads, 0, unroll=8)
     sc[5].to_pair()
     wide_grads(3, d_gate)
     sc[3].to_pair()
@@ -769,7 +768,7 @@
             put(2, g, j, turned_back[:, j * 128 : (j + 1) * 128])
         return carry
 
-    lax.fori_loop(0, 8, out_grads, 0)
+    lax.fori_loop(0, 8, out_grads, 0, unroll=8)
     sc[2].to_pair()
 
     def scores_back(h, carry):
@@ -780,7 +779,7 @@
         d_scores[rows, :] = (probs[rows, :].astype(F32) * (d_probs - delta)).astype(BF16)
         return carry
 
-    lax.fori_loop(0, H, scores_back, 0)
+    lax.fori_loop(0, H, scores_back, 0, unroll=4)
 
     def keys_back(n, key_gain_grad):
         at = pl.ds(pl.multiple_of(n * 256, 256), 256)
@@ -795,7 +794,7 @@
         d_kv[1, n] = low[TOK:]
         return key_gain_grad + gain_grad
 
-    key_gain_grad = lax.fori_loop(0, KEYS // 256, keys_back, jnp.zeros((1, HD), F32))
+    key_gain_grad = lax.fori_loop(0, KEYS // 256, keys_back, jnp.zeros((1, HD), F32), unroll=4)
     ds.first()
     sc[2].far()
 
@@ -821,7 +820,7 @@
             dot_nt(d_kv_low[at, :], kv_mat[...]) * scaled[at, :], axis=0, keepdims=True
         )
 
-    grad_one = lax.fori_loop(0, KEYS // 256, norm_one_grad, d_key_total)
+    grad_one = lax.fori_loop(0, KEYS // 256, norm_one_grad, d_key_total, unroll=4)
     grad_one = grad_one + jnp.sum(d_normed_q * scaled[mine, :], axis=0, keepdims=True)
 
     def by_device(row, count, matrix):
@@ -855,7 +854,7 @@
                 put(n, g, j, out[2 * n + j])
         return carry
 
-    lax.fori_loop(0, 8, grads_a, 0)
+    lax.fori_loop(0, 8, grads_a, 0, unroll=8)
     sc[1].to_pair()
     sc[0].to_pair()
     sc[1].far()

time: 121 us -> 113 us (0.934)
  Pallas kernels: 118 us -> 111 us
    pallas_call x1, Pallas kernels: 116 us -> 108 us  [body(): pl.pallas_call(block_kernel, out_shape=[jax.ShapeDtypeStruct((TOK, D), F3...]
where the time goes in v5:
time: 113 us
  Pallas kernels  111 us (98%)
    pallas_call x1, Pallas kernels, body(): pl.pallas_call(block_kernel, out_shape=[jax.ShapeDtypeStruct((TOK, D), F3...  108 us
    pallas_call x1, Pallas kernels, body(): pl.pallas_call(finish_kernel, out_shape=[jax.ShapeDtypeStruct((TOK, D), B...  2.34 us

profile of v5, /device:TPU:0, one launch (start us, length us, event | category | flops | bytes accessed | tf_op | source)
XLA Modules:
  0.0 113.0 jit_solution(1153493574253554558)
XLA Ops:
  0.6 0.0 copy-start
  0.7 0.0 copy-start.1
  0.7 0.0 copy-start.2
  0.7 0.6 copy-done
  1.3 0.0 copy-done.1
  1.3 0.0 copy-done.2
  1.3 0.7 fusion.2.gains
  2.0 108.5 %block.1 = (f32[128,640]{1,0:T(8,128)}, f32[128,640]{1,0:T(8,128)}, f32[32,128]{1,0:T(8,128)}, f32[32,128]{1,0:T(8,128)}, f32[48,128]{1,0:T(8,128)}, /*index=5*/...) custom-call(bf16[128,640]{1,0:T(8,128)(2,1)} %tokens.1, bf16[128,640]{1,0:T(8,128)(2,1)} %cotangent.1, ...), custom_call_target="tpu_custom_call" | custom-call | tf_op jit(solution)/shard_map/block/pallas_call | solution.py:959
  110.5 2.3 %finish.1 = (bf16[128,640]{1,0:T(8,128)(2,1)}, f32[128,640]{1,0:T(8,128)}, f32[5,1024]{1,0:T(8,128)}, f32[5,256]{1,0:T(8,128)}, f32[5,256]{1,0:T(8,128)}, /*inde...) custom-call(f32[32,128]{1,0:T(8,128)} %get-tuple-element.20.a0, ...), custom_call_target="tpu_custom_call" | custom-call | tf_op jit(solution)/shard_map/finish/pallas_call | solution.py:988
Async XLA Ops:
  0.6 0.7 copy-start
  0.7 0.7 copy-start.1
  0.7 0.7 copy-start.2

commit v6 on v5

--- a/solution.py
+++ b/solution.py
@@ -132,7 +132,7 @@
         total[first + i] = value.astype(BF16)
         return carry
 
-    lax.fori_loop(0, count, step, 0, unroll=4)
+    lax.fori_loop(0, count, step, 0, unroll=min(count, 8))
 
 
 class Scatter:
@@ -407,7 +407,9 @@
     w_gate,
     w_up,
     w_down,
-    gains,
+    attn_gain,
+    ffn_gain,
+    head_gains,
     block_out,
     input_grad,
     sum_a0,
@@ -464,7 +466,13 @@
         axis=0,
     )
     packed = dot(mixed_order().astype(BF16), mixed)
-    own_ref(1)[...] = jnp.concatenate([packed[:24], packed[24:] + gains[...]], axis=0).astype(BF16)
+    gains = jnp.concatenate(
+        [ref[...].astype(F32) for ref in (attn_gain, ffn_gain, head_gains)]
+        + [jnp.zeros((1, 114), F32)],
+        axis=1,
+    )
+    gain_place = lax.broadcasted_iota(jnp.int32, (8, 128), 0) == GAIN_ROW - 24
+    own_ref(1)[...] = jnp.concatenate([packed[:24], packed[24:] + jnp.where(gain_place, gains, 0.0)], axis=0).astype(BF16)
     packed = jnp.concatenate([stack_columns(w_out[...]), jnp.zeros((8, 128), F32)], axis=0)
     own_ref(2)[...] = packed.astype(BF16)
     order = wide_order().astype(BF16)
@@ -534,14 +542,18 @@
         return carry
 
     lax.fori_loop(0, GROUP, tables, 0, unroll=2)
-    for n in (1, 0, 2, 3, 4, 5):
+    for n in (1, 0, 2):
         ga[n].third()
     row_ids = me * TOK + lax.broadcasted_iota(jnp.int32, (TOK, KEYS), 0)
     key_ids = lax.broadcasted_iota(jnp.int32, (TOK, KEYS), 1)
     same = segment(row_ids)[0] == segment(key_ids)[0]
     allowed_ref[...] = jnp.where(same & (key_ids <= row_ids), 1.0, 0.0)
+    for n in (3, 4, 5):
+        ga[n].third()
     inputs = tokens[...].astype(F32)
     scale_one = rms(inputs)
+    for n in (1, 0):
+        ga[n].to_pair()
     tg.finish()
 
     def scale_tokens(m, carry):
@@ -551,8 +563,6 @@
         return carry
 
     lax.fori_loop(0, GROUP, scale_tokens, 0, unroll=2)
-    for n in (1, 0):
-        ga[n].to_pair()
     ga[1].finish()
     ga[0].finish()
 
@@ -735,13 +745,13 @@
 
         lax.fori_loop(0, 5, loop_r, 0, unroll=5)
 
+    wide_grads(4, d_up)
+    sc[4].to_pair()
+    wide_grads(3, d_gate)
+    sc[3].to_pair()
+    sc[4].far()
     lax.fori_loop(0, 8, down_grads, 0, unroll=8)
     sc[5].to_pair()
-    wide_grads(3, d_gate)
-    sc[3].to_pair()
-    sc[5].far()
-    wide_grads(4, d_up)
-    sc[4].to_pair()
     sc[3].far()
 
     d_ffn = split_dot_nt(d_acc[...], pick[...])
@@ -752,7 +762,7 @@
     d_attended_flat = dot_nt(d_branch, o_mat[...]).astype(BF16)
     for h in range(H):
         d_attended[h * TOK : (h + 1) * TOK, :] = d_attended_flat[:, h * HD : (h + 1) * HD]
-    sc[4].far()
+    sc[5].far()
 
     def out_grads(g, carry):
         at = pl.ds(pl.multiple_of(g * 128, 128), 128)
@@ -795,7 +805,6 @@
         return key_gain_grad + gain_grad
 
     key_gain_grad = lax.fori_loop(0, KEYS // 256, keys_back, jnp.zeros((1, HD), F32), unroll=4)
-    ds.first()
     sc[2].far()
 
     query_gain_grad = jnp.zeros((1, HD), F32)
@@ -859,10 +868,11 @@
     sc[0].to_pair()
     sc[1].far()
     sc[0].far()
+    ds.first()
+    for n in (4, 3, 5, 2, 1, 0):
+        sc[n].mid()
     ds.second()
-    for n in (5, 3, 4, 2, 1, 0):
-        sc[n].mid()
-    for n in (5, 3, 4, 2, 1, 0):
+    for n in (4, 3, 5, 2, 1, 0):
         sc[n].near()
 
     total = ds.finish()
@@ -870,7 +880,7 @@
     d_normed = split_dot_nt(d_normed, pick[...])
     d_norm, _ = norm_back(d_normed, inputs, scale_one, gain_rows[0:1, :])
     input_grad[...] += d_norm
-    for n in (5, 3, 4, 2, 1, 0):
+    for n in (4, 3, 5, 2, 1, 0):
         sc[n].finish()
 
 
@@ -927,8 +937,6 @@
     lengths,
     cotangent,
 ):
-    gains = jnp.concatenate([attn_gain, ffn_gain, head_gains]).astype(F32)
-    gains = jnp.pad(gains[None, :], ((GAIN_ROW - 24, 31 - GAIN_ROW), (0, 114)))
 
     def low(*shape):
         return pltpu.VMEM(shape, BF16)
@@ -960,7 +968,7 @@
         block_kernel,
         out_shape=[jax.ShapeDtypeStruct((TOK, D), F32)] * 2
         + [jax.ShapeDtypeStruct((rows, 128), F32) for phase in ROWS for rows in phase],
-        in_specs=vmem_specs(2) + [pl.BlockSpec(memory_space=pltpu.SMEM)] + vmem_specs(8),
+        in_specs=vmem_specs(2) + [pl.BlockSpec(memory_space=pltpu.SMEM)] + vmem_specs(10),
         out_specs=vmem_specs(8),
         scratch_shapes=scratch,
         compiler_params=pltpu.CompilerParams(
@@ -978,7 +986,9 @@
         w_gate,
         w_up,
         w_down,
-        gains,
+        attn_gain[None],
+        ffn_gain[None],
+        head_gains[None],
     )
     shards = [
         jax.ShapeDtypeStruct(shape, F32)

time: 113 us -> 108 us (0.956)
  Pallas kernels: 111 us -> 107 us
    pallas_call x1, Pallas kernels: 108 us -> 104 us  [body(): pl.pallas_call(block_kernel, out_shape=[jax.ShapeDtypeStruct((TOK, D), F3...]
where the time goes in v6:
time: 108 us
  Pallas kernels  107 us (99%)
    pallas_call x1, Pallas kernels, body(): pl.pallas_call(block_kernel, out_shape=[jax.ShapeDtypeStruct((TOK, D), F3...  104 us
    pallas_call x1, Pallas kernels, body(): pl.pallas_call(finish_kernel, out_shape=[jax.ShapeDtypeStruct((TOK, D), B...  2.34 us

profile of v6, /device:TPU:0, one launch (start us, length us, event | category | flops | bytes accessed | tf_op | source)
XLA Modules:
  0.0 107.6 jit_solution(17265526859688163597)
XLA Ops:
  0.6 104.4 %block.1 = (f32[128,640]{1,0:T(8,128)}, f32[128,640]{1,0:T(8,128)}, f32[32,128]{1,0:T(8,128)}, f32[32,128]{1,0:T(8,128)}, f32[48,128]{1,0:T(8,128)}, /*index=5*/...) custom-call(bf16[128,640]{1,0:T(8,128)(2,1)} %tokens.1, bf16[128,640]{1,0:T(8,128)(2,1)} %cotangent.1, ...), custom_call_target="tpu_custom_call" | custom-call | tf_op jit(solution)/shard_map/block/pallas_call | solution.py:967
  105.1 2.3 %finish.1 = (bf16[128,640]{1,0:T(8,128)(2,1)}, f32[128,640]{1,0:T(8,128)}, f32[5,1024]{1,0:T(8,128)}, f32[5,256]{1,0:T(8,128)}, f32[5,256]{1,0:T(8,128)}, /*inde...) custom-call(f32[32,128]{1,0:T(8,128)} %get-tuple-element.20.a0, ...), custom_call_target="tpu_custom_call" | custom-call | tf_op jit(solution)/shard_map/finish/pallas_call | solution.py:998

commit v7 on v6

--- a/solution.py
+++ b/solution.py
@@ -112,9 +112,8 @@
 
     def to_pair(self):
         kc = self.at[2]
-        for step, copy in zip((2, 1, 3), self.kept):
+        for step, copy in ((1, self.kept[1]), (3, self.kept[2]), (2, self.kept[0])):
             copy.wait_recv()
-        for step in (1, 2, 3):
             self.copy(9 + step, (kc - step + 4) % 4 * 16, 16, sibling(self.place), self.pair)
 
     def finish(self):

time: 108 us -> 108 us (level)
  no operation moved by 1% of the time
where the time goes in v7:
time: 108 us; the launch traced here: 107 us
  Pallas kernels  107 us (99%)
    pallas_call x1, Pallas kernels, body(): pl.pallas_call(block_kernel, out_shape=[jax.ShapeDtypeStruct((TOK, D), F3...  104 us
    pallas_call x1, Pallas kernels, body(): pl.pallas_call(finish_kernel, out_shape=[jax.ShapeDtypeStruct((TOK, D), B...  2.34 us

profile of v7, /device:TPU:0, one launch (start us, length us, event | category | flops | bytes accessed | tf_op | source)
XLA Modules:
  0.0 107.5 jit_solution(18174950570288624773)
XLA Ops:
  0.6 104.3 %block.1 = (f32[128,640]{1,0:T(8,128)}, f32[128,640]{1,0:T(8,128)}, f32[32,128]{1,0:T(8,128)}, f32[32,128]{1,0:T(8,128)}, f32[48,128]{1,0:T(8,128)}, /*index=5*/...) custom-call(bf16[128,640]{1,0:T(8,128)(2,1)} %tokens.1, bf16[128,640]{1,0:T(8,128)(2,1)} %cotangent.1, ...), custom_call_target="tpu_custom_call" | custom-call | tf_op jit(solution)/shard_map/block/pallas_call | solution.py:966
  105.0 2.3 %finish.1 = (bf16[128,640]{1,0:T(8,128)(2,1)}, f32[128,640]{1,0:T(8,128)}, f32[5,1024]{1,0:T(8,128)}, f32[5,256]{1,0:T(8,128)}, f32[5,256]{1,0:T(8,128)}, /*inde...) custom-call(f32[32,128]{1,0:T(8,128)} %get-tuple-element.20.a0, ...), custom_call_target="tpu_custom_call" | custom-call | tf_op jit(solution)/shard_map/finish/pallas_call | solution.py:997
